TPU v7x, 512 devices: a whole 4x8x8 slice. The times are simulated.
512 devices in a mesh: kv: 16 (over y, core), tp: 32 (over x, z).
Axes of the slice: x: 4, y: 8, z: 8, core: 2. Of those that a mesh axis runs over, the one named last changes fastest.
Arguments:
- tokens: bfloat16 [256, 7168], P('tp', 'kv'), may hold values from -8 to 8
- attn_gain: float32 [7168], P('kv'), may hold values from 0.5 to 1.5
- down_kv: bfloat16 [7168, 576], P('kv'), may hold values from -0.0625 to 0.0625
- latent_gain: float32 [512], replicated, may hold values from 0.5 to 1.5
- query_nope: bfloat16 [256, 16384], P(None, 'tp'), may hold values from -8 to 8
- query_rope: bfloat16 [256, 8192], P(None, 'tp'), may hold values from -8 to 8
- cache: bfloat16 [2, 12288, 576], P(None, 'kv'), may hold values from -6 to 6
- lengths: int32 [2], replicated, may hold values from 3072 to 12288, as said below
- key_up: bfloat16 [128, 128, 512], P('tp', None, 'kv'), may hold values from -0.5 to 0.5
- value_up: bfloat16 [128, 512, 128], P('tp', 'kv'), may hold values from -0.25 to 0.25
- out_proj: bfloat16 [16384, 7168], P('tp', 'kv'), may hold values from -0.1875 to 0.1875
- mlp_gain: float32 [7168], P('kv'), may hold values from 0.5 to 1.5
- expert_ids: int32 [256, 8], P('tp'), may hold values from 0 to 15, all different within a row; in each aligned block of 8 rows (0 to 7, 8 to 15, ...) at most 6 rows name the same one
- expert_weights: float32 [256, 8], P('tp'), may hold values from 0.1 to 1
- gate_proj: bfloat16 [32, 7168, 1024], P('tp', 'kv'), may hold values from -0.0625 to 0.0625
- up_proj: bfloat16 [32, 7168, 1024], P('tp', 'kv'), may hold values from -0.0625 to 0.0625
- down_proj: bfloat16 [32, 1024, 7168], P('tp', None, 'kv'), may hold values from -0.125 to 0.125
Outputs:
- attended: bfloat16 [256, 7168], P('tp', 'kv')
- mixed: bfloat16 [256, 7168], P('tp', 'kv')
Inputs may be any that keep to these rules, and one draw needn't show every extreme that they name: `expert_ids`: in each aligned block of 8 rows (the rows of one index of tp) no expert is named by more than 6 rows, a bound that some block reaches; a row names 8 different experts. `lengths`: some sequence has all 12288 positions.
All inputs are finite; a program needn't handle non-finite values.
Results may differ from a plain program's by a relative error of at most 0.011.
Values may be sent and summed in bfloat16 or wider, within the bound.
No kernel may reach another device: no remote copies, remote signals or barrier semaphores. Data moves between devices by JAX's collectives and lax.ppermute only.
A program may use at most 128 MiB of HBM per device.

v0:
```python
import math

import jax
import jax.numpy as jnp
from jax import lax
from jax.sharding import PartitionSpec as P

D = 7168
NOPE = 128
ROPE = 64
LAT = 512
VDIM = 128
SEQS = 2
QROWS = 32
STEPS = 4
TOKROWS = 256


EPS = 1e-06
LOWEST = -1e30


def normalize(values, gain):
    return values * lax.rsqrt(jnp.mean(values * values, axis=-1, keepdims=True) + EPS) * gain


def rotate(part, positions):
    half = part.shape[-1] // 2
    freq = 10000.0 ** (-2.0 * jnp.arange(half, dtype=jnp.float32) / part.shape[-1])
    angle = positions.astype(jnp.float32)[..., None] * freq
    cosine = jnp.cos(angle)
    sine = jnp.sin(angle)
    first = part[..., :half]
    second = part[..., half:]
    return jnp.concatenate(
        [first * cosine - second * sine, second * cosine + first * sine], axis=-1
    )


def head_values(latent, weights_up, head_count):
    shaped = latent.reshape(latent.shape[0], -1, head_count, latent.shape[2])
    return jnp.einsum(
        "bqhl,hlv->bqhv", shaped, weights_up.astype(jnp.float32), precision=lax.Precision.HIGHEST
    )


def per_device(
    tokens,
    attn_gain,
    down_kv,
    latent_gain,
    query_nope,
    query_rope,
    cache,
    lengths,
    key_up,
    value_up,
    out_proj,
    mlp_gain,
    expert_ids,
    expert_weights,
    gate_proj,
    up_proj,
    down_proj,
):
    scale = 1.0 / math.sqrt(NOPE + ROPE)
    kv_index = lax.axis_index("kv")
    tp_index = lax.axis_index("tp")
    tp_count = lax.axis_size("tp")
    rows_here = tokens.shape[0]
    head_count = key_up.shape[0]
    lat_width = key_up.shape[2]
    span = cache.shape[1]
    query_count = STEPS * QROWS * head_count
    wide_tokens = tokens.astype(jnp.float32)
    normed = (wide_tokens * attn_gain).astype(jnp.bfloat16)
    fresh = lax.psum(jnp.dot(normed, down_kv, preferred_element_type=jnp.float32), "kv")
    row_ids = tp_index * rows_here + jnp.arange(rows_here, dtype=jnp.int32)
    step_of = row_ids // (SEQS * QROWS)
    seq_of = row_ids // QROWS % SEQS
    seq_labels = jnp.arange(SEQS, dtype=jnp.int32)
    positions = (
        jnp.sum(jnp.where(seq_of[:, None] == seq_labels[None, :], lengths[None, :], 0), axis=1)
        + step_of
    )
    own_key = jnp.concatenate(
        [normalize(fresh[:, :LAT], latent_gain), rotate(fresh[:, LAT:], positions)], axis=1
    ).astype(jnp.bfloat16)
    fresh_key = lax.all_gather(own_key, "tp", axis=0, tiled=True)
    fresh_blocks = fresh_key.reshape(STEPS, SEQS, QROWS, LAT + ROPE)
    rope_steps = query_rope.reshape(STEPS, SEQS, QROWS, head_count, ROPE)
    rope_seq = rope_steps.transpose(1, 0, 2, 3, 4).reshape(SEQS, query_count, ROPE)
    start_scores = jnp.einsum(
        "bqc,btc->bqt", rope_seq, cache[:, :, LAT:], preferred_element_type=jnp.float32
    )
    start_fresh = jnp.einsum(
        "sbjhc,tbjc->sbjht", rope_steps, fresh_blocks[..., LAT:], preferred_element_type=jnp.float32
    )
    absorbed = jnp.einsum(
        "rhn,hnl->rhl",
        query_nope.reshape(TOKROWS, head_count, NOPE),
        key_up,
        preferred_element_type=jnp.float32,
    ).astype(jnp.bfloat16)
    lat_piece = lax.all_gather(absorbed, "kv", axis=2, tiled=True)
    cache_part = start_scores
    fresh_part = start_fresh
    width = lat_piece.shape[2]
    step_piece = lat_piece.reshape(STEPS, SEQS, QROWS, head_count, width)
    seq_piece = step_piece.transpose(1, 0, 2, 3, 4).reshape(SEQS, query_count, width)
    keys = lax.slice_in_dim(cache, 0, width, axis=2)
    fresh_keys = lax.slice_in_dim(fresh_blocks, 0, width, axis=3)
    cache_part = cache_part + jnp.einsum(
        "bqc,btc->bqt", seq_piece, keys, preferred_element_type=jnp.float32
    )
    fresh_part = fresh_part + jnp.einsum(
        "sbjhc,tbjc->sbjht", step_piece, fresh_keys, preferred_element_type=jnp.float32
    )
    scores = cache_part * scale
    places = kv_index * span + jnp.arange(span, dtype=jnp.int32)
    valid = (places[None, :] < lengths[:, None])[:, None, :]
    peak = jnp.max(jnp.where(valid, scores, LOWEST), axis=2)
    weights = jnp.where(valid, jnp.exp(scores - peak[..., None]), 0.0).astype(jnp.bfloat16)
    total = jnp.sum(weights.astype(jnp.float32), axis=2)
    weighted = jnp.einsum(
        "bqt,btc->bqc", weights, cache[:, :, :LAT], preferred_element_type=jnp.float32
    )
    step_scores = fresh_part * scale
    step_ids = jnp.arange(STEPS, dtype=jnp.int32)
    causal = (step_ids[None, :] <= step_ids[:, None])[:, None, None, None, :]
    fresh_peak = jnp.max(jnp.where(causal, step_scores, LOWEST), axis=4)
    fresh_weights = jnp.where(causal, jnp.exp(step_scores - fresh_peak[..., None]), 0.0).astype(
        jnp.bfloat16
    )
    fresh_total = jnp.sum(fresh_weights.astype(jnp.float32), axis=4)
    fresh_latent = jnp.einsum(
        "sbjht,tbjc->sbjhc",
        fresh_weights,
        fresh_blocks[..., :LAT],
        preferred_element_type=jnp.float32,
    )
    fresh_peak = fresh_peak.transpose(1, 0, 2, 3).reshape(SEQS, query_count)
    fresh_total = fresh_total.transpose(1, 0, 2, 3).reshape(SEQS, query_count)
    fresh_latent = fresh_latent.transpose(1, 0, 2, 3, 4).reshape(SEQS, query_count, LAT)
    own_fresh = lax.dynamic_slice_in_dim(fresh_latent, kv_index * lat_width, lat_width, 2)
    best = lax.pmax(peak, "kv")
    top = jnp.maximum(best, fresh_peak)
    factor = jnp.exp(peak - top)
    fresh_keep = jnp.exp(fresh_peak - top)
    total_all = lax.psum(total * factor, "kv") + fresh_total * fresh_keep
    share = lax.psum_scatter(weighted * factor[..., None], "kv", scatter_dimension=2, tiled=True)
    share = share + own_fresh * fresh_keep[..., None]
    seq_values = head_values(share / total_all[..., None], value_up, head_count)
    value_part = (
        seq_values.reshape(SEQS, STEPS, QROWS, head_count, VDIM)
        .transpose(1, 0, 2, 3, 4)
        .reshape(TOKROWS, head_count * VDIM)
    )
    values = lax.psum(value_part, "kv").astype(jnp.bfloat16)
    attended = lax.psum_scatter(
        jnp.dot(values, out_proj, preferred_element_type=jnp.float32),
        "tp",
        scatter_dimension=0,
        tiled=True,
    ).astype(jnp.bfloat16)
    mid = wide_tokens + attended.astype(jnp.float32)
    mid_squares = lax.psum(jnp.sum(mid * mid, axis=1), "kv")
    mlp_in = (mid * lax.rsqrt(mid_squares[:, None] / D + EPS) * mlp_gain).astype(jnp.bfloat16)
    expert_count = tp_count // 2
    chosen = expert_ids.shape[1]
    capacity = min(rows_here, rows_here * chosen // expert_count + 2)
    labels = jnp.arange(expert_count, dtype=jnp.int32)
    hits = (expert_ids.reshape(-1)[:, None] == labels[None, :]).astype(jnp.int32)
    ranks = jnp.cumsum(hits, axis=0) - hits
    slot = jnp.sum(ranks * hits, axis=1)
    slot_hit = (slot[:, None] == jnp.arange(capacity, dtype=jnp.int32)[None, :]).astype(jnp.float32)
    route = (hits.astype(jnp.float32)[:, :, None] * slot_hit[:, None, :]).reshape(
        rows_here, chosen, expert_count, capacity
    )
    placing = jnp.sum(route, axis=1)
    scaling = jnp.sum(route * expert_weights[:, :, None, None], axis=1)
    outgoing = jnp.einsum(
        "rec,rd->ecd", placing.astype(jnp.bfloat16), mlp_in, preferred_element_type=jnp.float32
    ).astype(jnp.bfloat16)
    outgoing = jnp.repeat(outgoing, 2, axis=0)
    received = lax.all_to_all(outgoing, "tp", split_axis=0, concat_axis=0, tiled=True)
    flat = received.reshape(-1, received.shape[2])
    gate_part = jnp.dot(flat, gate_proj[0], preferred_element_type=jnp.float32)
    up_part = jnp.dot(flat, up_proj[0], preferred_element_type=jnp.float32)
    gate, upward = lax.psum((gate_part, up_part), "kv")
    hidden = (jax.nn.silu(gate) * upward).astype(jnp.bfloat16)
    produced = jnp.dot(hidden, down_proj[0], preferred_element_type=jnp.float32)
    produced = produced.reshape(received.shape[0], received.shape[1], produced.shape[1])
    returned = lax.all_to_all(produced, "tp", split_axis=0, concat_axis=0, tiled=True)
    halves = returned.reshape(expert_count, 2, capacity, returned.shape[2])
    expert_out = halves[:, 0] + halves[:, 1]
    moe = jnp.einsum("rec,ecd->rd", scaling, expert_out, precision=lax.Precision.HIGHEST)
    mixed = (mid + moe).astype(jnp.bfloat16)
    return (attended, mixed)


def solution(mesh):
    return jax.shard_map(
        per_device,
        mesh=mesh,
        in_specs=(
            P("tp", "kv"),
            P("kv"),
            P("kv", None),
            P(),
            P(None, "tp"),
            P(None, "tp"),
            P(None, "kv", None),
            P(),
            P("tp", None, "kv"),
            P("tp", "kv", None),
            P("tp", "kv"),
            P("kv"),
            P("tp", None),
            P("tp", None),
            P("tp", "kv", None),
            P("tp", "kv", None),
            P("tp", None, "kv"),
        ),
        out_specs=(P("tp", "kv"), P("tp", "kv")),
        check_vma=False,
    )
```

profile of v0, /device:TPU:1, one launch (start us, length us, event | category | flops | bytes accessed | tf_op | source)
XLA Modules:
  0.0 691.9 jit_solution(17733568137194898827)
XLA Ops:
  7.2 1.9 fusion.3
  9.2 1.3 fusion.39
  10.5 49.5 %psum.42 = f32[8,576]{1,0:T(8,128)S(1)} all-reduce(f32[8,576]{1,0:T(8,128)S(1)} %fusion.39), channel_id=1, replica_groups=mesh['kv'=16,'tp'=32] {'kv'}, use_global_device_ids=true, to_apply=%region_2.3 | all-reduce | flops 4608 | bytes 36864 | tf_op jit(solution)/shard_map/psum | solution.py:77
  59.9 0.1 multiply_reduce_fusion.2
  60.0 0.7 fusion.52
  60.8 0.1 fusion.49
  60.9 0.8 multiply_convert_fusion.2
  61.7 0.1 pad_maximum_fusion
  61.8 41.1 %all_gather.7 = bf16[256,576]{1,0:T(8,128)(2,1)S(1)} all-gather(bf16[8,576]{1,0:T(8,128)(2,1)S(1)} %pad_maximum_fusion), channel_id=1, replica_groups=mesh['kv'=16,'tp'=32] {'tp'}, dimensions={0}, use_global_device_ids=true | all-gather | bytes 304128 | tf_op jit(solution)/shard_map/all_gather | solution.py:89
  102.9 1.1 reshape.210
  104.0 0.1 copy.108
  104.1 2.4 fusion.19
  106.5 0.4 copy.119
  106.9 0.7 broadcast_compare_fusion
  107.5 1.5 copy.111
  109.0 4.7 fusion.6
  113.7 0.4 copy.120
  114.1 0.1 fusion.28
  114.3 0.1 copy.122
  114.4 0.7 reshape.216
  115.1 0.8 copy.112
  115.9 0.3 reshape.214
  116.2 2.4 fusion
  118.7 3.4 select_reduce_fusion
  122.1 38.4 %pmax.7 = f32[2,512]{1,0:T(2,128)S(1)} all-reduce(f32[2,512]{1,0:T(2,128)S(1)} %get-tuple-element.18), channel_id=1, replica_groups=mesh['kv'=16,'tp'=32] {'kv'}, use_global_device_ids=true, to_apply=%region_1.2 | all-reduce | flops 1024 | bytes 8192 | tf_op jit(solution)/shard_map/pmax | solution.py:146
  160.5 2.8 convert_reduce_fusion
  163.4 2.5 convolution_multiply_fusion
  166.0 0.2 reduce-scatter.5.cloned.1.call-start
  166.2 0.1 convert_reduce_fusion.1
  166.4 0.1 copy.128
  166.5 0.1 reshape.218
  166.6 0.3 copy.124
  167.0 0.7 convolution_bitcast_fusion
  167.7 1.6 copy.125
  169.3 0.6 constant_dynamic-slice_fusion
  169.9 0.2 copy.149
  170.1 23.6 %psum.43 = f32[2,512]{1,0:T(2,128)S(1)} all-reduce(f32[2,512]{1,0:T(2,128)S(1)} %get-tuple-element.12), channel_id=1, replica_groups=mesh['kv'=16,'tp'=32] {'kv'}, use_global_device_ids=true, to_apply=%region_8.9 | all-reduce | flops 1024 | bytes 8192 | tf_op jit(solution)/shard_map/psum | solution.py:150
  193.7 26.6 %reduce-scatter.3.cloned.1.call-done = f32[2,512,32]{1,2,0:T(8,128)} async-done(((f32[2,512,512]{1,2,0:T(8,128)}), f32[2,512,32]{1,2,0:T(8,128)}) %reduce-scatter.3.cloned.1.call-update) | async-done | bytes 131088 | tf_op jit(solution)/shard_map/reduce_scatter | solution.py:151
  220.3 0.9 add_divide_fusion
  221.3 0.2 copy.129
  221.5 0.4 fusion.14
  221.9 0.3 copy.131
  222.3 51.2 %all-reduce.5 = bf16[256,512]{1,0:T(8,128)(2,1)S(1)} all-reduce(f32[256,512]{1,0:T(8,128)S(1)} %bitcast.105), channel_id=1, replica_groups=mesh['kv'=16,'tp'=32] {'kv'}, use_global_device_ids=true, to_apply=%region_10.11 | all-reduce | flops 131072 | bytes 786432 | tf_op jit(solution)/shard_map/psum | solution.py:159
  273.5 1.1 fusion.59
  274.7 0.1 eq.65
  274.8 0.1 reduce_window_sum.11
  274.9 0.2 select_reduce_fusion.1
  275.1 0.1 eq.69
  275.3 0.8 fusion.23
  276.1 216.0 %reduce-scatter.5.cloned.1.call-done = f32[8,448]{1,0:T(8,128)} async-done(((f32[256,448]{1,0:T(8,128)}), f32[8,448]{1,0:T(8,128)}) %reduce-scatter.5.cloned.1.call-update) | async-done | bytes 14352 | tf_op jit(solution)/shard_map/reduce_scatter | solution.py:160
  492.1 0.8 multiply_reduce_fusion.1
  493.0 28.7 %psum.45 = f32[8]{0:T(128)S(1)} all-reduce(f32[8]{0:T(128)S(1)} %get-tuple-element.6), channel_id=1, replica_groups=mesh['kv'=16,'tp'=32] {'kv'}, use_global_device_ids=true, to_apply=%region_17.18 | all-reduce | flops 8 | bytes 64 | tf_op jit(solution)/shard_map/psum | solution.py:167
  521.7 0.2 convolution_convert_fusion
  522.1 15.9 %all_to_all.10 = bf16[32,6,448]{2,1,0:T(8,128)(2,1)S(1)} all-to-all(bf16[32,6,448]{2,1,0:T(8,128)(2,1)S(1)} %bitcast.109), channel_id=1, replica_groups=mesh['kv'=16,'tp'=32] {'tp'}, dimensions={0} | all-to-all | bytes 344064 | tf_op jit(solution)/shard_map/all_to_all | solution.py:186
  537.9 0.1 reshape.223
  538.1 1.3 fusion.10
  539.3 1.3 fusion.12
  540.6 117.2 %all-reduce.4.cloned.1.call-done = (f32[192,1024]{1,0:T(8,128)}, f32[192,1024]{1,0:T(8,128)}) async-done(((f32[192,1024]{1,0:T(8,128)}, f32[192,1024]{1,0:T(8,128)}), (f32[192,1024]{1,0:T(8,128)}, f32[192,1024]{1,0:T(8,128)})) %all-reduce.4.cloned.1.call-update) | async-done | bytes 1572880 | tf_op jit(solution)/shard_map/psum | solution.py:190
  657.8 1.6 multiply_convert_fusion
  659.4 0.1 dot_general.60
  659.6 0.5 fusion.8
  660.1 0.2 copy.135
  660.3 23.8 %all_to_all.11 = f32[32,6,448]{2,1,0:T(8,128)S(1)} all-to-all(f32[32,6,448]{2,1,0:T(8,128)S(1)} %copy.135), channel_id=1, replica_groups=mesh['kv'=16,'tp'=32] {'tp'}, dimensions={0} | all-to-all | bytes 688128 | tf_op jit(solution)/shard_map/all_to_all | solution.py:194
  684.2 1.1 fusion.5
  (70 shorter events, 0.8 us)
Async XLA Ops:
  7.2 530.9 %copy-start = (bf16[1,448,1024]{2,1,0:T(8,128)(2,1)S(1)}, bf16[1,448,1024]{2,1,0:T(8,128)(2,1)}, u32[]{:S(2)}) copy-start(bf16[1,448,1024]{2,1,0:T(8,128)(2,1)} %param.32) | copy-start | bytes 2752516
  7.2 99.7 %copy-start.21 = (s32[2]{0:T(128)S(1)}, s32[2]{0:T(128)}, u32[]{:S(2)}) copy-start(s32[2]{0:T(128)} %param.24) | copy-start | bytes 28
  7.2 100.3 %all-gather.2.cloned.1.call-start = ((), (), s32[]{:S(2)}) async-start(), calls=%async_computation.4 | async-start | bytes 1114112 | tf_op jit(solution)/shard_map/all_gather | solution.py:105
  9.1 211.2 %reduce-scatter.3.cloned.1.call-start = ((), (), s32[]{:S(2)}) async-start(), calls=%async_computation.5 | async-start | bytes 2228224 | tf_op jit(solution)/shard_map/reduce_scatter | solution.py:151
  106.8 7.4 %copy-start.5 = (f32[2,32,4,4,4]{1,2,4,0,3:T(4,128)}, f32[2,32,4,4,4]{1,2,4,0,3:T(4,128)S(1)}, u32[]{:S(2)}) copy-start(f32[2,32,4,4,4]{1,2,4,0,3:T(4,128)S(1)} %copy.119) | copy-start | bytes 49156
  106.8 7.4 %copy-start.19 = (pred[4,4]{1,0:T(4,128)(4,1)}, pred[4,4]{1,0:T(4,128)(4,1)S(1)}, u32[]{:S(2)}) copy-start(pred[4,4]{1,0:T(4,128)(4,1)S(1)} %iota_compare_fusion.3) | copy-start | bytes 52
  114.1 1.0 copy-start.7
  116.2 2.4 copy-start.15
  118.7 44.7 %copy-start.2 = (bf16[2,768,576]{1,2,0:T(8,128)(2,1)S(1)}, bf16[2,768,576]{1,2,0:T(8,128)(2,1)}, u32[]{:S(2)}) copy-start(bf16[2,768,576]{1,2,0:T(8,128)(2,1)} %param.23) | copy-start | bytes 5308420
  122.1 41.3 %copy-start.13 = (f32[2,512]{1,0:T(2,128)S(1)}, f32[2,512]{1,0:T(2,128)}, u32[]{:S(2)}) copy-start(f32[2,512]{1,0:T(2,128)} %reshape.216) | copy-start | bytes 12292
  160.5 2.9 copy-start.1
  163.4 2.8 copy-start.6
  163.4 2.8 copy-start.8
  163.4 2.8 copy-start.20
  166.0 326.1 %reduce-scatter.5.cloned.1.call-start = ((), (), s32[]{:S(2)}) async-start(), calls=%async_computation.6 | async-start | bytes 540672 | tf_op jit(solution)/shard_map/reduce_scatter | solution.py:160
  167.7 53.8 %copy-start.14 = (bf16[4,32,128]{2,1,0:T(8,128)(2,1)S(1)}, bf16[4,32,128]{2,1,0:T(8,128)(2,1)}, u32[]{:S(2)}) copy-start(bf16[4,32,128]{2,1,0:T(8,128)(2,1)} %param.26) | copy-start | bytes 98308
  169.3 104.1 %copy-start.9 = (bf16[512,448]{0,1:T(8,128)(2,1)S(1)}, bf16[512,448]{0,1:T(8,128)(2,1)}, u32[]{:S(2)}) copy-start(bf16[512,448]{0,1:T(8,128)(2,1)} %param.27) | copy-start | bytes 1376260
  221.2 53.4 %copy-start.16 = (s32[8,8]{1,0:T(8,128)S(1)}, s32[8,8]{1,0:T(8,128)}, u32[]{:S(2)}) copy-start(s32[8,8]{1,0:T(8,128)} %param.29) | copy-start | bytes 772
  221.3 54.0 %copy-start.17 = (f32[8,8]{1,0:T(8,128)S(1)}, f32[8,8]{1,0:T(8,128)}, u32[]{:S(2)}) copy-start(f32[8,8]{1,0:T(8,128)} %param.30) | copy-start | bytes 772
  221.5 270.7 %copy-start.10 = (bf16[8,448]{1,0:T(8,128)(2,1)S(1)}, bf16[8,448]{1,0:T(8,128)(2,1)}, u32[]{:S(2)}) copy-start(bf16[8,448]{1,0:T(8,128)(2,1)} %param.17) | copy-start | bytes 21508
  221.5 300.2 %copy-start.18 = (f32[448]{0:T(512)S(1)}, f32[448]{0:T(512)}, u32[]{:S(2)}) copy-start(f32[448]{0:T(512)} %param.28) | copy-start | bytes 5380
  222.3 317.0 %copy-start.3 = (bf16[1,448,1024]{2,1,0:T(8,128)(2,1)S(1)}, bf16[1,448,1024]{2,1,0:T(8,128)(2,1)}, u32[]{:S(2)}) copy-start(bf16[1,448,1024]{2,1,0:T(8,128)(2,1)} %param.31) | copy-start | bytes 2752516
  274.6 383.2 %all-reduce.4.cloned.1.call-start = ((), (), s32[]{:S(2)}) async-start(), calls=%async_computation.7 | async-start | bytes 3145728 | tf_op jit(solution)/shard_map/psum | solution.py:190
  493.0 191.2 %copy-start.12 = (bf16[8,448]{1,0:T(8,128)(2,1)}, bf16[8,448]{1,0:T(8,128)(2,1)S(1)}, u32[]{:S(2)}) copy-start(bf16[8,448]{1,0:T(8,128)(2,1)S(1)} %get-tuple-element.7) | copy-start | bytes 21508
  539.3 120.2 %copy-start.4 = (bf16[1,1024,448]{1,2,0:T(8,128)(2,1)S(1)}, bf16[1,1024,448]{1,2,0:T(8,128)(2,1)}, u32[]{:S(2)}) copy-start(bf16[1,1024,448]{1,2,0:T(8,128)(2,1)} %param.33) | copy-start | bytes 2752516
  659.4 24.8 %copy-start.11 = (f32[8,16,6]{1,2,0:T(8,128)S(1)}, f32[8,16,6]{1,2,0:T(8,128)}, u32[]{:S(2)}) copy-start(f32[8,16,6]{1,2,0:T(8,128)} %get-tuple-element.2) | copy-start | bytes 9220
Sparse Core Ops, SparseCore 0:
  10.2 46.7 all-gather.1
  166.1 54.1 reduce-scatter.2
  274.7 217.3 reduce-scatter.4
  540.7 117.0 all-reduce.3
where the time goes:
time: 695 us; the launch traced here: 692 us
  waiting for transfers between devices  360 us (52%)
  blocking collectives  272 us (39%)
  matrix products  25.2 us (4%)
  between operations  14.3 us (2%)
  other arithmetic  10.3 us (1%)
  local copies, waits for them, and re-layouts  9.86 us (1%)
    reduce_scatter x1, waiting for transfers between devices, per_device(): lax.psum_scatter(jnp.dot(values, out_proj, preferred_element_type=jnp.flo...  216 us
    psum x1, waiting for transfers between devices, per_device(): gate, upward = lax.psum((gate_part, up_part), 'kv')  117 us
    psum x1, blocking collectives, per_device(): values = lax.psum(value_part, 'kv').astype(jnp.bfloat16)  51.2 us
    psum x1, blocking collectives, per_device(): lax.psum(jnp.dot(normed, down_kv, preferred_element_type=jnp.float32), 'kv')  49.5 us
    all_gather x1, blocking collectives, per_device(): fresh_key = lax.all_gather(own_key, 'tp', axis=0, tiled=True)  41.1 us
    pmax x1, blocking collectives, per_device(): best = lax.pmax(peak, 'kv')  38.4 us
    psum x1, blocking collectives, per_device(): mid_squares = lax.psum(jnp.sum(mid * mid, axis=1), 'kv')  28.7 us
    reduce_scatter x1, waiting for transfers between devices, per_device(): lax.psum_scatter(weighted * factor[..., None], 'kv', scatter_dimension=2,...  26.6 us
  transfers between devices with their start and end apart: 4, of which 3 were waited for; matrix products, arithmetic and copies ran while one was open for 2% of the time, Pallas kernels for 0%

commit v1 on v0

v1 whole, which is shorter than its diff:
```python
import functools
import math

import jax
import jax.numpy as jnp
from jax import lax
from jax.experimental import pallas as pl
from jax.experimental.pallas import tpu as pltpu
from jax.sharding import PartitionSpec as P

D = 7168
NOPE = 128
ROPE = 64
LAT = 512
VDIM = 128
SEQS = 2
QROWS = 32
STEPS = 4
TOKROWS = 256
EXPERTS = 16

N_KV = 16
N_TP = 32
HEADS_DEV = 4
FEAT = D // N_KV
ROWS_TP = TOKROWS // N_TP
ROWS_KV = TOKROWS // N_KV
KEY = LAT + ROPE
PAIRS = SEQS * QROWS
STAT = 2 * HEADS_DEV
ATT_W = LAT + 128
CHIPS = N_KV // 2
LAT_KV = LAT // N_KV
UP_ROWS = 2 * HEADS_DEV * LAT_KV
FRESH_W = KEY + ROPE
FRESH_ROWS = 48
CLASS = TOKROWS // 2
PART_ROWS = 2 * CLASS + 16
KEY_W = 384
HID = 1024
HID_Y = HID // 8

EPS = 1e-06
LOWEST = -1e30
SCALE = 1.0 / math.sqrt(NOPE + ROPE)

F32 = jnp.float32
BF16 = jnp.bfloat16
NT = (((1,), (1,)), ((), ()))
TN = (((0,), (0,)), ((), ()))


def kv_index():
    return lax.axis_index("kv")


def tp_index():
    return lax.axis_index("tp")


def iota(shape, dim):
    return lax.broadcasted_iota(jnp.int32, shape, dim)


def dot(a, b, dims=(((1,), (0,)), ((), ()))):
    return lax.dot_general(a, b, dims, preferred_element_type=F32)


def parts_of(value):
    high = value.astype(BF16).astype(F32)
    rest = value - high
    middle = rest.astype(BF16).astype(F32)
    return high, middle, rest - middle


def with_stats(stats, head, peak, total):
    lane = iota(stats.shape, 1)
    for at, part in enumerate(parts_of(peak)):
        stats = jnp.where(lane == at * STAT + head, part, stats)
    for at, part in enumerate(parts_of(total)):
        stats = jnp.where(lane == at * STAT + HEADS_DEV + head, part, stats)
    return stats


def whole_stats(tail):
    return tail[..., :STAT] + tail[..., STAT : 2 * STAT] + tail[..., 2 * STAT : 3 * STAT]


def by_pair(transposed):
    shape = (TOKROWS, TOKROWS)
    paired, stepped = iota(shape, 1 if transposed else 0), iota(shape, 0 if transposed else 1)
    return (stepped == paired % STEPS * PAIRS + paired // STEPS).astype(F32).astype(BF16)


def swap_halves(rows):
    return pltpu.roll(rows, 4, 0)


def start_kernel(tokens_ref, gain_ref, down_ref, key_ref, value_ref, mlp_gain_ref, out_ref, mine_ref):
    wide_tokens = tokens_ref[...].astype(F32)
    mine_ref[...] = jnp.concatenate([wide_tokens, jnp.broadcast_to(mlp_gain_ref[...], (8, FEAT))], axis=0)
    normed = (wide_tokens * gain_ref[...]).astype(BF16)
    fresh = dot(normed, down_ref[...])
    fresh = jnp.concatenate([fresh, jnp.zeros((ROWS_TP, ROPE), F32)], axis=1)
    tiles = [fresh[:, at * 128 : (at + 1) * 128] for at in range(FRESH_W // 128)]
    tiles.append(jnp.zeros((FRESH_ROWS - ROWS_TP * len(tiles), 128), F32))
    packed = jnp.concatenate(tiles, axis=0).astype(BF16)
    for place in range(CHIPS):
        for head in range(HEADS_DEV):
            out_ref[place, head * LAT_KV : (head + 1) * LAT_KV, :] = key_ref[head]
            out_ref[place, UP_ROWS // 2 + head * LAT_KV : UP_ROWS // 2 + (head + 1) * LAT_KV, :] = value_ref[head]
        out_ref[place, UP_ROWS:, :] = packed


def sum_kernel(ups_ref, out_ref):
    out_ref[...] = jnp.sum(ups_ref[:, UP_ROWS:, :].astype(F32), axis=0)


def fresh_kernel(own_ref, other_ref, gain_ref, lengths_ref, freq_ref, out_ref):
    packed = own_ref[...] + other_ref[...]
    tiles = [packed[at * ROWS_TP : (at + 1) * ROWS_TP] for at in range(FRESH_W // 128)]
    fresh = jnp.concatenate(tiles[:-1], axis=1)
    turn = tiles[-1][:, :ROPE]
    scaled = fresh * lax.rsqrt(jnp.mean(fresh * fresh, axis=1, keepdims=True) + EPS) * gain_ref[...]
    row = tp_index() * ROWS_TP
    lengths = lengths_ref[...]
    start = jnp.where(row // QROWS % SEQS == 0, lengths[:, 0:1], lengths[:, 1:2])
    angle = (start + row // PAIRS).astype(F32) * freq_ref[...]
    cosine, sine = jnp.cos(angle), jnp.sin(angle)
    first, second = turn[:, : ROPE // 2], turn[:, ROPE // 2 :]
    turned = [first * cosine - second * sine, second * cosine + first * sine]
    key = jnp.concatenate([scaled] + turned + [jnp.zeros((ROWS_TP, ROPE), F32)], axis=1)
    key = jnp.where(kv_index() % 2 == 0, key, swap_halves(key))
    upper = jnp.concatenate([key[:, :256], key[:, LAT:]], axis=1)
    lower = jnp.concatenate([swap_halves(key[:, 256:LAT]), jnp.zeros((ROWS_TP, KEY_W - 256), F32)], axis=1)
    key = jnp.where(iota(upper.shape, 0) < ROWS_TP // 2, upper, lower).astype(BF16)
    for place in range(N_TP):
        out_ref[place] = key


def attend_kernel(
    lengths_ref, own_ups_ref, other_ups_ref, nope_ref, rope_ref, keys_ref,
    out_ref, own_ref, ups_ref, queries,
):
    core = kv_index() % 2
    rows_seq = TOKROWS // SEQS
    for source, whose in ((own_ups_ref, core), (other_ups_ref, 1 - core)):
        for chip in range(CHIPS):
            for which in range(2 * HEADS_DEV):
                ups_ref[which, 2 * chip + whose] = source[chip, which * LAT_KV : (which + 1) * LAT_KV, :]
    reorder = by_pair(False)
    nope = dot(reorder, nope_ref[...]).astype(BF16)
    rope = dot(reorder, rope_ref[...]).astype(BF16)
    for head in range(HEADS_DEV):
        key_up = ups_ref[head].reshape(LAT, NOPE)
        absorbed = dot(nope[:, head * NOPE : (head + 1) * NOPE], key_up, NT).astype(BF16)
        turned = rope[:, head * ROPE : (head + 1) * ROPE]
        for seq in range(SEQS):
            rows = slice(seq * rows_seq, (seq + 1) * rows_seq)
            place = slice(head * rows_seq, (head + 1) * rows_seq)
            queries[seq, place, :LAT] = absorbed[rows]
            queries[seq, place, LAT:] = turned[rows]
    own_seq = kv_index() // (N_KV // SEQS)
    own_row = kv_index() % (N_KV // SEQS) * ROWS_KV
    for head in range(HEADS_DEV):
        start = pl.multiple_of(head * rows_seq + own_row, ROWS_KV)
        own_ref[head * ROWS_KV : (head + 1) * ROWS_KV, :] = queries[own_seq, pl.ds(start, ROWS_KV), :]
    span = keys_ref.shape[2]
    lengths = lengths_ref[...]
    for seq in range(SEQS):
        valid = kv_index() * span + iota((1, span), 1) < lengths[:, seq : seq + 1]
        scores = dot(queries[seq], keys_ref[seq]) * SCALE + jnp.where(valid, 0.0, LOWEST)
        peak = jnp.max(scores, axis=1, keepdims=True)
        weights = jnp.where(valid, jnp.exp(scores - peak), 0.0).astype(BF16)
        total = jnp.sum(weights.astype(F32), axis=1, keepdims=True)
        latent = dot(weights, keys_ref[seq, :LAT, :], NT).astype(BF16)
        stats = jnp.zeros((rows_seq, 128), F32)
        rows = slice(seq * rows_seq, (seq + 1) * rows_seq)
        for head in range(HEADS_DEV):
            place = slice(head * rows_seq, (head + 1) * rows_seq)
            value_up = ups_ref[HEADS_DEV + head].reshape(LAT, VDIM)
            out_ref[rows, head * VDIM : (head + 1) * VDIM] = dot(latent[place], value_up).astype(BF16)
            stats = with_stats(stats, head, peak[place], total[place])
        out_ref[rows, LAT:] = stats.astype(BF16)


def merge_kernel(parts_ref, own_ref, ups_ref, keys_ref, out_ref):
    kv = kv_index()
    out_ref[...] = parts_ref[...]
    rows = pl.ds(pl.multiple_of(kv * ROWS_KV, ROWS_KV), ROWS_KV)
    mine = parts_ref[rows, :].astype(F32)
    stats = whole_stats(mine[:, LAT:])
    keys = []
    for step in range(STEPS):
        block = keys_ref[step * (PAIRS // ROWS_TP) + kv // 2].astype(F32)
        keys.append(jnp.concatenate([block[:, :256], swap_halves(block[:, :256]), block[:, 256 : 256 + ROPE]], axis=1))
    keys = jnp.concatenate(keys, axis=0).astype(BF16)
    scores = dot(own_ref[...], keys, NT) * SCALE
    row = iota(scores.shape, 0) % ROWS_KV
    key = iota(scores.shape, 1)
    causal = (row // STEPS == key % ROWS_TP) & (key // ROWS_TP <= row % STEPS)
    scores = jnp.where(causal, scores, LOWEST)
    fresh_peak = jnp.max(scores, axis=1, keepdims=True)
    weights = jnp.where(causal, jnp.exp(scores - fresh_peak), 0.0).astype(BF16)
    fresh_total = jnp.sum(weights.astype(F32), axis=1, keepdims=True)
    fresh_latent = dot(weights, keys[:, :LAT]).astype(BF16)
    tail = jnp.zeros((ROWS_KV, 128), F32)
    merged = []
    for head in range(HEADS_DEV):
        own = slice(head * ROWS_KV, (head + 1) * ROWS_KV)
        peak = stats[:, head : head + 1]
        top = jnp.maximum(peak, fresh_peak[own])
        keep = jnp.exp(peak - top)
        fresh_keep = jnp.exp(fresh_peak[own] - top)
        value_up = ups_ref[HEADS_DEV + head].reshape(LAT, VDIM)
        part = mine[:, head * VDIM : (head + 1) * VDIM]
        merged.append(part * keep + dot(fresh_latent[own], value_up) * fresh_keep)
        total = stats[:, HEADS_DEV + head : HEADS_DEV + head + 1] * keep + fresh_total[own] * fresh_keep
        tail = with_stats(tail, head, top, total)
    out_ref[rows, :] = jnp.concatenate(merged + [tail], axis=1).astype(BF16)


def combine_kernel(parts_ref, out_ref):
    stats = whole_stats(parts_ref[:, :, LAT:].astype(F32))
    for head in range(HEADS_DEV):
        peak = stats[:, :, head : head + 1]
        total = stats[:, :, HEADS_DEV + head : HEADS_DEV + head + 1]
        keep = jnp.exp(peak - jnp.max(peak, axis=0, keepdims=True))
        part = parts_ref[:, :, head * VDIM : (head + 1) * VDIM].astype(F32)
        value = jnp.sum(part * keep, axis=0) / jnp.sum(total * keep, axis=0)
        for place in range(CHIPS):
            out_ref[place, :, head * VDIM : (head + 1) * VDIM] = value.astype(BF16)


def own_half(shape, dim):
    return iota(shape, dim) % ROWS_TP // (ROWS_TP // 2) == kv_index() % 2


def project_kernel(values_ref, own_ref, other_ref, out_ref):
    values = values_ref[...].reshape(CLASS, HEADS_DEV * VDIM)
    shape = (TOKROWS, CLASS)
    row, source = iota(shape, 0), iota(shape, 1)
    block, pair = row // ROWS_TP, row % (ROWS_TP // 2)
    match = source == block % CHIPS * ROWS_KV + pair * STEPS + block // CHIPS
    own = (match & own_half(shape, 0)).astype(F32).astype(BF16)
    other = (match & ~own_half(shape, 0)).astype(F32).astype(BF16)
    out = dot(dot(own, values).astype(BF16), own_ref[...], NT)
    out = out + dot(dot(other, values).astype(BF16), other_ref[...], NT)
    out_ref[...] = out.reshape(N_TP, ROWS_TP, FEAT).astype(BF16)


def route_kernel(parts_ref, mine_ref, other_ref, attended_ref, out_ref):
    attended = jnp.sum(parts_ref[...].astype(F32), axis=0).astype(BF16)
    attended_ref[...] = attended
    own = own_half((ROWS_TP, FEAT), 0)
    tokens = jnp.where(own, mine_ref[:ROWS_TP], swap_halves(other_ref[:ROWS_TP]))
    gain = jnp.where(own, mine_ref[ROWS_TP:], other_ref[ROWS_TP:])
    mid = tokens + attended.astype(F32)
    lane = iota((ROWS_TP, 512 - FEAT), 1)
    extra = jnp.zeros(lane.shape, F32)
    for at, part in enumerate(parts_of(jnp.sum(mid * mid, axis=1, keepdims=True))):
        extra = jnp.where(lane == at, part, extra)
    row_data = jnp.concatenate([mid * gain, extra], axis=1).astype(BF16)
    for place in range(N_TP):
        out_ref[place] = row_data


def gate_kernel(rows_ref, own_gate_ref, own_up_ref, other_gate_ref, other_up_ref, out_ref):
    rows = rows_ref[...].astype(F32).reshape(TOKROWS, 512).astype(BF16)
    shape = (CLASS, TOKROWS)
    place, row = iota(shape, 0), iota(shape, 1)
    match = place == row // ROWS_TP * (ROWS_TP // 2) + row % (ROWS_TP // 2)
    own = dot((match & own_half(shape, 1)).astype(F32).astype(BF16), rows).astype(BF16)
    other = dot((match & ~own_half(shape, 1)).astype(F32).astype(BF16), rows).astype(BF16)
    sixteen, column = iota((16, 512), 0), iota((16, 512), 1)
    first = ((sixteen < 3) & (column == FEAT + sixteen)).astype(F32).astype(BF16)
    second = ((sixteen >= 3) & (sixteen < 6) & (column == FEAT + sixteen - 3)).astype(F32).astype(BF16)
    squares = (dot(first, own, NT) + dot(second, other, NT)).astype(BF16)
    own, other = own[:, :FEAT], other[:, :FEAT]
    for place in range(CHIPS):
        columns = slice(place * HID_Y, (place + 1) * HID_Y)
        gate = dot(own, own_gate_ref[0, :, columns]) + dot(other, other_gate_ref[0, :, columns])
        up = dot(own, own_up_ref[0, :, columns]) + dot(other, other_up_ref[0, :, columns])
        out_ref[place, :CLASS, :] = gate.astype(BF16)
        out_ref[place, CLASS : 2 * CLASS, :] = up.astype(BF16)
        out_ref[place, 2 * CLASS :, :] = squares


def hidden_kernel(parts_ref, out_ref):
    gate = jnp.sum(parts_ref[:, :CLASS, :].astype(F32), axis=0)
    up = jnp.sum(parts_ref[:, CLASS : 2 * CLASS, :].astype(F32), axis=0)
    squares = jnp.sum(parts_ref[:, 2 * CLASS :, :].astype(F32), axis=0)
    squares = jnp.sum(squares[:6], axis=0, keepdims=True)
    diagonal = iota((CLASS, CLASS), 0) == iota((CLASS, CLASS), 1)
    squares = jnp.sum(jnp.where(diagonal, squares, 0.0), axis=1, keepdims=True)
    scale = lax.rsqrt(squares / D + EPS)
    gate = gate * scale
    hidden = (gate / (1.0 + jnp.exp(-gate)) * (up * scale)).astype(BF16)
    for place in range(N_KV):
        out_ref[place] = hidden


def down_kernel(hidden_ref, down_ref, out_ref):
    out = jnp.zeros((TOKROWS, FEAT), F32)
    shape = (TOKROWS, CLASS)
    row, source = iota(shape, 0), iota(shape, 1)
    match = source == row // ROWS_TP * (ROWS_TP // 2) + row % (ROWS_TP // 2)
    for core in range(2):
        hidden = jnp.concatenate([hidden_ref[2 * chip + core] for chip in range(CHIPS)], axis=1)
        produced = dot(hidden, down_ref[0], NT).astype(BF16)
        back = (match & (row % ROWS_TP // (ROWS_TP // 2) == core)).astype(F32).astype(BF16)
        out = out + dot(back, produced)
    out_ref[...] = out.reshape(N_TP, ROWS_TP, FEAT).astype(BF16)


def mix_kernel(parts_ref, mine_ref, own_ref, other_ref, ids_ref, weights_ref, attended_ref, out_ref):
    own = own_ref[...].astype(F32)
    attended = jnp.where(own_half(own.shape, 0), own, swap_halves(other_ref[...].astype(F32)))
    attended_ref[...] = attended.astype(BF16)
    total = mine_ref[:ROWS_TP] + attended
    ids = ids_ref[...]
    weights = weights_ref[...]
    for expert in range(EXPERTS):
        share = jnp.sum(jnp.where(ids == expert, weights, 0.0), axis=1, keepdims=True)
        both = parts_ref[2 * expert].astype(F32) + parts_ref[2 * expert + 1].astype(F32)
        total = total + share * both
    out_ref[...] = total.astype(BF16)


def run(kernel, outs, *operands, scratch=(), cost=None, limit=40, after=()):
    single = not isinstance(outs, list)
    placed = [pl.BlockSpec(memory_space=pltpu.VMEM)] * (1 if single else len(outs))
    count = len(operands)

    def body(*refs):
        kernel(*refs[:count], *refs[count + len(after) :])

    return pl.pallas_call(
        body,
        out_shape=outs if single else tuple(outs),
        in_specs=[pl.BlockSpec(memory_space=pltpu.VMEM)] * count + [pl.BlockSpec(memory_space=pl.ANY)] * len(after),
        out_specs=placed[0] if single else tuple(placed),
        scratch_shapes=list(scratch),
        cost_estimate=cost,
        compiler_params=pltpu.CompilerParams(vmem_limit_bytes=limit * 2**20),
    )(*operands, *after)


def shaped(*shape, dtype=BF16):
    return jax.ShapeDtypeStruct(shape, dtype)


def start(tokens, attn_gain, down_kv, key_up, value_up, mlp_gain):
    return run(
        start_kernel, [shaped(CHIPS, UP_ROWS + FRESH_ROWS, 128), shaped(16, FEAT, dtype=F32)],
        tokens, attn_gain.reshape(1, FEAT), down_kv, jnp.swapaxes(key_up, 1, 2), value_up,
        mlp_gain.reshape(1, FEAT), limit=60,
    )


def own_sum(ups):
    return run(sum_kernel, shaped(FRESH_ROWS, 128, dtype=F32), ups)


def fresh(own, other, latent_gain, lengths, after):
    freq = 10000.0 ** (-2.0 * jnp.arange(ROPE // 2, dtype=F32) / ROPE)
    return run(
        fresh_kernel, shaped(N_TP, ROWS_TP, KEY_W),
        own, other, latent_gain.reshape(1, LAT), lengths.reshape(1, SEQS), freq[None], after=after,
    )


def attend(lengths, own, other, query_nope, query_rope, cache):
    return run(
        attend_kernel,
        [
            shaped(TOKROWS, ATT_W),
            shaped(HEADS_DEV * ROWS_KV, KEY),
            shaped(2 * HEADS_DEV, N_KV, LAT_KV, 128),
        ],
        lengths.reshape(1, SEQS), own, other, query_nope, query_rope, jnp.swapaxes(cache, 1, 2),
        scratch=[pltpu.VMEM((SEQS, HEADS_DEV * TOKROWS // SEQS, KEY), BF16)],
        cost=pl.CostEstimate(flops=2_200_000_000, bytes_accessed=4_000_000, transcendentals=800_000),
    )


def merge(parts, own, ups, keys, after):
    return run(merge_kernel, shaped(TOKROWS, ATT_W), parts, own, ups, keys, after=after)


def combine(parts):
    return run(combine_kernel, shaped(CHIPS, ROWS_KV, HEADS_DEV * VDIM), parts)


def project(values, own, other):
    return run(project_kernel, shaped(N_TP, ROWS_TP, FEAT), values, own, other)


def route(parts, mine, other):
    return run(route_kernel, [shaped(ROWS_TP, FEAT), shaped(N_TP, ROWS_TP, 512)], parts, mine, other)


def gate(rows, own_gate, own_up, other_gate, other_up):
    return run(gate_kernel, shaped(CHIPS, PART_ROWS, 128), rows, own_gate, own_up, other_gate, other_up)


def hidden(parts):
    return run(hidden_kernel, shaped(N_KV, CLASS, HID_Y), parts)


def down(packed, down_proj):
    return run(down_kernel, shaped(N_TP, ROWS_TP, FEAT), packed, jnp.swapaxes(down_proj, 1, 2))


def mix(parts, mine, own, other, expert_ids, expert_weights):
    outs = [shaped(ROWS_TP, FEAT), shaped(ROWS_TP, FEAT)]
    return run(mix_kernel, outs, parts, mine, own, other, expert_ids, expert_weights)


def exchange(array, axis, groups=None):
    return lax.all_to_all(array, axis, split_axis=0, concat_axis=0, axis_index_groups=groups, tiled=True)


def along_y(array):
    return exchange(array, "kv", [[2 * chip + core for chip in range(CHIPS)] for core in range(2)])


def other_core(array):
    return lax.ppermute(array, "kv", [(index, index ^ 1) for index in range(N_KV)])


def per_device(
    tokens, attn_gain, down_kv, latent_gain, query_nope, query_rope, cache, lengths, key_up, value_up,
    out_proj, mlp_gain, expert_ids, expert_weights, gate_proj, up_proj, down_proj,
):
    ups, mine = start(tokens, attn_gain, down_kv, key_up, value_up, mlp_gain)
    out_own = out_proj.T
    ups, *moved = lax.optimization_barrier((ups, mine, out_own, gate_proj, up_proj))
    own = along_y(ups)
    moved = [other_core(array) for array in moved]
    part = own_sum(own)
    keys = fresh(part, other_core(part), latent_gain, lengths, moved[2:])
    keys, own = lax.optimization_barrier((keys, own))
    keys = exchange(keys, "tp")
    parts, queries, ups = attend(lengths, own, other_core(own), query_nope, query_rope, cache)
    parts = merge(parts, queries, ups, keys, moved[:2])
    parts = exchange(parts.reshape(N_KV, ROWS_KV, ATT_W), "kv")
    values = along_y(combine(parts))
    parts = exchange(project(values, out_own, moved[1]), "tp")
    attended, rows = route(parts, mine, moved[0])
    other_attended = other_core(attended)
    rows = exchange(rows, "tp")
    parts = along_y(gate(rows, gate_proj, up_proj, moved[2], moved[3]))
    packed = exchange(hidden(parts), "kv")
    parts = exchange(down(packed, down_proj), "tp")
    return mix(parts, mine, attended, other_attended, expert_ids, expert_weights)


def solution(mesh):
    return jax.shard_map(
        per_device,
        mesh=mesh,
        in_specs=(
            P("tp", "kv"),
            P("kv"),
            P("kv", None),
            P(),
            P(None, "tp"),
            P(None, "tp"),
            P(None, "kv", None),
            P(),
            P("tp", None, "kv"),
            P("tp", "kv", None),
            P("tp", "kv"),
            P("kv"),
            P("tp", None),
            P("tp", None),
            P("tp", "kv", None),
            P("tp", "kv", None),
            P("tp", None, "kv"),
        ),
        out_specs=(P("tp", "kv"), P("tp", "kv")),
        check_vma=False,
    )
```

time: 695 us -> 193 us (0.28)
  waiting for transfers between devices: 360 us -> 20.8 us
  blocking collectives: 272 us -> 102 us
  starting transfers between devices: 0.34 us -> 46.3 us
  matrix products: 25.2 us -> 0 us
  Pallas kernels: 0 us -> 16.7 us
  between operations: 14.3 us -> 0.88 us
  other arithmetic: 10.3 us -> 0.01 us
    reduce_scatter x2 -> x0, waiting for transfers between devices: 243 us -> none  [the longest x1 216 us: per_device(): lax.psum_scatter(jnp.dot(values, out_proj, preferred_element_type=jnp.flo...]
    psum x4 -> x0, blocking collectives: 153 us -> none  [the longest x1 51.2 us: per_device(): values = lax.psum(value_part, 'kv').astype(jnp.bfloat16)]
    psum x1 -> x0, waiting for transfers between devices: 117 us -> none  [per_device(): gate, upward = lax.psum((gate_part, up_part), 'kv')]
    all_to_all x2 -> x6, blocking collectives: 39.7 us -> 102 us  [exchange(): lax.all_to_all(array, axis, split_axis=0, concat_axis=0, axis_index_group...]
    all_gather x1 -> x0, blocking collectives: 41.1 us -> none  [per_device(): fresh_key = lax.all_gather(own_key, 'tp', axis=0, tiled=True)]
    pmax x1 -> x0, blocking collectives: 38.4 us -> none  [per_device(): best = lax.pmax(peak, 'kv')]
    all_to_all x0 -> x3, starting transfers between devices: none -> 25.7 us  [exchange(): lax.all_to_all(array, axis, split_axis=0, concat_axis=0, axis_index_group...]
    dot_general x15 -> x0, matrix products: 25.2 us -> none  [the longest x1 4.71 us: per_device(): jnp.einsum('sbjhc,tbjc->sbjht', step_piece, fresh_keys, preferred_element...]
  transfers between devices with their start and end apart: 4 -> 10, of which waited for: 3 -> 4; matrix products, arithmetic and copies ran while one was open for 2% -> 0% of each run, Pallas kernels for 0% -> 3%
where the time goes in v1:
time: 193 us; the launch traced here: 192 us
  blocking collectives  102 us (53%)
  starting transfers between devices  46.3 us (24%)
  waiting for transfers between devices  20.8 us (11%)
  Pallas kernels  16.7 us (9%)
  local copies, waits for them, and re-layouts  5.57 us (3%)
    all_to_all x6, blocking collectives, exchange(): lax.all_to_all(array, axis, split_axis=0, concat_axis=0, axis_index_group...  102 us
    all_to_all x3, starting transfers between devices, exchange(): lax.all_to_all(array, axis, split_axis=0, concat_axis=0, axis_index_group...  25.7 us
    ppermute x7, starting transfers between devices, other_core(): lax.ppermute(array, 'kv', [(index, index ^ 1) for index in range(N_KV)])  20.6 us
    all_to_all x3, waiting for transfers between devices, exchange(): lax.all_to_all(array, axis, split_axis=0, concat_axis=0, axis_index_group...  18.9 us
    pallas_call x12, Pallas kernels, run(): pl.pallas_call(body, out_shape=outs if single else tuple(outs), in_specs=...  16.7 us
    unnamed x28, local copies, waits for them, and re-layouts  5.57 us
  transfers between devices with their start and end apart: 10, of which 4 were waited for; matrix products, arithmetic and copies ran while one was open for 0% of the time, Pallas kernels for 3%

profile of v1, /device:TPU:1, one launch (start us, length us, event | category | flops | bytes accessed | tf_op | source)
XLA Modules:
  0.0 192.1 jit_solution(14622577585144707445)
XLA Ops:
  0.6 0.0 copy-start.3
  0.6 0.0 copy-start.10
  0.7 0.0 copy-start.9
  0.7 2.2 %shard_map.176 = (bf16[8,304,128]{2,1,0:T(8,128)(2,1)}, f32[16,448]{1,0:T(8,128)}) custom-call(bf16[8,448]{1,0:T(8,128)(2,1)} %refs_0_.1, f32[1,448]{1,0:T(1,128)} %bitcast.16, bf16[448,576]{1,0:T(8,128)(2,1)} %refs_2_.2, bf16[4,32,128]{2,1,0:T(8,128)(2,1)} %bitcast.15, bf16[4,32,128]{2,1,0:T(8,128)(2,1)} %refs_4_.3, f32[1,448]{1,0:T(1,128)} %bitcast.17), custom_call_target="tpu_custom_call" | custom-call | tf_op jit(solution)/shard_map/pallas_call | solution.py:338
  2.9 7.7 %all-to-all-start = ((bf16[8,304,128]{2,1,0:T(8,128)(2,1)}), bf16[8,304,128]{2,1,0:T(8,128)(2,1)S(1)}, u32[]{:S(2)}, u32[]{:S(2)}) async-start(bf16[8,304,128]{2,1,0:T(8,128)(2,1)} %get-tuple-element.18), calls=%async_computation | async-start | bytes 1245184 | tf_op jit(solution)/shard_map/all_to_all | solution.py:421
  10.5 0.0 copy-done.3
  10.5 0.0 copy-start.6
  10.6 4.7 %collective-permute-start.1 = (bf16[1,448,1024]{2,1,0:T(8,128)(2,1)S(1)}, bf16[1,448,1024]{2,1,0:T(8,128)(2,1)S(1)}, u32[]{:S(2)}, u32[]{:S(2)}) collective-permute-start(bf16[1,448,1024]{2,1,0:T(8,128)(2,1)S(1)} %copy-done.3), channel_id=1, source_target_pairs={{0,32},{32,0},{64,96},{96,64},{128,160},{160,128},{192,224},{224,1... | collective-permute-start | bytes 2752520 | tf_op jit(solution)/shard_map/ppermute | solution.py:429
  15.3 1.9 %collective-permute-start.2 = (bf16[1,448,1024]{2,1,0:T(8,128)(2,1)}, bf16[1,448,1024]{2,1,0:T(8,128)(2,1)S(1)}, u32[]{:S(2)}, u32[]{:S(2)}) collective-permute-start(bf16[1,448,1024]{2,1,0:T(8,128)(2,1)} %refs_2_.3), channel_id=1, source_target_pairs={{0,32},{32,0},{64,96},{96,64},{128,160},{160,128},{192,224},{224,1... | collective-permute-start | bytes 2752520 | tf_op jit(solution)/shard_map/ppermute | solution.py:429
  17.2 10.7 %all-to-all-done.refs_0_.refs_1_ = bf16[8,304,128]{2,1,0:T(8,128)(2,1)S(1)} async-done(((bf16[8,304,128]{2,1,0:T(8,128)(2,1)}), bf16[8,304,128]{2,1,0:T(8,128)(2,1)S(1)}, u32[]{:S(2)}, u32[]{:S(2)}) %all-to-all-start) | async-done | bytes 622624 | tf_op jit(solution)/shard_map/all_to_all | solution.py:421
  27.9 5.2 %collective-permute-start = (f32[48,128]{1,0:T(8,128)S(1)}, f32[48,128]{1,0:T(8,128)S(1)}, u32[]{:S(2)}, u32[]{:S(2)}) collective-permute-start(f32[48,128]{1,0:T(8,128)S(1)} %shard_map.177.refs_0_), channel_id=1, source_target_pairs={{0,32},{32,0},{64,96},{96,64},{128,160},{160,128},{192,224},{224,1... | collective-permute-start | bytes 73736 | tf_op jit(solution)/shard_map/ppermute | solution.py:429
  33.1 0.0 collective-permute-done.1.refs_5_.refs_3_
  33.1 0.0 collective-permute-done.2.refs_6_.refs_4_
  33.1 0.8 collective-permute-done.refs_1_
  33.9 0.0 copy-done.10
  33.9 0.0 copy-done.9
  33.9 1.0 shard_map.178
  34.9 2.2 %collective-permute-start.3 = (bf16[8,304,128]{2,1,0:T(8,128)(2,1)S(1)}, bf16[8,304,128]{2,1,0:T(8,128)(2,1)}, u32[]{:S(2)}, u32[]{:S(2)}) collective-permute-start(bf16[8,304,128]{2,1,0:T(8,128)(2,1)S(1)} %all-to-all-done.refs_0_.refs_1_), channel_id=1, source_target_pairs={{0,32},{32,0},{64,96},{96,64},{128,160},{160,128},{192,224},{224,1... | collective-permute-start | bytes 1867784 | tf_op jit(solution)/shard_map/ppermute | solution.py:429
  37.2 2.1 %collective-permute-start.5 = (bf16[448,512]{1,0:T(8,128)(2,1)}, bf16[448,512]{1,0:T(8,128)(2,1)S(1)}, u32[]{:S(2)}, u32[]{:S(2)}) collective-permute-start(bf16[448,512]{1,0:T(8,128)(2,1)} %bitcast.4.refs_1_), channel_id=1, source_target_pairs={{0,32},{32,0},{64,96},{96,64},{128,160},{160,128},{192,224},{224,1... | collective-permute-start | bytes 1376264 | tf_op jit(solution)/shard_map/ppermute | solution.py:429
  39.3 13.0 %all-to-all-start.1 = ((bf16[32,8,384]{2,1,0:T(8,128)(2,1)}), bf16[32,8,384]{2,1,0:T(8,128)(2,1)}, u32[]{:S(2)}, u32[]{:S(2)}) async-start(bf16[32,8,384]{2,1,0:T(8,128)(2,1)} %shard_map.178), calls=%async_computation.1 | async-start | bytes 393216 | tf_op jit(solution)/shard_map/all_to_all | solution.py:421
  52.2 0.0 copy-done.6
  52.2 2.5 %collective-permute-start.4 = (f32[16,448]{1,0:T(8,128)S(1)}, f32[16,448]{1,0:T(8,128)S(1)}, u32[]{:S(2)}, u32[]{:S(2)}) collective-permute-start(f32[16,448]{1,0:T(8,128)S(1)} %copy-done.6), channel_id=1, source_target_pairs={{0,32},{32,0},{64,96},{96,64},{128,160},{160,128},{192,224},{224,1... | collective-permute-start | bytes 86024 | tf_op jit(solution)/shard_map/ppermute | solution.py:429
  54.8 0.0 collective-permute-done.3.refs_2_
  54.8 0.0 copy-start.11
  54.8 1.5 copy-done.11
  56.3 0.0 copy-start.12
  56.3 0.9 copy-done.12
  57.2 0.0 copy-start.13
  57.2 0.9 copy-done.13
  58.1 5.3 %shard_map.179 = (bf16[256,640]{1,0:T(8,128)(2,1)S(1)}, bf16[64,576]{1,0:T(8,128)(2,1)S(1)}, bf16[8,16,32,128]{3,2,1,0:T(8,128)(2,1)S(1)}) custom-call(s32[1,2]{1,0:T(1,128)S(1)} %bitcast.13, bf16[8,304,128]{2,1,0:T(8,128)(2,1)S(1)} %all-to-all-done.refs_0_.refs_1_, bf16[8,304,128]{2,1,0:T(8,128)(2,1)} %collective-permute-done.3.refs_2_, ...), custom_call_target="tpu_custom_call" | custom-call | flops 2200000000 | bytes 4000000 | tf_op jit(solution)/shard_map/pallas_call | solution.py:338
  63.5 0.0 copy-start
  63.5 1.0 copy-done
  64.5 0.0 collective-permute-done.4.refs_4_.refs_2_
  64.5 0.0 collective-permute-done.5.refs_5_.refs_2_
  64.5 0.0 all-to-all-done.1.refs_3_
  64.5 0.0 copy-start.1
  64.5 1.2 copy-done.1
  65.7 1.5 shard_map.180
  67.2 15.5 %all_to_all.45.refs_0_ = bf16[16,16,640]{2,1,0:T(8,128)(2,1)S(1)} all-to-all(bf16[16,16,640]{2,1,0:T(8,128)(2,1)S(1)} %bitcast.9), channel_id=1, replica_groups=mesh['kv'=16,'tp'=32] {'kv'}, dimensions={0} | all-to-all | bytes 655360 | tf_op jit(solution)/shard_map/all_to_all | solution.py:421
  82.7 0.0 copy-start.4
  82.7 0.7 shard_map.181
  83.4 10.8 %all_to_all.46.refs_0_ = bf16[8,16,512]{2,1,0:T(8,128)(2,1)S(1)} all-to-all(bf16[8,16,512]{2,1,0:T(8,128)(2,1)S(1)} %shard_map.181), channel_id=1, replica_groups={{0,64,128,192,256,320,384,448},{32,96,160,224,288,352,416,480},{1,65,12..., dimensions={0} | all-to-all | bytes 262144 | tf_op jit(solution)/shard_map/all_to_all | solution.py:421
  94.2 1.7 shard_map.182
  95.8 18.8 %all_to_all.47.refs_0_ = bf16[32,8,448]{2,1,0:T(8,128)(2,1)S(1)} all-to-all(bf16[32,8,448]{2,1,0:T(8,128)(2,1)S(1)} %shard_map.182), channel_id=1, replica_groups=mesh['kv'=16,'tp'=32] {'tp'}, dimensions={0} | all-to-all | bytes 458752 | tf_op jit(solution)/shard_map/all_to_all | solution.py:421
  114.7 0.2 shard_map.183
  114.9 14.8 %all_to_all.48.refs_0_ = bf16[32,8,512]{2,1,0:T(8,128)(2,1)S(1)} all-to-all(bf16[32,8,512]{2,1,0:T(8,128)(2,1)S(1)} %get-tuple-element.28), channel_id=1, replica_groups=mesh['kv'=16,'tp'=32] {'tp'}, dimensions={0} | all-to-all | bytes 524288 | tf_op jit(solution)/shard_map/all_to_all | solution.py:421
  129.8 0.0 copy-done.4
  129.8 0.0 copy-done.5
  129.8 1.5 shard_map.184
  131.3 0.0 copy-start.2
  131.3 16.2 %all_to_all.49.refs_0_ = bf16[8,272,128]{2,1,0:T(8,128)(2,1)S(1)} all-to-all(bf16[8,272,128]{2,1,0:T(8,128)(2,1)S(1)} %shard_map.184), channel_id=1, replica_groups={{0,64,128,192,256,320,384,448},{32,96,160,224,288,352,416,480},{1,65,12..., dimensions={0} | all-to-all | bytes 1114112 | tf_op jit(solution)/shard_map/all_to_all | solution.py:421
  147.5 0.2 shard_map.185
  147.7 0.0 copy-start.7
  147.7 0.0 copy-start.8
  147.7 25.6 %all_to_all.50.refs_0_ = bf16[16,128,128]{2,1,0:T(8,128)(2,1)S(1)} all-to-all(bf16[16,128,128]{2,1,0:T(8,128)(2,1)S(1)} %shard_map.185), channel_id=1, replica_groups=mesh['kv'=16,'tp'=32] {'kv'}, dimensions={0} | all-to-all | bytes 1048576 | tf_op jit(solution)/shard_map/all_to_all | solution.py:421
  173.3 0.0 copy-done.2
  173.3 1.7 shard_map.186
  175.0 5.1 %all-to-all-start.8 = ((bf16[32,8,448]{2,1,0:T(8,128)(2,1)}), bf16[32,8,448]{2,1,0:T(8,128)(2,1)S(1)}, u32[]{:S(2)}, u32[]{:S(2)}) async-start(bf16[32,8,448]{2,1,0:T(8,128)(2,1)} %shard_map.186), calls=%async_computation.8 | async-start | bytes 524288 | tf_op jit(solution)/shard_map/all_to_all | solution.py:421
  180.1 1.9 collective-permute-start.6
  182.0 1.1 collective-permute-done.6.refs_3_
  183.2 8.2 %all-to-all-done.8.refs_0_ = bf16[32,8,448]{2,1,0:T(8,128)(2,1)S(1)} async-done(((bf16[32,8,448]{2,1,0:T(8,128)(2,1)}), bf16[32,8,448]{2,1,0:T(8,128)(2,1)S(1)}, u32[]{:S(2)}, u32[]{:S(2)}) %all-to-all-start.8) | async-done | bytes 229408 | tf_op jit(solution)/shard_map/all_to_all | solution.py:421
  191.4 0.0 copy-done.7
  191.4 0.0 copy-done.8
  191.4 0.7 shard_map.187
  (3 shorter events, 0.0 us)
Async XLA Ops:
  0.6 9.9 %copy-start.3 = (bf16[1,448,1024]{2,1,0:T(8,128)(2,1)S(1)}, bf16[1,448,1024]{2,1,0:T(8,128)(2,1)}, u32[]{:S(2)}) copy-start(bf16[1,448,1024]{2,1,0:T(8,128)(2,1)} %refs_1_.1) | copy-start | bytes 2752516
  0.6 33.3 %copy-start.10 = (s32[2]{0:T(128)S(1)}, s32[2]{0:T(128)}, u32[]{:S(2)}) copy-start(s32[2]{0:T(128)} %param.24) | copy-start | bytes 28
  0.7 33.3 %copy-start.9 = (f32[512]{0:T(512)S(1)}, f32[512]{0:T(512)}, u32[]{:S(2)}) copy-start(f32[512]{0:T(512)} %param.20) | copy-start | bytes 6148
  2.9 25.0 %all-to-all-start = ((bf16[8,304,128]{2,1,0:T(8,128)(2,1)}), bf16[8,304,128]{2,1,0:T(8,128)(2,1)S(1)}, u32[]{:S(2)}, u32[]{:S(2)}) async-start(bf16[8,304,128]{2,1,0:T(8,128)(2,1)} %get-tuple-element.18), calls=%async_computation | async-start | bytes 1245184 | tf_op jit(solution)/shard_map/all_to_all | solution.py:421
  10.5 41.7 %copy-start.6 = (f32[16,448]{1,0:T(8,128)S(1)}, f32[16,448]{1,0:T(8,128)}, u32[]{:S(2)}) copy-start(f32[16,448]{1,0:T(8,128)} %get-tuple-element.26.refs_1_) | copy-start | bytes 86020
  10.6 22.5 %collective-permute-start.1 = (bf16[1,448,1024]{2,1,0:T(8,128)(2,1)S(1)}, bf16[1,448,1024]{2,1,0:T(8,128)(2,1)S(1)}, u32[]{:S(2)}, u32[]{:S(2)}) collective-permute-start(bf16[1,448,1024]{2,1,0:T(8,128)(2,1)S(1)} %copy-done.3), channel_id=1, source_target_pairs={{0,32},{32,0},{64,96},{96,64},{128,160},{160,128},{192,224},{224,1... | collective-permute-start | bytes 2752520 | tf_op jit(solution)/shard_map/ppermute | solution.py:429
  15.3 17.9 %collective-permute-start.2 = (bf16[1,448,1024]{2,1,0:T(8,128)(2,1)}, bf16[1,448,1024]{2,1,0:T(8,128)(2,1)S(1)}, u32[]{:S(2)}, u32[]{:S(2)}) collective-permute-start(bf16[1,448,1024]{2,1,0:T(8,128)(2,1)} %refs_2_.3), channel_id=1, source_target_pairs={{0,32},{32,0},{64,96},{96,64},{128,160},{160,128},{192,224},{224,1... | collective-permute-start | bytes 2752520 | tf_op jit(solution)/shard_map/ppermute | solution.py:429
  27.9 6.0 %collective-permute-start = (f32[48,128]{1,0:T(8,128)S(1)}, f32[48,128]{1,0:T(8,128)S(1)}, u32[]{:S(2)}, u32[]{:S(2)}) collective-permute-start(f32[48,128]{1,0:T(8,128)S(1)} %shard_map.177.refs_0_), channel_id=1, source_target_pairs={{0,32},{32,0},{64,96},{96,64},{128,160},{160,128},{192,224},{224,1... | collective-permute-start | bytes 73736 | tf_op jit(solution)/shard_map/ppermute | solution.py:429
  34.9 19.9 %collective-permute-start.3 = (bf16[8,304,128]{2,1,0:T(8,128)(2,1)S(1)}, bf16[8,304,128]{2,1,0:T(8,128)(2,1)}, u32[]{:S(2)}, u32[]{:S(2)}) collective-permute-start(bf16[8,304,128]{2,1,0:T(8,128)(2,1)S(1)} %all-to-all-done.refs_0_.refs_1_), channel_id=1, source_target_pairs={{0,32},{32,0},{64,96},{96,64},{128,160},{160,128},{192,224},{224,1... | collective-permute-start | bytes 1867784 | tf_op jit(solution)/shard_map/ppermute | solution.py:429
  37.2 27.3 %collective-permute-start.5 = (bf16[448,512]{1,0:T(8,128)(2,1)}, bf16[448,512]{1,0:T(8,128)(2,1)S(1)}, u32[]{:S(2)}, u32[]{:S(2)}) collective-permute-start(bf16[448,512]{1,0:T(8,128)(2,1)} %bitcast.4.refs_1_), channel_id=1, source_target_pairs={{0,32},{32,0},{64,96},{96,64},{128,160},{160,128},{192,224},{224,1... | collective-permute-start | bytes 1376264 | tf_op jit(solution)/shard_map/ppermute | solution.py:429
  39.3 25.2 %all-to-all-start.1 = ((bf16[32,8,384]{2,1,0:T(8,128)(2,1)}), bf16[32,8,384]{2,1,0:T(8,128)(2,1)}, u32[]{:S(2)}, u32[]{:S(2)}) async-start(bf16[32,8,384]{2,1,0:T(8,128)(2,1)} %shard_map.178), calls=%async_computation.1 | async-start | bytes 393216 | tf_op jit(solution)/shard_map/all_to_all | solution.py:421
  52.2 12.2 %collective-permute-start.4 = (f32[16,448]{1,0:T(8,128)S(1)}, f32[16,448]{1,0:T(8,128)S(1)}, u32[]{:S(2)}, u32[]{:S(2)}) collective-permute-start(f32[16,448]{1,0:T(8,128)S(1)} %copy-done.6), channel_id=1, source_target_pairs={{0,32},{32,0},{64,96},{96,64},{128,160},{160,128},{192,224},{224,1... | collective-permute-start | bytes 86024 | tf_op jit(solution)/shard_map/ppermute | solution.py:429
  54.8 1.5 copy-start.11
  56.3 0.9 copy-start.12
  57.2 0.9 copy-start.13
  63.5 1.0 copy-start
  64.5 1.2 copy-start.1
  82.7 47.0 %copy-start.4 = (bf16[1,448,1024]{2,1,0:T(8,128)(2,1)S(1)}, bf16[1,448,1024]{2,1,0:T(8,128)(2,1)}, u32[]{:S(2)}) copy-start(bf16[1,448,1024]{2,1,0:T(8,128)(2,1)} %refs_1_.1) | copy-start | bytes 2752516
  82.7 47.0 %copy-start.5 = (bf16[1,448,1024]{2,1,0:T(8,128)(2,1)S(1)}, bf16[1,448,1024]{2,1,0:T(8,128)(2,1)}, u32[]{:S(2)}) copy-start(bf16[1,448,1024]{2,1,0:T(8,128)(2,1)} %refs_2_.3) | copy-start | bytes 2752516
  131.3 42.0 %copy-start.2 = (bf16[1,1024,448]{1,2,0:T(8,128)(2,1)S(1)}, bf16[1,1024,448]{1,2,0:T(8,128)(2,1)}, u32[]{:S(2)}) copy-start(bf16[1,1024,448]{1,2,0:T(8,128)(2,1)} %param.33) | copy-start | bytes 2752516
  147.7 43.7 %copy-start.7 = (s32[8,8]{1,0:T(8,128)S(1)}, s32[8,8]{1,0:T(8,128)}, u32[]{:S(2)}) copy-start(s32[8,8]{1,0:T(8,128)} %refs_4_.5) | copy-start | bytes 772
  147.7 43.7 %copy-start.8 = (f32[8,8]{1,0:T(8,128)S(1)}, f32[8,8]{1,0:T(8,128)}, u32[]{:S(2)}) copy-start(f32[8,8]{1,0:T(8,128)} %refs_5_.1) | copy-start | bytes 772
  175.0 16.4 %all-to-all-start.8 = ((bf16[32,8,448]{2,1,0:T(8,128)(2,1)}), bf16[32,8,448]{2,1,0:T(8,128)(2,1)S(1)}, u32[]{:S(2)}, u32[]{:S(2)}) async-start(bf16[32,8,448]{2,1,0:T(8,128)(2,1)} %shard_map.186), calls=%async_computation.8 | async-start | bytes 524288 | tf_op jit(solution)/shard_map/all_to_all | solution.py:421
  180.1 3.1 %collective-permute-start.6 = (bf16[8,448]{1,0:T(8,128)(2,1)S(1)}, bf16[8,448]{1,0:T(8,128)(2,1)S(1)}, u32[]{:S(2)}, u32[]{:S(2)}) collective-permute-start(bf16[8,448]{1,0:T(8,128)(2,1)S(1)} %get-tuple-element.29.refs_2_), channel_id=1, source_target_pairs={{0,32},{32,0},{64,96},{96,64},{128,160},{160,128},{192,224},{224,1... | collective-permute-start | bytes 21512 | tf_op jit(solution)/shard_map/ppermute | solution.py:429

commit v2 on v1

--- a/solution.py
+++ b/solution.py
@@ -86,12 +86,6 @@
     return tail[..., :STAT] + tail[..., STAT : 2 * STAT] + tail[..., 2 * STAT : 3 * STAT]
 
 
-def by_pair(transposed):
-    shape = (TOKROWS, TOKROWS)
-    paired, stepped = iota(shape, 1 if transposed else 0), iota(shape, 0 if transposed else 1)
-    return (stepped == paired % STEPS * PAIRS + paired // STEPS).astype(F32).astype(BF16)
-
-
 def swap_halves(rows):
     return pltpu.roll(rows, 4, 0)
 
@@ -139,16 +133,31 @@
 
 
 def attend_kernel(
-    lengths_ref, own_ups_ref, other_ups_ref, nope_ref, rope_ref, keys_ref,
-    out_ref, own_ref, ups_ref, queries,
+    lengths_ref, own_ups_hbm, other_ups_hbm, nope_hbm, rope_hbm, keys_hbm, other_keys_hbm,
+    out_ref, own_ref, ups_ref, queries, nope_ref, rope_ref, keys_ref, other_keys_ref, sems,
 ):
-    core = kv_index() % 2
-    rows_seq = TOKROWS // SEQS
-    for source, whose in ((own_ups_ref, core), (other_ups_ref, 1 - core)):
-        for chip in range(CHIPS):
-            for which in range(2 * HEADS_DEV):
-                ups_ref[which, 2 * chip + whose] = source[chip, which * LAT_KV : (which + 1) * LAT_KV, :]
-    reorder = by_pair(False)
+    kv = kv_index()
+    core = kv % 2
+    waits = []
+
+    def fetch(source, target):
+        waits.append(pltpu.make_async_copy(source, target, sems.at[len(waits)]))
+        waits[-1].start()
+
+    fetch(nope_hbm, nope_ref)
+    fetch(rope_hbm, rope_ref)
+    for which in range(2 * HEADS_DEV):
+        rows = pl.ds(which * LAT_KV, LAT_KV)
+        fetch(own_ups_hbm.at[:, rows, :], ups_ref.at[which, :, core])
+        fetch(other_ups_hbm.at[:, rows, :], ups_ref.at[which, :, 1 - core])
+    fetch(keys_hbm, keys_ref)
+    fetch(other_keys_hbm, other_keys_ref)
+    row, source = iota((CLASS, TOKROWS), 0), iota((CLASS, TOKROWS), 1)
+    pair = row // ROWS_KV * ROWS_TP + core * (ROWS_TP // 2) + row % ROWS_KV // STEPS
+    reorder = (source == row % STEPS * PAIRS + pair).astype(F32).astype(BF16)
+    rows_seq = CLASS // SEQS
+    for wait in waits[:-2]:
+        wait.wait()
     nope = dot(reorder, nope_ref[...]).astype(BF16)
     rope = dot(reorder, rope_ref[...]).astype(BF16)
     for head in range(HEADS_DEV):
@@ -160,20 +169,28 @@
             place = slice(head * rows_seq, (head + 1) * rows_seq)
             queries[seq, place, :LAT] = absorbed[rows]
             queries[seq, place, LAT:] = turned[rows]
-    own_seq = kv_index() // (N_KV // SEQS)
-    own_row = kv_index() % (N_KV // SEQS) * ROWS_KV
+    own_seq = kv // (N_KV // SEQS)
+    own_row = kv // 2 % (CHIPS // SEQS) * ROWS_KV
     for head in range(HEADS_DEV):
-        start = pl.multiple_of(head * rows_seq + own_row, ROWS_KV)
-        own_ref[head * ROWS_KV : (head + 1) * ROWS_KV, :] = queries[own_seq, pl.ds(start, ROWS_KV), :]
+        begin = pl.multiple_of(head * rows_seq + own_row, ROWS_KV)
+        own_ref[head * ROWS_KV : (head + 1) * ROWS_KV, :] = queries[own_seq, pl.ds(begin, ROWS_KV), :]
+    for wait in waits[-2:]:
+        wait.wait()
     span = keys_ref.shape[2]
     lengths = lengths_ref[...]
     for seq in range(SEQS):
-        valid = kv_index() * span + iota((1, span), 1) < lengths[:, seq : seq + 1]
-        scores = dot(queries[seq], keys_ref[seq]) * SCALE + jnp.where(valid, 0.0, LOWEST)
-        peak = jnp.max(scores, axis=1, keepdims=True)
-        weights = jnp.where(valid, jnp.exp(scores - peak), 0.0).astype(BF16)
-        total = jnp.sum(weights.astype(F32), axis=1, keepdims=True)
-        latent = dot(weights, keys_ref[seq, :LAT, :], NT).astype(BF16)
+        blocks = []
+        for keys, index in ((keys_ref, kv), (other_keys_ref, kv + 1 - 2 * core)):
+            valid = index * span + iota((1, span), 1) < lengths[:, seq : seq + 1]
+            scores = dot(queries[seq], keys[seq]) * SCALE + jnp.where(valid, 0.0, LOWEST)
+            blocks.append((keys, valid, scores, jnp.max(scores, axis=1, keepdims=True)))
+        peak = jnp.maximum(blocks[0][3], blocks[1][3])
+        total, latent = 0.0, 0.0
+        for keys, valid, scores, _ in blocks:
+            weights = jnp.where(valid, jnp.exp(scores - peak), 0.0).astype(BF16)
+            total = total + jnp.sum(weights.astype(F32), axis=1, keepdims=True)
+            latent = latent + dot(weights, keys[seq, :LAT, :], NT)
+        latent = latent.astype(BF16)
         stats = jnp.zeros((rows_seq, 128), F32)
         rows = slice(seq * rows_seq, (seq + 1) * rows_seq)
         for head in range(HEADS_DEV):
@@ -187,7 +204,7 @@
 def merge_kernel(parts_ref, own_ref, ups_ref, keys_ref, out_ref):
     kv = kv_index()
     out_ref[...] = parts_ref[...]
-    rows = pl.ds(pl.multiple_of(kv * ROWS_KV, ROWS_KV), ROWS_KV)
+    rows = pl.ds(pl.multiple_of(kv // 2 * ROWS_KV, ROWS_KV), ROWS_KV)
     mine = parts_ref[rows, :].astype(F32)
     stats = whole_stats(mine[:, LAT:])
     keys = []
@@ -249,13 +266,14 @@
     out_ref[...] = out.reshape(N_TP, ROWS_TP, FEAT).astype(BF16)
 
 
-def route_kernel(parts_ref, mine_ref, other_ref, attended_ref, out_ref):
+def route_kernel(parts_ref, mine_ref, other_ref, attended_ref, mid_ref, out_ref):
     attended = jnp.sum(parts_ref[...].astype(F32), axis=0).astype(BF16)
     attended_ref[...] = attended
     own = own_half((ROWS_TP, FEAT), 0)
     tokens = jnp.where(own, mine_ref[:ROWS_TP], swap_halves(other_ref[:ROWS_TP]))
     gain = jnp.where(own, mine_ref[ROWS_TP:], other_ref[ROWS_TP:])
     mid = tokens + attended.astype(F32)
+    mid_ref[...] = mid
     lane = iota((ROWS_TP, 512 - FEAT), 1)
     extra = jnp.zeros(lane.shape, F32)
     for at, part in enumerate(parts_of(jnp.sum(mid * mid, axis=1, keepdims=True))):
@@ -296,41 +314,51 @@
     scale = lax.rsqrt(squares / D + EPS)
     gate = gate * scale
     hidden = (gate / (1.0 + jnp.exp(-gate)) * (up * scale)).astype(BF16)
-    for place in range(N_KV):
+    for place in range(CHIPS):
         out_ref[place] = hidden
 
 
-def down_kernel(hidden_ref, down_ref, out_ref):
-    out = jnp.zeros((TOKROWS, FEAT), F32)
+def down_kernel(hidden_ref, own_ref, other_ref, out_ref):
+    hidden = jnp.concatenate([hidden_ref[chip] for chip in range(CHIPS)], axis=1)
     shape = (TOKROWS, CLASS)
     row, source = iota(shape, 0), iota(shape, 1)
     match = source == row // ROWS_TP * (ROWS_TP // 2) + row % (ROWS_TP // 2)
-    for core in range(2):
-        hidden = jnp.concatenate([hidden_ref[2 * chip + core] for chip in range(CHIPS)], axis=1)
-        produced = dot(hidden, down_ref[0], NT).astype(BF16)
-        back = (match & (row % ROWS_TP // (ROWS_TP // 2) == core)).astype(F32).astype(BF16)
-        out = out + dot(back, produced)
+    own = (match & own_half(shape, 0)).astype(F32).astype(BF16)
+    other = (match & ~own_half(shape, 0)).astype(F32).astype(BF16)
+    out = dot(own, dot(hidden, own_ref[0], NT).astype(BF16))
+    out = out + dot(other, dot(hidden, other_ref[0], NT).astype(BF16))
     out_ref[...] = out.reshape(N_TP, ROWS_TP, FEAT).astype(BF16)
 
 
-def mix_kernel(parts_ref, mine_ref, own_ref, other_ref, ids_ref, weights_ref, attended_ref, out_ref):
-    own = own_ref[...].astype(F32)
-    attended = jnp.where(own_half(own.shape, 0), own, swap_halves(other_ref[...].astype(F32)))
-    attended_ref[...] = attended.astype(BF16)
-    total = mine_ref[:ROWS_TP] + attended
-    ids = ids_ref[...]
+def mix_kernel(parts_ref, mid_ref, ids_ref, weights_ref, out_ref):
+    ids = ids_ref[...].astype(F32)
     weights = weights_ref[...]
+    own = own_half(ids.shape, 0)
+    ids = jnp.where(own, ids, swap_halves(ids))
+    weights = jnp.where(own, weights, swap_halves(weights))
+    total = mid_ref[...]
     for expert in range(EXPERTS):
-        share = jnp.sum(jnp.where(ids == expert, weights, 0.0), axis=1, keepdims=True)
+        share = jnp.sum(jnp.where(ids == float(expert), weights, 0.0), axis=1, keepdims=True)
         both = parts_ref[2 * expert].astype(F32) + parts_ref[2 * expert + 1].astype(F32)
         total = total + share * both
     out_ref[...] = total.astype(BF16)
 
 
-def run(kernel, outs, *operands, scratch=(), cost=None, limit=40, after=()):
+def finish_kernel(own_attended_ref, other_attended_ref, own_mixed_ref, other_mixed_ref, attended_ref, mixed_ref):
+    own = own_half((ROWS_TP, FEAT), 0)
+    for mine_ref, other_ref, out_ref in (
+        (own_attended_ref, other_attended_ref, attended_ref),
+        (own_mixed_ref, other_mixed_ref, mixed_ref),
+    ):
+        other = swap_halves(other_ref[...].astype(F32))
+        out_ref[...] = jnp.where(own, mine_ref[...].astype(F32), other).astype(BF16)
+
+
+def run(kernel, outs, *operands, fetched=(), scratch=(), cost=None, limit=40, after=()):
     single = not isinstance(outs, list)
     placed = [pl.BlockSpec(memory_space=pltpu.VMEM)] * (1 if single else len(outs))
-    count = len(operands)
+    count = len(operands) + len(fetched)
+    left = len(fetched) + len(after)
 
     def body(*refs):
         kernel(*refs[:count], *refs[count + len(after) :])
@@ -338,12 +366,12 @@
     return pl.pallas_call(
         body,
         out_shape=outs if single else tuple(outs),
-        in_specs=[pl.BlockSpec(memory_space=pltpu.VMEM)] * count + [pl.BlockSpec(memory_space=pl.ANY)] * len(after),
+        in_specs=[pl.BlockSpec(memory_space=pltpu.VMEM)] * len(operands) + [pl.BlockSpec(memory_space=pl.ANY)] * left,
         out_specs=placed[0] if single else tuple(placed),
         scratch_shapes=list(scratch),
         cost_estimate=cost,
         compiler_params=pltpu.CompilerParams(vmem_limit_bytes=limit * 2**20),
-    )(*operands, *after)
+    )(*operands, *fetched, *after)
 
 
 def shaped(*shape, dtype=BF16):
@@ -358,34 +386,43 @@
     )
 
 
-def own_sum(ups):
-    return run(sum_kernel, shaped(FRESH_ROWS, 128, dtype=F32), ups)
-
-
-def fresh(own, other, latent_gain, lengths, after):
+def own_sum(ups, after):
+    return run(sum_kernel, shaped(FRESH_ROWS, 128, dtype=F32), ups, after=after)
+
+
+def fresh(own, other, latent_gain, lengths):
     freq = 10000.0 ** (-2.0 * jnp.arange(ROPE // 2, dtype=F32) / ROPE)
     return run(
         fresh_kernel, shaped(N_TP, ROWS_TP, KEY_W),
-        own, other, latent_gain.reshape(1, LAT), lengths.reshape(1, SEQS), freq[None], after=after,
+        own, other, latent_gain.reshape(1, LAT), lengths.reshape(1, SEQS), freq[None],
     )
 
 
-def attend(lengths, own, other, query_nope, query_rope, cache):
+def attend(lengths, own, other, query_nope, query_rope, keys, other_keys):
     return run(
         attend_kernel,
         [
-            shaped(TOKROWS, ATT_W),
+            shaped(CLASS, ATT_W),
             shaped(HEADS_DEV * ROWS_KV, KEY),
-            shaped(2 * HEADS_DEV, N_KV, LAT_KV, 128),
+            shaped(2 * HEADS_DEV, CHIPS, 2, LAT_KV, 128),
         ],
-        lengths.reshape(1, SEQS), own, other, query_nope, query_rope, jnp.swapaxes(cache, 1, 2),
-        scratch=[pltpu.VMEM((SEQS, HEADS_DEV * TOKROWS // SEQS, KEY), BF16)],
+        lengths.reshape(1, SEQS),
+        fetched=(own, other, query_nope, query_rope, keys, other_keys),
+        scratch=[
+            pltpu.VMEM((SEQS, HEADS_DEV * CLASS // SEQS, KEY), BF16),
+            pltpu.VMEM(query_nope.shape, BF16),
+            pltpu.VMEM(query_rope.shape, BF16),
+            pltpu.VMEM(keys.shape, BF16),
+            pltpu.VMEM(keys.shape, BF16),
+            pltpu.SemaphoreType.DMA((4 + 4 * HEADS_DEV,)),
+        ],
         cost=pl.CostEstimate(flops=2_200_000_000, bytes_accessed=4_000_000, transcendentals=800_000),
+        limit=20,
     )
 
 
-def merge(parts, own, ups, keys, after):
-    return run(merge_kernel, shaped(TOKROWS, ATT_W), parts, own, ups, keys, after=after)
+def merge(parts, own, ups, keys):
+    return run(merge_kernel, shaped(CLASS, ATT_W), parts, own, ups, keys)
 
 
 def combine(parts):
@@ -397,7 +434,8 @@
 
 
 def route(parts, mine, other):
-    return run(route_kernel, [shaped(ROWS_TP, FEAT), shaped(N_TP, ROWS_TP, 512)], parts, mine, other)
+    outs = [shaped(ROWS_TP, FEAT), shaped(ROWS_TP, FEAT, dtype=F32), shaped(N_TP, ROWS_TP, 512)]
+    return run(route_kernel, outs, parts, mine, other)
 
 
 def gate(rows, own_gate, own_up, other_gate, other_up):
@@ -405,16 +443,20 @@
 
 
 def hidden(parts):
-    return run(hidden_kernel, shaped(N_KV, CLASS, HID_Y), parts)
-
-
-def down(packed, down_proj):
-    return run(down_kernel, shaped(N_TP, ROWS_TP, FEAT), packed, jnp.swapaxes(down_proj, 1, 2))
-
-
-def mix(parts, mine, own, other, expert_ids, expert_weights):
+    return run(hidden_kernel, shaped(CHIPS, CLASS, HID_Y), parts)
+
+
+def down(packed, own, other):
+    return run(down_kernel, shaped(N_TP, ROWS_TP, FEAT), packed, own, other)
+
+
+def mix(parts, mid, expert_ids, expert_weights):
+    return run(mix_kernel, shaped(ROWS_TP, FEAT), parts, mid, expert_ids, expert_weights)
+
+
+def finish(own_attended, other_attended, own_mixed, other_mixed):
     outs = [shaped(ROWS_TP, FEAT), shaped(ROWS_TP, FEAT)]
-    return run(mix_kernel, outs, parts, mine, own, other, expert_ids, expert_weights)
+    return run(finish_kernel, outs, own_attended, other_attended, own_mixed, other_mixed)
 
 
 def exchange(array, axis, groups=None):
@@ -434,26 +476,28 @@
     out_proj, mlp_gain, expert_ids, expert_weights, gate_proj, up_proj, down_proj,
 ):
     ups, mine = start(tokens, attn_gain, down_kv, key_up, value_up, mlp_gain)
-    out_own = out_proj.T
-    ups, *moved = lax.optimization_barrier((ups, mine, out_own, gate_proj, up_proj))
+    own_cache, own_out, own_down = jnp.swapaxes(cache, 1, 2), out_proj.T, jnp.swapaxes(down_proj, 1, 2)
+    ups, *moved = lax.optimization_barrier((ups, own_cache, mine, own_out, gate_proj, up_proj, own_down))
     own = along_y(ups)
     moved = [other_core(array) for array in moved]
-    part = own_sum(own)
-    keys = fresh(part, other_core(part), latent_gain, lengths, moved[2:])
+    other_cache, other_mine, other_out, other_gate, other_up, other_down = moved
+    part = own_sum(own, moved)
+    keys = fresh(part, other_core(part), latent_gain, lengths)
     keys, own = lax.optimization_barrier((keys, own))
     keys = exchange(keys, "tp")
-    parts, queries, ups = attend(lengths, own, other_core(own), query_nope, query_rope, cache)
-    parts = merge(parts, queries, ups, keys, moved[:2])
-    parts = exchange(parts.reshape(N_KV, ROWS_KV, ATT_W), "kv")
+    parts, queries, ups = attend(lengths, own, other_core(own), query_nope, query_rope, own_cache, other_cache)
+    parts = merge(parts, queries, ups, keys)
+    parts = along_y(parts.reshape(CHIPS, ROWS_KV, ATT_W))
     values = along_y(combine(parts))
-    parts = exchange(project(values, out_own, moved[1]), "tp")
-    attended, rows = route(parts, mine, moved[0])
+    parts = exchange(project(values, own_out, other_out), "tp")
+    attended, mid, rows = route(parts, mine, other_mine)
     other_attended = other_core(attended)
     rows = exchange(rows, "tp")
-    parts = along_y(gate(rows, gate_proj, up_proj, moved[2], moved[3]))
-    packed = exchange(hidden(parts), "kv")
-    parts = exchange(down(packed, down_proj), "tp")
-    return mix(parts, mine, attended, other_attended, expert_ids, expert_weights)
+    parts = along_y(gate(rows, gate_proj, up_proj, other_gate, other_up))
+    packed = along_y(hidden(parts))
+    parts = exchange(down(packed, own_down, other_down), "tp")
+    mixed = mix(parts, mid, expert_ids, expert_weights)
+    return finish(attended, other_attended, mixed, other_core(mixed))
 
 
 def solution(mesh):

time: 193 us -> 184 us (0.953)
  blocking collectives: 102 us -> 80.9 us
  starting transfers between devices: 46.3 us -> 64.3 us
  waiting for transfers between devices: 20.8 us -> 9.97 us
  local copies, waits for them, and re-layouts: 5.57 us -> 10.2 us
    ppermute x7 -> x10, starting transfers between devices: 20.6 us -> 45.2 us  [other_core(): lax.ppermute(array, 'kv', [(index, index ^ 1) for index in range(N_KV)])]
    all_to_all x6, blocking collectives: 102 us -> 80.9 us  [exchange(): lax.all_to_all(array, axis, split_axis=0, concat_axis=0, axis_index_group...]
    all_to_all x3, waiting for transfers between devices: 18.9 us -> 5.64 us  [exchange(): lax.all_to_all(array, axis, split_axis=0, concat_axis=0, axis_index_group...]
    all_to_all x3, starting transfers between devices: 25.7 us -> 19.1 us  [exchange(): lax.all_to_all(array, axis, split_axis=0, concat_axis=0, axis_index_group...]
    unnamed x28 -> x40, local copies, waits for them, and re-layouts: 5.57 us -> 10.2 us
    ppermute x7 -> x10, waiting for transfers between devices: 1.94 us -> 4.33 us  [other_core(): lax.ppermute(array, 'kv', [(index, index ^ 1) for index in range(N_KV)])]
    pallas_call x12 -> x13, Pallas kernels: 16.7 us -> 16.4 us  [run(): pl.pallas_call(body, out_shape=outs if single else tuple(outs), in_specs=...]
  transfers between devices with their start and end apart: 10 -> 13, of which waited for: 4 -> 5; matrix products, arithmetic and copies ran while one was open for 0% -> 0% of each run, Pallas kernels for 3% -> 3%
where the time goes in v2:
time: 184 us; the launch traced here: 183 us
  blocking collectives  80.9 us (44%)
  starting transfers between devices  64.3 us (35%)
  Pallas kernels  16.4 us (9%)
  local copies, waits for them, and re-layouts  10.2 us (6%)
  waiting for transfers between devices  9.97 us (5%)
    all_to_all x6, blocking collectives, exchange(): lax.all_to_all(array, axis, split_axis=0, concat_axis=0, axis_index_group...  80.9 us
    ppermute x10, starting transfers between devices, other_core(): lax.ppermute(array, 'kv', [(index, index ^ 1) for index in range(N_KV)])  45.2 us
    all_to_all x3, starting transfers between devices, exchange(): lax.all_to_all(array, axis, split_axis=0, concat_axis=0, axis_index_group...  19.1 us
    pallas_call x13, Pallas kernels, run(): pl.pallas_call(body, out_shape=outs if single else tuple(outs), in_specs=...  16.4 us
    unnamed x40, local copies, waits for them, and re-layouts  10.2 us
    all_to_all x3, waiting for transfers between devices, exchange(): lax.all_to_all(array, axis, split_axis=0, concat_axis=0, axis_index_group...  5.64 us
    ppermute x10, waiting for transfers between devices, other_core(): lax.ppermute(array, 'kv', [(index, index ^ 1) for index in range(N_KV)])  4.33 us
  transfers between devices with their start and end apart: 13, of which 5 were waited for; matrix products, arithmetic and copies ran while one was open for 0% of the time, Pallas kernels for 3%

profile of v2, /device:TPU:1, one launch (start us, length us, event | category | flops | bytes accessed | tf_op | source)
XLA Modules:
  0.0 182.7 jit_solution(14308096017284677469)
XLA Ops:
  0.6 2.1 %shard_map.176 = (bf16[8,304,128]{2,1,0:T(8,128)(2,1)}, f32[16,448]{1,0:T(8,128)}) custom-call(bf16[8,448]{1,0:T(8,128)(2,1)} %refs_0_.1, f32[1,448]{1,0:T(1,128)} %bitcast.20, bf16[448,576]{1,0:T(8,128)(2,1)} %refs_2_.3, bf16[4,32,128]{2,1,0:T(8,128)(2,1)} %bitcast.19, bf16[4,32,128]{2,1,0:T(8,128)(2,1)} %refs_4_.2, f32[1,448]{1,0:T(1,128)} %bitcast.21), custom_call_target="tpu_custom_call" | custom-call | tf_op jit(solution)/shard_map/pallas_call | solution.py:366
  2.8 8.8 %collective-permute-start = (bf16[2,576,768]{2,1,0:T(8,128)(2,1)}, bf16[2,576,768]{2,1,0:T(8,128)(2,1)}, u32[]{:S(2)}, u32[]{:S(2)}) collective-permute-start(bf16[2,576,768]{2,1,0:T(8,128)(2,1)} %bitcast.17), channel_id=1, source_target_pairs={{0,32},{32,0},{64,96},{96,64},{128,160},{160,128},{192,224},{224,1... | collective-permute-start | bytes 5308424 | tf_op jit(solution)/shard_map/ppermute | solution.py:471
  11.6 0.0 copy-start.15
  11.6 0.0 copy-start.16
  11.6 3.6 %all-to-all-start = ((bf16[8,304,128]{2,1,0:T(8,128)(2,1)}), bf16[8,304,128]{2,1,0:T(8,128)(2,1)S(1)}, u32[]{:S(2)}, u32[]{:S(2)}) async-start(bf16[8,304,128]{2,1,0:T(8,128)(2,1)} %get-tuple-element.21), calls=%async_computation | async-start | bytes 1245184 | tf_op jit(solution)/shard_map/all_to_all | solution.py:463
  15.1 1.9 %collective-permute-start.3 = (bf16[1,448,1024]{2,1,0:T(8,128)(2,1)}, bf16[1,448,1024]{2,1,0:T(8,128)(2,1)S(1)}, u32[]{:S(2)}, u32[]{:S(2)}) collective-permute-start(bf16[1,448,1024]{2,1,0:T(8,128)(2,1)} %refs_1_.1), channel_id=1, source_target_pairs={{0,32},{32,0},{64,96},{96,64},{128,160},{160,128},{192,224},{224,1... | collective-permute-start | bytes 2752520 | tf_op jit(solution)/shard_map/ppermute | solution.py:471
  17.1 2.4 %collective-permute-start.4 = (bf16[1,448,1024]{2,1,0:T(8,128)(2,1)}, bf16[1,448,1024]{2,1,0:T(8,128)(2,1)S(1)}, u32[]{:S(2)}, u32[]{:S(2)}) collective-permute-start(bf16[1,448,1024]{2,1,0:T(8,128)(2,1)} %refs_2_.4), channel_id=1, source_target_pairs={{0,32},{32,0},{64,96},{96,64},{128,160},{160,128},{192,224},{224,1... | collective-permute-start | bytes 2752520 | tf_op jit(solution)/shard_map/ppermute | solution.py:471
  19.5 1.9 %collective-permute-start.5 = (bf16[1,448,1024]{2,1,0:T(8,128)(2,1)}, bf16[1,448,1024]{2,1,0:T(8,128)(2,1)S(1)}, u32[]{:S(2)}, u32[]{:S(2)}) collective-permute-start(bf16[1,448,1024]{2,1,0:T(8,128)(2,1)} %bitcast.9), channel_id=1, source_target_pairs={{0,32},{32,0},{64,96},{96,64},{128,160},{160,128},{192,224},{224,1... | collective-permute-start | bytes 2752520 | tf_op jit(solution)/shard_map/ppermute | solution.py:471
  21.4 2.4 %collective-permute-start.1 = (f32[16,448]{1,0:T(8,128)}, f32[16,448]{1,0:T(8,128)S(1)}, u32[]{:S(2)}, u32[]{:S(2)}) collective-permute-start(f32[16,448]{1,0:T(8,128)} %get-tuple-element.23.refs_1_), channel_id=1, source_target_pairs={{0,32},{32,0},{64,96},{96,64},{128,160},{160,128},{192,224},{224,1... | collective-permute-start | bytes 86024 | tf_op jit(solution)/shard_map/ppermute | solution.py:471
  23.8 1.0 collective-permute-done.1.refs_2_
  24.9 2.2 %collective-permute-start.2 = (bf16[448,512]{1,0:T(8,128)(2,1)}, bf16[448,512]{1,0:T(8,128)(2,1)S(1)}, u32[]{:S(2)}, u32[]{:S(2)}) collective-permute-start(bf16[448,512]{1,0:T(8,128)(2,1)} %bitcast.12), channel_id=1, source_target_pairs={{0,32},{32,0},{64,96},{96,64},{128,160},{160,128},{192,224},{224,1... | collective-permute-start | bytes 1376264 | tf_op jit(solution)/shard_map/ppermute | solution.py:471
  27.1 1.7 collective-permute-done.2.refs_3_.refs_2_
  28.8 0.8 copy-done
  29.6 0.0 collective-permute-done.3.refs_4_.refs_3_
  29.6 0.0 collective-permute-done.4.refs_5_.refs_4_
  29.6 0.0 collective-permute-done.5.refs_6_.refs_2_
  29.6 5.6 %all-to-all-done.refs_0_.refs_1_ = bf16[8,304,128]{2,1,0:T(8,128)(2,1)S(1)} async-done(((bf16[8,304,128]{2,1,0:T(8,128)(2,1)}), bf16[8,304,128]{2,1,0:T(8,128)(2,1)S(1)}, u32[]{:S(2)}, u32[]{:S(2)}) %all-to-all-start) | async-done | bytes 622624 | tf_op jit(solution)/shard_map/all_to_all | solution.py:463
  35.2 0.0 collective-permute-done.refs_1_.refs_6_
  35.2 1.0 copy-done.1
  36.3 0.6 copy-done.8
  36.9 2.3 %collective-permute-start.6 = (f32[48,128]{1,0:T(8,128)S(1)}, f32[48,128]{1,0:T(8,128)S(1)}, u32[]{:S(2)}, u32[]{:S(2)}) collective-permute-start(f32[48,128]{1,0:T(8,128)S(1)} %shard_map.177.refs_0_), channel_id=1, source_target_pairs={{0,32},{32,0},{64,96},{96,64},{128,160},{160,128},{192,224},{224,1... | collective-permute-start | bytes 73736 | tf_op jit(solution)/shard_map/ppermute | solution.py:471
  39.2 0.8 collective-permute-done.6.refs_1_
  40.0 0.0 copy-done.16
  40.0 0.3 shard_map.178
  40.4 0.7 copy-done.6
  41.1 2.2 %collective-permute-start.7 = (bf16[8,304,128]{2,1,0:T(8,128)(2,1)S(1)}, bf16[8,304,128]{2,1,0:T(8,128)(2,1)}, u32[]{:S(2)}, u32[]{:S(2)}) collective-permute-start(bf16[8,304,128]{2,1,0:T(8,128)(2,1)S(1)} %all-to-all-done.refs_0_.refs_1_), channel_id=1, source_target_pairs={{0,32},{32,0},{64,96},{96,64},{128,160},{160,128},{192,224},{224,1... | collective-permute-start | bytes 1867784 | tf_op jit(solution)/shard_map/ppermute | solution.py:471
  43.3 11.0 %all-to-all-start.1 = ((bf16[32,8,384]{2,1,0:T(8,128)(2,1)}), bf16[32,8,384]{2,1,0:T(8,128)(2,1)}, u32[]{:S(2)}, u32[]{:S(2)}) async-start(bf16[32,8,384]{2,1,0:T(8,128)(2,1)} %copy-done.6), calls=%async_computation.1 | async-start | bytes 393216 | tf_op jit(solution)/shard_map/all_to_all | solution.py:463
  54.3 0.0 collective-permute-done.7.refs_2_
  54.3 0.0 copy-start.17
  54.3 1.5 copy-done.17
  55.8 0.9 copy-done.18
  56.8 0.9 copy-done.19
  57.7 5.6 %shard_map.179 = (bf16[128,640]{1,0:T(8,128)(2,1)S(1)}, bf16[64,576]{1,0:T(8,128)(2,1)S(1)}, bf16[8,8,2,32,128]{4,3,2,1,0:T(8,128)(2,1)S(1)}) custom-call(s32[1,2]{1,0:T(1,128)S(1)} %bitcast.16, bf16[8,304,128]{2,1,0:T(8,128)(2,1)S(1)} %all-to-all-done.refs_0_.refs_1_, bf16[8,304,128]{2,1,0:T(8,128)(2,1)} %collective-permute-done.7.refs_2_, ...), custom_call_target="tpu_custom_call" | custom-call | flops 2200000000 | bytes 4000000 | tf_op jit(solution)/shard_map/pallas_call | solution.py:366
  63.3 0.0 copy-start.3
  63.3 1.0 copy-done.3
  64.3 0.6 copy-done.10
  64.9 0.0 all-to-all-done.1.refs_3_
  64.9 1.3 copy-done.4
  66.2 0.9 copy-done.11
  67.1 1.6 shard_map.180
  68.7 10.8 %all_to_all.45.refs_0_ = bf16[8,16,640]{2,1,0:T(8,128)(2,1)S(1)} all-to-all(bf16[8,16,640]{2,1,0:T(8,128)(2,1)S(1)} %bitcast.11), channel_id=1, replica_groups={{0,64,128,192,256,320,384,448},{32,96,160,224,288,352,416,480},{1,65,12..., dimensions={0} | all-to-all | bytes 327680 | tf_op jit(solution)/shard_map/all_to_all | solution.py:463
  79.5 0.4 shard_map.181
  79.9 10.3 %all_to_all.46.refs_0_ = bf16[8,16,512]{2,1,0:T(8,128)(2,1)S(1)} all-to-all(bf16[8,16,512]{2,1,0:T(8,128)(2,1)S(1)} %shard_map.181), channel_id=1, replica_groups={{0,64,128,192,256,320,384,448},{32,96,160,224,288,352,416,480},{1,65,12..., dimensions={0} | all-to-all | bytes 262144 | tf_op jit(solution)/shard_map/all_to_all | solution.py:463
  90.2 0.0 copy-done.2
  90.2 0.7 shard_map.182
  90.9 19.0 %all_to_all.47.refs_0_ = bf16[32,8,448]{2,1,0:T(8,128)(2,1)S(1)} all-to-all(bf16[32,8,448]{2,1,0:T(8,128)(2,1)S(1)} %shard_map.182), channel_id=1, replica_groups=mesh['kv'=16,'tp'=32] {'tp'}, dimensions={0} | all-to-all | bytes 458752 | tf_op jit(solution)/shard_map/all_to_all | solution.py:463
  109.9 0.2 shard_map.183
  110.1 14.0 %all_to_all.48.refs_0_ = bf16[32,8,512]{2,1,0:T(8,128)(2,1)S(1)} all-to-all(bf16[32,8,512]{2,1,0:T(8,128)(2,1)S(1)} %get-tuple-element.34), channel_id=1, replica_groups=mesh['kv'=16,'tp'=32] {'tp'}, dimensions={0} | all-to-all | bytes 524288 | tf_op jit(solution)/shard_map/all_to_all | solution.py:463
  124.1 3.0 %shard_map.184 = bf16[8,272,128]{2,1,0:T(8,128)(2,1)S(1)} custom-call(bf16[32,8,512]{2,1,0:T(8,128)(2,1)S(1)} %all_to_all.48.refs_0_, bf16[1,448,1024]{2,1,0:T(8,128)(2,1)} %refs_1_.1, bf16[1,448,1024]{2,1,0:T(8,128)(2,1)} %refs_2_.4, bf16[1,448,1024]{2,1,0:T(8,128)(2,1)S(1)} %collective-permute-done.3.refs_4_.refs_3_, ...), custom_call_target="tpu_custom_call" | custom-call | tf_op jit(solution)/shard_map/pallas_call | solution.py:366
  127.1 0.0 copy-start.5
  127.1 15.0 %all_to_all.49.refs_0_ = bf16[8,272,128]{2,1,0:T(8,128)(2,1)S(1)} all-to-all(bf16[8,272,128]{2,1,0:T(8,128)(2,1)S(1)} %shard_map.184), channel_id=1, replica_groups={{0,64,128,192,256,320,384,448},{32,96,160,224,288,352,416,480},{1,65,12..., dimensions={0} | all-to-all | bytes 1114112 | tf_op jit(solution)/shard_map/all_to_all | solution.py:463
  142.1 0.1 shard_map.185
  142.3 0.0 copy-start.13
  142.3 0.0 copy-start.14
  142.3 11.7 %all_to_all.50.refs_0_ = bf16[8,128,128]{2,1,0:T(8,128)(2,1)S(1)} all-to-all(bf16[8,128,128]{2,1,0:T(8,128)(2,1)S(1)} %shard_map.185), channel_id=1, replica_groups={{0,64,128,192,256,320,384,448},{32,96,160,224,288,352,416,480},{1,65,12..., dimensions={0} | all-to-all | bytes 524288 | tf_op jit(solution)/shard_map/all_to_all | solution.py:463
  154.0 1.7 shard_map.186
  155.6 4.5 %all-to-all-start.8 = ((bf16[32,8,448]{2,1,0:T(8,128)(2,1)}), bf16[32,8,448]{2,1,0:T(8,128)(2,1)S(1)}, u32[]{:S(2)}, u32[]{:S(2)}) async-start(bf16[32,8,448]{2,1,0:T(8,128)(2,1)} %shard_map.186), calls=%async_computation.8 | async-start | bytes 524288 | tf_op jit(solution)/shard_map/all_to_all | solution.py:463
  160.2 10.2 %collective-permute-start.8 = (bf16[8,448]{1,0:T(8,128)(2,1)S(1)}, bf16[8,448]{1,0:T(8,128)(2,1)S(1)}, u32[]{:S(2)}, u32[]{:S(2)}) collective-permute-start(bf16[8,448]{1,0:T(8,128)(2,1)S(1)} %get-tuple-element.33.refs_0_), channel_id=1, source_target_pairs={{0,32},{32,0},{64,96},{96,64},{128,160},{160,128},{192,224},{224,1... | collective-permute-start | bytes 21512 | tf_op jit(solution)/shard_map/ppermute | solution.py:471
  170.4 0.0 all-to-all-done.8.refs_0_
  170.4 0.1 shard_map.187.refs_2_
  170.5 10.8 %collective-permute-start.9 = (bf16[8,448]{1,0:T(8,128)(2,1)S(1)}, bf16[8,448]{1,0:T(8,128)(2,1)S(1)}, u32[]{:S(2)}, u32[]{:S(2)}) collective-permute-start(bf16[8,448]{1,0:T(8,128)(2,1)S(1)} %shard_map.187.refs_2_), channel_id=1, source_target_pairs={{0,32},{32,0},{64,96},{96,64},{128,160},{160,128},{192,224},{224,1... | collective-permute-start | bytes 21512 | tf_op jit(solution)/shard_map/ppermute | solution.py:471
  181.3 0.0 collective-permute-done.8.refs_1_
  181.3 0.8 collective-permute-done.9.refs_3_
  182.1 0.6 shard_map.188
  (22 shorter events, 0.1 us)
Async XLA Ops:
  2.8 32.4 %collective-permute-start = (bf16[2,576,768]{2,1,0:T(8,128)(2,1)}, bf16[2,576,768]{2,1,0:T(8,128)(2,1)}, u32[]{:S(2)}, u32[]{:S(2)}) collective-permute-start(bf16[2,576,768]{2,1,0:T(8,128)(2,1)} %bitcast.17), channel_id=1, source_target_pairs={{0,32},{32,0},{64,96},{96,64},{128,160},{160,128},{192,224},{224,1... | collective-permute-start | bytes 5308424 | tf_op jit(solution)/shard_map/ppermute | solution.py:471
  11.6 28.5 %copy-start.15 = (f32[512]{0:T(512)S(1)}, f32[512]{0:T(512)}, u32[]{:S(2)}) copy-start(f32[512]{0:T(512)} %param.20) | copy-start | bytes 6148
  11.6 28.5 %copy-start.16 = (s32[2]{0:T(128)S(1)}, s32[2]{0:T(128)}, u32[]{:S(2)}) copy-start(s32[2]{0:T(128)} %param.24) | copy-start | bytes 28
  11.6 23.6 %all-to-all-start = ((bf16[8,304,128]{2,1,0:T(8,128)(2,1)}), bf16[8,304,128]{2,1,0:T(8,128)(2,1)S(1)}, u32[]{:S(2)}, u32[]{:S(2)}) async-start(bf16[8,304,128]{2,1,0:T(8,128)(2,1)} %get-tuple-element.21), calls=%async_computation | async-start | bytes 1245184 | tf_op jit(solution)/shard_map/all_to_all | solution.py:463
  15.1 14.4 %collective-permute-start.3 = (bf16[1,448,1024]{2,1,0:T(8,128)(2,1)}, bf16[1,448,1024]{2,1,0:T(8,128)(2,1)S(1)}, u32[]{:S(2)}, u32[]{:S(2)}) collective-permute-start(bf16[1,448,1024]{2,1,0:T(8,128)(2,1)} %refs_1_.1), channel_id=1, source_target_pairs={{0,32},{32,0},{64,96},{96,64},{128,160},{160,128},{192,224},{224,1... | collective-permute-start | bytes 2752520 | tf_op jit(solution)/shard_map/ppermute | solution.py:471
  17.1 12.5 %collective-permute-start.4 = (bf16[1,448,1024]{2,1,0:T(8,128)(2,1)}, bf16[1,448,1024]{2,1,0:T(8,128)(2,1)S(1)}, u32[]{:S(2)}, u32[]{:S(2)}) collective-permute-start(bf16[1,448,1024]{2,1,0:T(8,128)(2,1)} %refs_2_.4), channel_id=1, source_target_pairs={{0,32},{32,0},{64,96},{96,64},{128,160},{160,128},{192,224},{224,1... | collective-permute-start | bytes 2752520 | tf_op jit(solution)/shard_map/ppermute | solution.py:471
  19.5 10.1 %collective-permute-start.5 = (bf16[1,448,1024]{2,1,0:T(8,128)(2,1)}, bf16[1,448,1024]{2,1,0:T(8,128)(2,1)S(1)}, u32[]{:S(2)}, u32[]{:S(2)}) collective-permute-start(bf16[1,448,1024]{2,1,0:T(8,128)(2,1)} %bitcast.9), channel_id=1, source_target_pairs={{0,32},{32,0},{64,96},{96,64},{128,160},{160,128},{192,224},{224,1... | collective-permute-start | bytes 2752520 | tf_op jit(solution)/shard_map/ppermute | solution.py:471
  21.4 3.5 %collective-permute-start.1 = (f32[16,448]{1,0:T(8,128)}, f32[16,448]{1,0:T(8,128)S(1)}, u32[]{:S(2)}, u32[]{:S(2)}) collective-permute-start(f32[16,448]{1,0:T(8,128)} %get-tuple-element.23.refs_1_), channel_id=1, source_target_pairs={{0,32},{32,0},{64,96},{96,64},{128,160},{160,128},{192,224},{224,1... | collective-permute-start | bytes 86024 | tf_op jit(solution)/shard_map/ppermute | solution.py:471
  24.9 3.9 %collective-permute-start.2 = (bf16[448,512]{1,0:T(8,128)(2,1)}, bf16[448,512]{1,0:T(8,128)(2,1)S(1)}, u32[]{:S(2)}, u32[]{:S(2)}) collective-permute-start(bf16[448,512]{1,0:T(8,128)(2,1)} %bitcast.12), channel_id=1, source_target_pairs={{0,32},{32,0},{64,96},{96,64},{128,160},{160,128},{192,224},{224,1... | collective-permute-start | bytes 1376264 | tf_op jit(solution)/shard_map/ppermute | solution.py:471
  28.8 0.8 copy-start
  35.2 1.0 copy-start.1
  36.3 0.6 copy-start.8
  36.9 3.2 %collective-permute-start.6 = (f32[48,128]{1,0:T(8,128)S(1)}, f32[48,128]{1,0:T(8,128)S(1)}, u32[]{:S(2)}, u32[]{:S(2)}) collective-permute-start(f32[48,128]{1,0:T(8,128)S(1)} %shard_map.177.refs_0_), channel_id=1, source_target_pairs={{0,32},{32,0},{64,96},{96,64},{128,160},{160,128},{192,224},{224,1... | collective-permute-start | bytes 73736 | tf_op jit(solution)/shard_map/ppermute | solution.py:471
  40.4 0.7 copy-start.6
  41.1 13.3 %collective-permute-start.7 = (bf16[8,304,128]{2,1,0:T(8,128)(2,1)S(1)}, bf16[8,304,128]{2,1,0:T(8,128)(2,1)}, u32[]{:S(2)}, u32[]{:S(2)}) collective-permute-start(bf16[8,304,128]{2,1,0:T(8,128)(2,1)S(1)} %all-to-all-done.refs_0_.refs_1_), channel_id=1, source_target_pairs={{0,32},{32,0},{64,96},{96,64},{128,160},{160,128},{192,224},{224,1... | collective-permute-start | bytes 1867784 | tf_op jit(solution)/shard_map/ppermute | solution.py:471
  43.3 21.6 %all-to-all-start.1 = ((bf16[32,8,384]{2,1,0:T(8,128)(2,1)}), bf16[32,8,384]{2,1,0:T(8,128)(2,1)}, u32[]{:S(2)}, u32[]{:S(2)}) async-start(bf16[32,8,384]{2,1,0:T(8,128)(2,1)} %copy-done.6), calls=%async_computation.1 | async-start | bytes 393216 | tf_op jit(solution)/shard_map/all_to_all | solution.py:463
  54.3 1.5 copy-start.17
  55.8 0.9 copy-start.18
  56.8 0.9 copy-start.19
  63.3 1.0 copy-start.3
  64.3 0.6 copy-start.10
  64.9 25.3 %copy-start.2 = (bf16[448,512]{1,0:T(8,128)(2,1)S(1)}, bf16[448,512]{1,0:T(8,128)(2,1)}, u32[]{:S(2)}) copy-start(bf16[448,512]{1,0:T(8,128)(2,1)} %copy-done) | copy-start | bytes 1376260
  64.9 1.3 copy-start.4
  66.2 0.9 copy-start.11
  67.1 23.1 %copy-start.7 = (bf16[512,448]{0,1:T(8,128)(2,1)S(1)}, bf16[512,448]{0,1:T(8,128)(2,1)}, u32[]{:S(2)}) copy-start(bf16[512,448]{0,1:T(8,128)(2,1)} %param.27) | copy-start | bytes 1376260
  68.6 41.3 %copy-start.9 = (f32[16,448]{1,0:T(8,128)S(1)}, f32[16,448]{1,0:T(8,128)}, u32[]{:S(2)}) copy-start(f32[16,448]{1,0:T(8,128)} %copy-done.8) | copy-start | bytes 86020
  68.6 41.3 %copy-start.12 = (f32[16,448]{1,0:T(8,128)S(1)}, f32[16,448]{1,0:T(8,128)}, u32[]{:S(2)}) copy-start(f32[16,448]{1,0:T(8,128)} %get-tuple-element.23.refs_1_) | copy-start | bytes 86020
  127.1 26.9 %copy-start.5 = (bf16[1,1024,448]{1,2,0:T(8,128)(2,1)S(1)}, bf16[1,1024,448]{1,2,0:T(8,128)(2,1)}, u32[]{:S(2)}) copy-start(bf16[1,1024,448]{1,2,0:T(8,128)(2,1)} %param.33) | copy-start | bytes 2752516
  142.3 28.1 %copy-start.13 = (s32[8,8]{1,0:T(8,128)S(1)}, s32[8,8]{1,0:T(8,128)}, u32[]{:S(2)}) copy-start(s32[8,8]{1,0:T(8,128)} %refs_2_.5) | copy-start | bytes 772
  142.3 28.1 %copy-start.14 = (f32[8,8]{1,0:T(8,128)S(1)}, f32[8,8]{1,0:T(8,128)}, u32[]{:S(2)}) copy-start(f32[8,8]{1,0:T(8,128)} %refs_3_.3) | copy-start | bytes 772
  155.6 14.7 %all-to-all-start.8 = ((bf16[32,8,448]{2,1,0:T(8,128)(2,1)}), bf16[32,8,448]{2,1,0:T(8,128)(2,1)S(1)}, u32[]{:S(2)}, u32[]{:S(2)}) async-start(bf16[32,8,448]{2,1,0:T(8,128)(2,1)} %shard_map.186), calls=%async_computation.8 | async-start | bytes 524288 | tf_op jit(solution)/shard_map/all_to_all | solution.py:463
  160.2 21.1 %collective-permute-start.8 = (bf16[8,448]{1,0:T(8,128)(2,1)S(1)}, bf16[8,448]{1,0:T(8,128)(2,1)S(1)}, u32[]{:S(2)}, u32[]{:S(2)}) collective-permute-start(bf16[8,448]{1,0:T(8,128)(2,1)S(1)} %get-tuple-element.33.refs_0_), channel_id=1, source_target_pairs={{0,32},{32,0},{64,96},{96,64},{128,160},{160,128},{192,224},{224,1... | collective-permute-start | bytes 21512 | tf_op jit(solution)/shard_map/ppermute | solution.py:471
  170.5 11.6 %collective-permute-start.9 = (bf16[8,448]{1,0:T(8,128)(2,1)S(1)}, bf16[8,448]{1,0:T(8,128)(2,1)S(1)}, u32[]{:S(2)}, u32[]{:S(2)}) collective-permute-start(bf16[8,448]{1,0:T(8,128)(2,1)S(1)} %shard_map.187.refs_2_), channel_id=1, source_target_pairs={{0,32},{32,0},{64,96},{96,64},{128,160},{160,128},{192,224},{224,1... | collective-permute-start | bytes 21512 | tf_op jit(solution)/shard_map/ppermute | solution.py:471

commit v3 on v2

--- a/solution.py
+++ b/solution.py
@@ -34,6 +34,9 @@
 UP_ROWS = 2 * HEADS_DEV * LAT_KV
 FRESH_W = KEY + ROPE
 FRESH_ROWS = 48
+TOKEN_AT = FRESH_ROWS
+GAIN_AT = TOKEN_AT + 4 * ROWS_TP
+PACK_ROWS = GAIN_AT + 4 * ROWS_TP
 CLASS = TOKROWS // 2
 PART_ROWS = 2 * CLASS + 16
 KEY_W = 384
@@ -90,9 +93,20 @@
     return pltpu.roll(rows, 4, 0)
 
 
+def in_tiles(rows):
+    rows = jnp.concatenate([rows, jnp.zeros((ROWS_TP, 512 - FEAT), F32)], axis=1)
+    return [rows[:, at * 128 : (at + 1) * 128] for at in range(4)]
+
+
+def from_tiles(tiles):
+    return jnp.concatenate([tiles[at * ROWS_TP : (at + 1) * ROWS_TP] for at in range(4)], axis=1)[:, :FEAT]
+
+
 def start_kernel(tokens_ref, gain_ref, down_ref, key_ref, value_ref, mlp_gain_ref, out_ref, mine_ref):
     wide_tokens = tokens_ref[...].astype(F32)
-    mine_ref[...] = jnp.concatenate([wide_tokens, jnp.broadcast_to(mlp_gain_ref[...], (8, FEAT))], axis=0)
+    mine_ref[...] = jnp.concatenate(
+        in_tiles(wide_tokens) + in_tiles(jnp.broadcast_to(mlp_gain_ref[...], (ROWS_TP, FEAT))), axis=0
+    )
     normed = (wide_tokens * gain_ref[...]).astype(BF16)
     fresh = dot(normed, down_ref[...])
     fresh = jnp.concatenate([fresh, jnp.zeros((ROWS_TP, ROPE), F32)], axis=1)
@@ -106,12 +120,21 @@
         out_ref[place, UP_ROWS:, :] = packed
 
 
-def sum_kernel(ups_ref, out_ref):
-    out_ref[...] = jnp.sum(ups_ref[:, UP_ROWS:, :].astype(F32), axis=0)
-
-
-def fresh_kernel(own_ref, other_ref, gain_ref, lengths_ref, freq_ref, out_ref):
-    packed = own_ref[...] + other_ref[...]
+def sum_kernel(ups_hbm, mine_hbm, out_ref, fresh_ref, mine_ref, sems):
+    fetches = [
+        pltpu.make_async_copy(ups_hbm.at[:, pl.ds(UP_ROWS, FRESH_ROWS), :], fresh_ref, sems.at[0]),
+        pltpu.make_async_copy(mine_hbm, mine_ref, sems.at[1]),
+    ]
+    for fetch in fetches:
+        fetch.start()
+    for fetch in fetches:
+        fetch.wait()
+    out_ref[FRESH_ROWS:, :] = mine_ref[...]
+    out_ref[:FRESH_ROWS, :] = jnp.sum(fresh_ref[...].astype(F32), axis=0)
+
+
+def fresh_kernel(own_ref, other_ref, gain_ref, lengths_ref, freq_ref, out_hbm, out_ref, sem):
+    packed = own_ref[:FRESH_ROWS, :] + other_ref[:FRESH_ROWS, :]
     tiles = [packed[at * ROWS_TP : (at + 1) * ROWS_TP] for at in range(FRESH_W // 128)]
     fresh = jnp.concatenate(tiles[:-1], axis=1)
     turn = tiles[-1][:, :ROPE]
@@ -130,11 +153,14 @@
     key = jnp.where(iota(upper.shape, 0) < ROWS_TP // 2, upper, lower).astype(BF16)
     for place in range(N_TP):
         out_ref[place] = key
+    leave = pltpu.make_async_copy(out_ref, out_hbm, sem)
+    leave.start()
+    leave.wait()
 
 
 def attend_kernel(
     lengths_ref, own_ups_hbm, other_ups_hbm, nope_hbm, rope_hbm, keys_hbm, other_keys_hbm,
-    out_ref, own_ref, ups_ref, queries, nope_ref, rope_ref, keys_ref, other_keys_ref, sems,
+    out_ref, own_hbm, values_hbm, ups_ref, own_ref, queries, nope_ref, rope_ref, keys_ref, other_keys_ref, sems,
 ):
     kv = kv_index()
     core = kv % 2
@@ -174,6 +200,12 @@
     for head in range(HEADS_DEV):
         begin = pl.multiple_of(head * rows_seq + own_row, ROWS_KV)
         own_ref[head * ROWS_KV : (head + 1) * ROWS_KV, :] = queries[own_seq, pl.ds(begin, ROWS_KV), :]
+    leaves = [
+        pltpu.make_async_copy(own_ref, own_hbm, sems.at[len(waits)]),
+        pltpu.make_async_copy(ups_ref.at[pl.ds(HEADS_DEV, HEADS_DEV)], values_hbm, sems.at[len(waits) + 1]),
+    ]
+    for leave in leaves:
+        leave.start()
     for wait in waits[-2:]:
         wait.wait()
     span = keys_ref.shape[2]
@@ -199,19 +231,26 @@
             out_ref[rows, head * VDIM : (head + 1) * VDIM] = dot(latent[place], value_up).astype(BF16)
             stats = with_stats(stats, head, peak[place], total[place])
         out_ref[rows, LAT:] = stats.astype(BF16)
-
-
-def merge_kernel(parts_ref, own_ref, ups_ref, keys_ref, out_ref):
+    for leave in leaves:
+        leave.wait()
+
+
+def combine_kernel(parts_ref, keys_ref, own_hbm, values_hbm, out_ref, own_ref, values_ref, sems):
+    fetches = [
+        pltpu.make_async_copy(own_hbm, own_ref, sems.at[0]),
+        pltpu.make_async_copy(values_hbm, values_ref, sems.at[1]),
+    ]
+    for fetch in fetches:
+        fetch.start()
     kv = kv_index()
-    out_ref[...] = parts_ref[...]
-    rows = pl.ds(pl.multiple_of(kv // 2 * ROWS_KV, ROWS_KV), ROWS_KV)
-    mine = parts_ref[rows, :].astype(F32)
-    stats = whole_stats(mine[:, LAT:])
+    stats = whole_stats(parts_ref[:, :, LAT:].astype(F32))
     keys = []
     for step in range(STEPS):
         block = keys_ref[step * (PAIRS // ROWS_TP) + kv // 2].astype(F32)
         keys.append(jnp.concatenate([block[:, :256], swap_halves(block[:, :256]), block[:, 256 : 256 + ROPE]], axis=1))
     keys = jnp.concatenate(keys, axis=0).astype(BF16)
+    for fetch in fetches:
+        fetch.wait()
     scores = dot(own_ref[...], keys, NT) * SCALE
     row = iota(scores.shape, 0) % ROWS_KV
     key = iota(scores.shape, 1)
@@ -221,32 +260,20 @@
     weights = jnp.where(causal, jnp.exp(scores - fresh_peak), 0.0).astype(BF16)
     fresh_total = jnp.sum(weights.astype(F32), axis=1, keepdims=True)
     fresh_latent = dot(weights, keys[:, :LAT]).astype(BF16)
-    tail = jnp.zeros((ROWS_KV, 128), F32)
-    merged = []
     for head in range(HEADS_DEV):
         own = slice(head * ROWS_KV, (head + 1) * ROWS_KV)
-        peak = stats[:, head : head + 1]
-        top = jnp.maximum(peak, fresh_peak[own])
-        keep = jnp.exp(peak - top)
-        fresh_keep = jnp.exp(fresh_peak[own] - top)
-        value_up = ups_ref[HEADS_DEV + head].reshape(LAT, VDIM)
-        part = mine[:, head * VDIM : (head + 1) * VDIM]
-        merged.append(part * keep + dot(fresh_latent[own], value_up) * fresh_keep)
-        total = stats[:, HEADS_DEV + head : HEADS_DEV + head + 1] * keep + fresh_total[own] * fresh_keep
-        tail = with_stats(tail, head, top, total)
-    out_ref[rows, :] = jnp.concatenate(merged + [tail], axis=1).astype(BF16)
-
-
-def combine_kernel(parts_ref, out_ref):
-    stats = whole_stats(parts_ref[:, :, LAT:].astype(F32))
-    for head in range(HEADS_DEV):
         peak = stats[:, :, head : head + 1]
         total = stats[:, :, HEADS_DEV + head : HEADS_DEV + head + 1]
-        keep = jnp.exp(peak - jnp.max(peak, axis=0, keepdims=True))
+        top = jnp.maximum(jnp.max(peak, axis=0), fresh_peak[own])
+        keep = jnp.exp(peak - top[None])
+        fresh_keep = jnp.exp(fresh_peak[own] - top)
+        value_up = values_ref[head].reshape(LAT, VDIM)
         part = parts_ref[:, :, head * VDIM : (head + 1) * VDIM].astype(F32)
-        value = jnp.sum(part * keep, axis=0) / jnp.sum(total * keep, axis=0)
+        value = jnp.sum(part * keep, axis=0) + dot(fresh_latent[own], value_up) * fresh_keep
+        whole = jnp.sum(total * keep, axis=0) + fresh_total[own] * fresh_keep
+        value = (value / whole).astype(BF16)
         for place in range(CHIPS):
-            out_ref[place, :, head * VDIM : (head + 1) * VDIM] = value.astype(BF16)
+            out_ref[place, :, head * VDIM : (head + 1) * VDIM] = value
 
 
 def own_half(shape, dim):
@@ -266,14 +293,13 @@
     out_ref[...] = out.reshape(N_TP, ROWS_TP, FEAT).astype(BF16)
 
 
-def route_kernel(parts_ref, mine_ref, other_ref, attended_ref, mid_ref, out_ref):
+def route_kernel(parts_ref, mine_ref, other_ref, attended_ref, out_ref):
     attended = jnp.sum(parts_ref[...].astype(F32), axis=0).astype(BF16)
     attended_ref[...] = attended
     own = own_half((ROWS_TP, FEAT), 0)
-    tokens = jnp.where(own, mine_ref[:ROWS_TP], swap_halves(other_ref[:ROWS_TP]))
-    gain = jnp.where(own, mine_ref[ROWS_TP:], other_ref[ROWS_TP:])
+    tokens = jnp.where(own, from_tiles(mine_ref[TOKEN_AT:, :]), swap_halves(from_tiles(other_ref[TOKEN_AT:, :])))
+    gain = jnp.where(own, from_tiles(mine_ref[GAIN_AT:, :]), from_tiles(other_ref[GAIN_AT:, :]))
     mid = tokens + attended.astype(F32)
-    mid_ref[...] = mid
     lane = iota((ROWS_TP, 512 - FEAT), 1)
     extra = jnp.zeros(lane.shape, F32)
     for at, part in enumerate(parts_of(jnp.sum(mid * mid, axis=1, keepdims=True))):
@@ -320,53 +346,64 @@
 
 def down_kernel(hidden_ref, own_ref, other_ref, out_ref):
     hidden = jnp.concatenate([hidden_ref[chip] for chip in range(CHIPS)], axis=1)
-    shape = (TOKROWS, CLASS)
+    shape = (4 * CLASS, 4 * CLASS)
     row, source = iota(shape, 0), iota(shape, 1)
-    match = source == row // ROWS_TP * (ROWS_TP // 2) + row % (ROWS_TP // 2)
-    own = (match & own_half(shape, 0)).astype(F32).astype(BF16)
-    other = (match & ~own_half(shape, 0)).astype(F32).astype(BF16)
-    out = dot(own, dot(hidden, own_ref[0], NT).astype(BF16))
-    out = out + dot(other, dot(hidden, other_ref[0], NT).astype(BF16))
-    out_ref[...] = out.reshape(N_TP, ROWS_TP, FEAT).astype(BF16)
-
-
-def mix_kernel(parts_ref, mid_ref, ids_ref, weights_ref, out_ref):
-    ids = ids_ref[...].astype(F32)
+    order = (source == row % 16 // 4 * CLASS + row // 16 * 4 + row % 4).astype(F32).astype(BF16)
+    core = kv_index() % 2
+    for weights_ref, whose in ((own_ref, core), (other_ref, 1 - core)):
+        rows = dot(hidden, weights_ref[0], NT)
+        rows = jnp.concatenate([rows, jnp.zeros((CLASS, 512 - FEAT), F32)], axis=1).astype(BF16)
+        tiles = jnp.concatenate([rows[:, at * 128 : (at + 1) * 128] for at in range(4)], axis=0)
+        place = pl.ds(pl.multiple_of(whose * N_TP, N_TP), N_TP)
+        out_ref[place] = dot(order, tiles).reshape(N_TP, 16, 128).astype(BF16)
+
+
+def mix_kernel(parts_ref, mine_ref, own_ref, other_ref, ids_ref, weights_ref, attended_ref, out_ref):
+    own = own_ref[...].astype(F32)
+    attended = jnp.where(own_half(own.shape, 0), own, swap_halves(other_ref[...].astype(F32)))
+    attended_ref[...] = attended.astype(BF16)
+    ids = ids_ref[...]
     weights = weights_ref[...]
-    own = own_half(ids.shape, 0)
-    ids = jnp.where(own, ids, swap_halves(ids))
-    weights = jnp.where(own, weights, swap_halves(weights))
-    total = mid_ref[...]
-    for expert in range(EXPERTS):
-        share = jnp.sum(jnp.where(ids == float(expert), weights, 0.0), axis=1, keepdims=True)
-        both = parts_ref[2 * expert].astype(F32) + parts_ref[2 * expert + 1].astype(F32)
-        total = total + share * both
-    out_ref[...] = total.astype(BF16)
-
-
-def finish_kernel(own_attended_ref, other_attended_ref, own_mixed_ref, other_mixed_ref, attended_ref, mixed_ref):
-    own = own_half((ROWS_TP, FEAT), 0)
-    for mine_ref, other_ref, out_ref in (
-        (own_attended_ref, other_attended_ref, attended_ref),
-        (own_mixed_ref, other_mixed_ref, mixed_ref),
-    ):
-        other = swap_halves(other_ref[...].astype(F32))
-        out_ref[...] = jnp.where(own, mine_ref[...].astype(F32), other).astype(BF16)
-
-
-def run(kernel, outs, *operands, fetched=(), scratch=(), cost=None, limit=40, after=()):
+    lane = iota((ROWS_TP, 128), 1)
+    upper = iota((ROWS_TP, 128), 0) < ROWS_TP // 2
+    shares = jnp.zeros(lane.shape, F32)
+    for choice in range(ids.shape[1]):
+        one = slice(choice, choice + 1)
+        shares = jnp.where(ids[:, one] == lane, weights[:, one], shares)
+    sums = []
+    for core in range(2):
+        mine = jnp.where(upper == (core == 0), shares, swap_halves(shares))
+        mine = jnp.concatenate([mine, mine], axis=0)
+        total = jnp.zeros((16, 128), F32)
+        for expert in range(EXPERTS):
+            at = core * N_TP + 2 * expert
+            both = parts_ref[at].astype(F32) + parts_ref[at + 1].astype(F32)
+            total = total + mine[:, expert : expert + 1] * both
+        sums.append(total)
+    tiles = []
+    for at in range(2):
+        first, second = (total[at * ROWS_TP : (at + 1) * ROWS_TP] for total in sums)
+        tiles.append(jnp.where(upper, first, swap_halves(second)))
+        tiles.append(jnp.where(upper, swap_halves(first), second))
+    experts = jnp.concatenate(tiles, axis=1)[:, :FEAT]
+    out_ref[...] = (from_tiles(mine_ref[TOKEN_AT:, :]) + attended + experts).astype(BF16)
+
+
+def run(kernel, outs, *operands, fetched=(), left=0, scratch=(), cost=None, limit=24, after=()):
     single = not isinstance(outs, list)
-    placed = [pl.BlockSpec(memory_space=pltpu.VMEM)] * (1 if single else len(outs))
+    outs = [outs] if single else outs
+    vmem, hbm, free = (pl.BlockSpec(memory_space=space) for space in (pltpu.VMEM, pltpu.HBM, pl.ANY))
+    outs = outs[: len(outs) - left] + [pltpu.HBM(out.shape, out.dtype) for out in outs[len(outs) - left :]]
+    placed = [vmem] * (len(outs) - left) + [hbm] * left
     count = len(operands) + len(fetched)
-    left = len(fetched) + len(after)
 
     def body(*refs):
         kernel(*refs[:count], *refs[count + len(after) :])
 
     return pl.pallas_call(
         body,
-        out_shape=outs if single else tuple(outs),
-        in_specs=[pl.BlockSpec(memory_space=pltpu.VMEM)] * len(operands) + [pl.BlockSpec(memory_space=pl.ANY)] * left,
+        out_shape=outs[0] if single else tuple(outs),
+        in_specs=[vmem] * len(operands) + [free] * (len(fetched) + len(after)),
         out_specs=placed[0] if single else tuple(placed),
         scratch_shapes=list(scratch),
         cost_estimate=cost,
@@ -374,20 +411,29 @@
     )(*operands, *fetched, *after)
 
 
+def in_hbm(array):
+    return pltpu.with_memory_space_constraint(array, pltpu.HBM)
+
+
 def shaped(*shape, dtype=BF16):
     return jax.ShapeDtypeStruct(shape, dtype)
 
 
 def start(tokens, attn_gain, down_kv, key_up, value_up, mlp_gain):
     return run(
-        start_kernel, [shaped(CHIPS, UP_ROWS + FRESH_ROWS, 128), shaped(16, FEAT, dtype=F32)],
+        start_kernel, [shaped(CHIPS, UP_ROWS + FRESH_ROWS, 128), shaped(8 * ROWS_TP, 128, dtype=F32)],
         tokens, attn_gain.reshape(1, FEAT), down_kv, jnp.swapaxes(key_up, 1, 2), value_up,
         mlp_gain.reshape(1, FEAT), limit=60,
     )
 
 
-def own_sum(ups, after):
-    return run(sum_kernel, shaped(FRESH_ROWS, 128, dtype=F32), ups, after=after)
+def own_sum(ups, mine, after):
+    return run(
+        sum_kernel, shaped(PACK_ROWS, 128, dtype=F32), fetched=(ups, in_hbm(mine)), after=after,
+        scratch=[
+            pltpu.VMEM((CHIPS, FRESH_ROWS, 128), BF16), pltpu.VMEM(mine.shape, F32), pltpu.SemaphoreType.DMA((2,)),
+        ],
+    )
 
 
 def fresh(own, other, latent_gain, lengths):
@@ -395,6 +441,7 @@
     return run(
         fresh_kernel, shaped(N_TP, ROWS_TP, KEY_W),
         own, other, latent_gain.reshape(1, LAT), lengths.reshape(1, SEQS), freq[None],
+        left=1, scratch=[pltpu.VMEM((N_TP, ROWS_TP, KEY_W), BF16), pltpu.SemaphoreType.DMA],
     )
 
 
@@ -404,29 +451,33 @@
         [
             shaped(CLASS, ATT_W),
             shaped(HEADS_DEV * ROWS_KV, KEY),
-            shaped(2 * HEADS_DEV, CHIPS, 2, LAT_KV, 128),
+            shaped(HEADS_DEV, CHIPS, 2, LAT_KV, 128),
         ],
         lengths.reshape(1, SEQS),
-        fetched=(own, other, query_nope, query_rope, keys, other_keys),
+        fetched=(own, other, in_hbm(query_nope), in_hbm(query_rope), in_hbm(keys), other_keys),
+        left=2,
         scratch=[
+            pltpu.VMEM((2 * HEADS_DEV, CHIPS, 2, LAT_KV, 128), BF16),
+            pltpu.VMEM((HEADS_DEV * ROWS_KV, KEY), BF16),
             pltpu.VMEM((SEQS, HEADS_DEV * CLASS // SEQS, KEY), BF16),
             pltpu.VMEM(query_nope.shape, BF16),
             pltpu.VMEM(query_rope.shape, BF16),
             pltpu.VMEM(keys.shape, BF16),
             pltpu.VMEM(keys.shape, BF16),
-            pltpu.SemaphoreType.DMA((4 + 4 * HEADS_DEV,)),
+            pltpu.SemaphoreType.DMA((6 + 4 * HEADS_DEV,)),
         ],
         cost=pl.CostEstimate(flops=2_200_000_000, bytes_accessed=4_000_000, transcendentals=800_000),
-        limit=20,
-    )
-
-
-def merge(parts, own, ups, keys):
-    return run(merge_kernel, shaped(CLASS, ATT_W), parts, own, ups, keys)
-
-
-def combine(parts):
-    return run(combine_kernel, shaped(CHIPS, ROWS_KV, HEADS_DEV * VDIM), parts)
+    )
+
+
+def combine(parts, own, values, keys):
+    return run(
+        combine_kernel, shaped(CHIPS, ROWS_KV, HEADS_DEV * VDIM), parts, keys,
+        fetched=(in_hbm(own), in_hbm(values)),
+        scratch=[
+            pltpu.VMEM(own.shape, BF16), pltpu.VMEM(values.shape, BF16), pltpu.SemaphoreType.DMA((2,)),
+        ],
+    )
 
 
 def project(values, own, other):
@@ -434,8 +485,7 @@
 
 
 def route(parts, mine, other):
-    outs = [shaped(ROWS_TP, FEAT), shaped(ROWS_TP, FEAT, dtype=F32), shaped(N_TP, ROWS_TP, 512)]
-    return run(route_kernel, outs, parts, mine, other)
+    return run(route_kernel, [shaped(ROWS_TP, FEAT), shaped(N_TP, ROWS_TP, 512)], parts, mine, other)
 
 
 def gate(rows, own_gate, own_up, other_gate, other_up):
@@ -447,16 +497,12 @@
 
 
 def down(packed, own, other):
-    return run(down_kernel, shaped(N_TP, ROWS_TP, FEAT), packed, own, other)
-
-
-def mix(parts, mid, expert_ids, expert_weights):
-    return run(mix_kernel, shaped(ROWS_TP, FEAT), parts, mid, expert_ids, expert_weights)
-
-
-def finish(own_attended, other_attended, own_mixed, other_mixed):
+    return run(down_kernel, shaped(2 * N_TP, 16, 128), packed, own, other)
+
+
+def mix(parts, mine, own, other, expert_ids, expert_weights):
     outs = [shaped(ROWS_TP, FEAT), shaped(ROWS_TP, FEAT)]
-    return run(finish_kernel, outs, own_attended, other_attended, own_mixed, other_mixed)
+    return run(mix_kernel, outs, parts, mine, own, other, expert_ids, expert_weights)
 
 
 def exchange(array, axis, groups=None):
@@ -465,6 +511,11 @@
 
 def along_y(array):
     return exchange(array, "kv", [[2 * chip + core for chip in range(CHIPS)] for core in range(2)])
+
+
+def to_owners(array):
+    groups = [[(2 * chip + core) * N_TP + place for core in range(2) for place in range(N_TP)] for chip in range(CHIPS)]
+    return exchange(array, ("kv", "tp"), groups)
 
 
 def other_core(array):
@@ -477,27 +528,27 @@
 ):
     ups, mine = start(tokens, attn_gain, down_kv, key_up, value_up, mlp_gain)
     own_cache, own_out, own_down = jnp.swapaxes(cache, 1, 2), out_proj.T, jnp.swapaxes(down_proj, 1, 2)
-    ups, *moved = lax.optimization_barrier((ups, own_cache, mine, own_out, gate_proj, up_proj, own_down))
+    ups, *moved = lax.optimization_barrier((ups, own_cache, own_out, gate_proj, up_proj, own_down))
     own = along_y(ups)
     moved = [other_core(array) for array in moved]
-    other_cache, other_mine, other_out, other_gate, other_up, other_down = moved
-    part = own_sum(own, moved)
-    keys = fresh(part, other_core(part), latent_gain, lengths)
+    other_cache, other_out, other_gate, other_up, other_down = moved
+    mine = own_sum(own, mine, moved)
+    other = other_core(mine)
+    keys = fresh(mine, other, latent_gain, lengths)
     keys, own = lax.optimization_barrier((keys, own))
     keys = exchange(keys, "tp")
-    parts, queries, ups = attend(lengths, own, other_core(own), query_nope, query_rope, own_cache, other_cache)
-    parts = merge(parts, queries, ups, keys)
+    parts, queries, values = attend(lengths, own, other_core(own), query_nope, query_rope, own_cache, other_cache)
+    parts, keys = lax.optimization_barrier((parts, keys))
     parts = along_y(parts.reshape(CHIPS, ROWS_KV, ATT_W))
-    values = along_y(combine(parts))
+    values = along_y(combine(parts, queries, values, keys))
     parts = exchange(project(values, own_out, other_out), "tp")
-    attended, mid, rows = route(parts, mine, other_mine)
+    attended, rows = route(parts, mine, other)
     other_attended = other_core(attended)
     rows = exchange(rows, "tp")
     parts = along_y(gate(rows, gate_proj, up_proj, other_gate, other_up))
     packed = along_y(hidden(parts))
-    parts = exchange(down(packed, own_down, other_down), "tp")
-    mixed = mix(parts, mid, expert_ids, expert_weights)
-    return finish(attended, other_attended, mixed, other_core(mixed))
+    parts = to_owners(down(packed, own_down, other_down))
+    return mix(parts, mine, attended, other_attended, expert_ids, expert_weights)
 
 
 def solution(mesh):

time: 184 us -> 180 us (0.978)
  waiting for transfers between devices: 9.97 us -> 25.4 us
  starting transfers between devices: 64.3 us -> 51.9 us
  local copies, waits for them, and re-layouts: 10.2 us -> 2.5 us
  Pallas kernels: 16.4 us -> 19.5 us
  blocking collectives: 80.9 us -> 78.9 us
    ppermute x10 -> x8, starting transfers between devices: 45.2 us -> 24.3 us  [other_core(): lax.ppermute(array, 'kv', [(index, index ^ 1) for index in range(N_KV)])]
    all_to_all x3, waiting for transfers between devices: 5.64 us -> 22.1 us  [exchange(): lax.all_to_all(array, axis, split_axis=0, concat_axis=0, axis_index_group...]
    all_to_all x3, starting transfers between devices: 19.1 us -> 27.6 us  [exchange(): lax.all_to_all(array, axis, split_axis=0, concat_axis=0, axis_index_group...]
    unnamed x40 -> x20, local copies, waits for them, and re-layouts: 10.2 us -> 2.5 us
    pallas_call x13 -> x11, Pallas kernels: 16.4 us -> 19.5 us  [run(): pl.pallas_call(body, out_shape=outs[0] if single else tuple(outs), in_spe...]
    all_to_all x6, blocking collectives: 80.9 us -> 78.9 us  [exchange(): lax.all_to_all(array, axis, split_axis=0, concat_axis=0, axis_index_group...]
    ppermute x10 -> x8, waiting for transfers between devices: 4.33 us -> 3.31 us  [other_core(): lax.ppermute(array, 'kv', [(index, index ^ 1) for index in range(N_KV)])]
  transfers between devices with their start and end apart: 13 -> 11, of which waited for: 5 -> 6; matrix products, arithmetic and copies ran while one was open for 0% -> 0% of each run, Pallas kernels for 3% -> 3%
where the time goes in v3:
time: 180 us; the launch traced here: 179 us
  blocking collectives  78.9 us (44%)
  starting transfers between devices  51.9 us (29%)
  waiting for transfers between devices  25.4 us (14%)
  Pallas kernels  19.5 us (11%)
  local copies, waits for them, and re-layouts  2.5 us (1%)
    all_to_all x6, blocking collectives, exchange(): lax.all_to_all(array, axis, split_axis=0, concat_axis=0, axis_index_group...  78.9 us
    all_to_all x3, starting transfers between devices, exchange(): lax.all_to_all(array, axis, split_axis=0, concat_axis=0, axis_index_group...  27.6 us
    ppermute x8, starting transfers between devices, other_core(): lax.ppermute(array, 'kv', [(index, index ^ 1) for index in range(N_KV)])  24.3 us
    all_to_all x3, waiting for transfers between devices, exchange(): lax.all_to_all(array, axis, split_axis=0, concat_axis=0, axis_index_group...  22.1 us
    pallas_call x11, Pallas kernels, run(): pl.pallas_call(body, out_shape=outs[0] if single else tuple(outs), in_spe...  19.5 us
  transfers between devices with their start and end apart: 11, of which 6 were waited for; matrix products, arithmetic and copies ran while one was open for 0% of the time, Pallas kernels for 3%

profile of v3, /device:TPU:1, one launch (start us, length us, event | category | flops | bytes accessed | tf_op | source)
XLA Modules:
  0.0 179.1 jit_solution(15328382836856588374)
XLA Ops:
  0.6 2.2 %shard_map.176 = (bf16[8,304,128]{2,1,0:T(8,128)(2,1)}, f32[64,128]{1,0:T(8,128)}) custom-call(bf16[8,448]{1,0:T(8,128)(2,1)} %refs_0_.1, f32[1,448]{1,0:T(1,128)} %bitcast.18, bf16[448,576]{1,0:T(8,128)(2,1)} %refs_2_.2, bf16[4,32,128]{2,1,0:T(8,128)(2,1)} %bitcast.17, bf16[4,32,128]{2,1,0:T(8,128)(2,1)} %refs_4_.3, f32[1,448]{1,0:T(1,128)} %bitcast.19), custom_call_target="tpu_custom_call" | custom-call | tf_op jit(solution)/shard_map/pallas_call | solution.py:403
  2.8 8.8 %collective-permute-start = (bf16[2,576,768]{2,1,0:T(8,128)(2,1)}, bf16[2,576,768]{2,1,0:T(8,128)(2,1)}, u32[]{:S(2)}, u32[]{:S(2)}) collective-permute-start(bf16[2,576,768]{2,1,0:T(8,128)(2,1)} %bitcast.20), channel_id=1, source_target_pairs={{0,32},{32,0},{64,96},{96,64},{128,160},{160,128},{192,224},{224,1... | collective-permute-start | bytes 5308424 | tf_op jit(solution)/shard_map/ppermute | solution.py:522
  11.6 3.6 %all-to-all-start = ((bf16[8,304,128]{2,1,0:T(8,128)(2,1)}), bf16[8,304,128]{2,1,0:T(8,128)(2,1)S(1)}, u32[]{:S(2)}, u32[]{:S(2)}) async-start(bf16[8,304,128]{2,1,0:T(8,128)(2,1)} %get-tuple-element.20), calls=%async_computation | async-start | bytes 1245184 | tf_op jit(solution)/shard_map/all_to_all | solution.py:509
  15.1 1.9 %collective-permute-start.2 = (bf16[1,448,1024]{2,1,0:T(8,128)(2,1)}, bf16[1,448,1024]{2,1,0:T(8,128)(2,1)S(1)}, u32[]{:S(2)}, u32[]{:S(2)}) collective-permute-start(bf16[1,448,1024]{2,1,0:T(8,128)(2,1)} %refs_1_.1), channel_id=1, source_target_pairs={{0,32},{32,0},{64,96},{96,64},{128,160},{160,128},{192,224},{224,1... | collective-permute-start | bytes 2752520 | tf_op jit(solution)/shard_map/ppermute | solution.py:522
  17.1 2.4 %collective-permute-start.3 = (bf16[1,448,1024]{2,1,0:T(8,128)(2,1)}, bf16[1,448,1024]{2,1,0:T(8,128)(2,1)S(1)}, u32[]{:S(2)}, u32[]{:S(2)}) collective-permute-start(bf16[1,448,1024]{2,1,0:T(8,128)(2,1)} %refs_2_.3), channel_id=1, source_target_pairs={{0,32},{32,0},{64,96},{96,64},{128,160},{160,128},{192,224},{224,1... | collective-permute-start | bytes 2752520 | tf_op jit(solution)/shard_map/ppermute | solution.py:522
  19.5 1.9 %collective-permute-start.4 = (bf16[1,448,1024]{2,1,0:T(8,128)(2,1)}, bf16[1,448,1024]{2,1,0:T(8,128)(2,1)S(1)}, u32[]{:S(2)}, u32[]{:S(2)}) collective-permute-start(bf16[1,448,1024]{2,1,0:T(8,128)(2,1)} %bitcast.9), channel_id=1, source_target_pairs={{0,32},{32,0},{64,96},{96,64},{128,160},{160,128},{192,224},{224,1... | collective-permute-start | bytes 2752520 | tf_op jit(solution)/shard_map/ppermute | solution.py:522
  21.4 2.4 %collective-permute-start.1 = (bf16[448,512]{1,0:T(8,128)(2,1)}, bf16[448,512]{1,0:T(8,128)(2,1)S(1)}, u32[]{:S(2)}, u32[]{:S(2)}) collective-permute-start(bf16[448,512]{1,0:T(8,128)(2,1)} %bitcast.11), channel_id=1, source_target_pairs={{0,32},{32,0},{64,96},{96,64},{128,160},{160,128},{192,224},{224,1... | collective-permute-start | bytes 1376264 | tf_op jit(solution)/shard_map/ppermute | solution.py:522
  23.8 1.6 collective-permute-done.1.refs_3_.refs_2_
  25.5 0.0 copy-start
  25.5 0.8 copy-done
  26.3 0.0 collective-permute-done.2.refs_4_.refs_3_
  26.3 0.0 collective-permute-done.3.refs_5_.refs_4_
  26.3 0.0 collective-permute-done.4.refs_6_.refs_2_
  26.3 9.0 %all-to-all-done.refs_0_.refs_1_ = bf16[8,304,128]{2,1,0:T(8,128)(2,1)S(1)} async-done(((bf16[8,304,128]{2,1,0:T(8,128)(2,1)}), bf16[8,304,128]{2,1,0:T(8,128)(2,1)S(1)}, u32[]{:S(2)}, u32[]{:S(2)}) %all-to-all-start) | async-done | bytes 622624 | tf_op jit(solution)/shard_map/all_to_all | solution.py:509
  35.2 0.0 collective-permute-done.refs_2_.refs_6_
  35.2 0.0 copy-start.1
  35.2 1.0 copy-done.1
  36.2 0.0 copy-start.8
  36.2 0.0 copy-start.9
  36.2 0.8 shard_map.177.refs_0_.refs_1_
  37.1 2.3 %collective-permute-start.5 = (f32[112,128]{1,0:T(8,128)S(1)}, f32[112,128]{1,0:T(8,128)S(1)}, u32[]{:S(2)}, u32[]{:S(2)}) collective-permute-start(f32[112,128]{1,0:T(8,128)S(1)} %shard_map.177.refs_0_.refs_1_), channel_id=1, source_target_pairs={{0,32},{32,0},{64,96},{96,64},{128,160},{160,128},{192,224},{224,1... | collective-permute-start | bytes 172040 | tf_op jit(solution)/shard_map/ppermute | solution.py:522
  39.4 0.9 collective-permute-done.5.refs_1_.refs_2_
  40.3 0.0 copy-done.8
  40.3 0.0 copy-done.9
  40.3 1.0 shard_map.178
  41.3 2.3 %collective-permute-start.6 = (bf16[8,304,128]{2,1,0:T(8,128)(2,1)S(1)}, bf16[8,304,128]{2,1,0:T(8,128)(2,1)}, u32[]{:S(2)}, u32[]{:S(2)}) collective-permute-start(bf16[8,304,128]{2,1,0:T(8,128)(2,1)S(1)} %all-to-all-done.refs_0_.refs_1_), channel_id=1, source_target_pairs={{0,32},{32,0},{64,96},{96,64},{128,160},{160,128},{192,224},{224,1... | collective-permute-start | bytes 1867784 | tf_op jit(solution)/shard_map/ppermute | solution.py:522
  43.6 11.0 %all-to-all-start.1 = ((bf16[32,8,384]{2,1,0:T(8,128)(2,1)}), bf16[32,8,384]{2,1,0:T(8,128)(2,1)}, u32[]{:S(2)}, u32[]{:S(2)}) async-start(bf16[32,8,384]{2,1,0:T(8,128)(2,1)} %shard_map.178), calls=%async_computation.1 | async-start | bytes 393216 | tf_op jit(solution)/shard_map/all_to_all | solution.py:509
  54.6 0.0 collective-permute-done.6.refs_2_
  54.6 5.9 %shard_map.179 = (bf16[128,640]{1,0:T(8,128)(2,1)S(1)}, bf16[64,576]{1,0:T(8,128)(2,1)}, bf16[4,8,2,32,128]{4,3,2,1,0:T(8,128)(2,1)}) custom-call(s32[1,2]{1,0:T(1,128)S(1)} %bitcast.16, bf16[8,304,128]{2,1,0:T(8,128)(2,1)S(1)} %all-to-all-done.refs_0_.refs_1_, bf16[8,304,128]{2,1,0:T(8,128)(2,1)} %collective-permute-done.6.refs_2_, ...), custom_call_target="tpu_custom_call" | custom-call | flops 2200000000 | bytes 4000000 | tf_op jit(solution)/shard_map/pallas_call | solution.py:403
  60.5 0.0 copy-start.5
  60.5 0.7 copy-done.5
  61.2 0.0 copy-start.2
  61.2 2.8 %all-to-all-done.1.refs_1_ = bf16[32,8,384]{2,1,0:T(8,128)(2,1)} async-done(((bf16[32,8,384]{2,1,0:T(8,128)(2,1)}), bf16[32,8,384]{2,1,0:T(8,128)(2,1)}, u32[]{:S(2)}, u32[]{:S(2)}) %all-to-all-start.1) | async-done | bytes 196640 | tf_op jit(solution)/shard_map/all_to_all | solution.py:509
  64.0 0.0 copy-start.4
  64.0 11.7 %all_to_all.45.refs_0_ = bf16[8,16,640]{2,1,0:T(8,128)(2,1)S(1)} all-to-all(bf16[8,16,640]{2,1,0:T(8,128)(2,1)} %bitcast.13), channel_id=1, replica_groups={{0,64,128,192,256,320,384,448},{32,96,160,224,288,352,416,480},{1,65,12..., dimensions={0} | all-to-all | bytes 327680 | tf_op jit(solution)/shard_map/all_to_all | solution.py:509
  75.7 2.7 %shard_map.180 = bf16[8,16,512]{2,1,0:T(8,128)(2,1)S(1)} custom-call(bf16[8,16,640]{2,1,0:T(8,128)(2,1)S(1)} %all_to_all.45.refs_0_, bf16[32,8,384]{2,1,0:T(8,128)(2,1)} %all-to-all-done.1.refs_1_, bf16[64,576]{1,0:T(8,128)(2,1)} %get-tuple-element.32.refs_2_, bf16[4,8,2,32,128]{4,3,2,1,0:T(8,128)(2,1)} %get-tuple-element.33.refs_3_), custom_call_target="tpu_custom_call" | custom-call | tf_op jit(solution)/shard_map/pallas_call | solution.py:403
  78.5 10.3 %all_to_all.46.refs_0_ = bf16[8,16,512]{2,1,0:T(8,128)(2,1)S(1)} all-to-all(bf16[8,16,512]{2,1,0:T(8,128)(2,1)S(1)} %shard_map.180), channel_id=1, replica_groups={{0,64,128,192,256,320,384,448},{32,96,160,224,288,352,416,480},{1,65,12..., dimensions={0} | all-to-all | bytes 262144 | tf_op jit(solution)/shard_map/all_to_all | solution.py:509
  88.8 0.0 copy-done.2
  88.8 0.0 copy-done.4
  88.8 0.7 shard_map.181
  89.5 16.2 %all_to_all.47.refs_0_ = bf16[32,8,448]{2,1,0:T(8,128)(2,1)S(1)} all-to-all(bf16[32,8,448]{2,1,0:T(8,128)(2,1)S(1)} %shard_map.181), channel_id=1, replica_groups=mesh['kv'=16,'tp'=32] {'tp'}, dimensions={0} | all-to-all | bytes 458752 | tf_op jit(solution)/shard_map/all_to_all | solution.py:509
  105.7 0.2 shard_map.182
  105.9 14.0 %all_to_all.48.refs_0_ = bf16[32,8,512]{2,1,0:T(8,128)(2,1)S(1)} all-to-all(bf16[32,8,512]{2,1,0:T(8,128)(2,1)S(1)} %get-tuple-element.34), channel_id=1, replica_groups=mesh['kv'=16,'tp'=32] {'tp'}, dimensions={0} | all-to-all | bytes 524288 | tf_op jit(solution)/shard_map/all_to_all | solution.py:509
  119.9 3.0 %shard_map.183 = bf16[8,272,128]{2,1,0:T(8,128)(2,1)S(1)} custom-call(bf16[32,8,512]{2,1,0:T(8,128)(2,1)S(1)} %all_to_all.48.refs_0_, bf16[1,448,1024]{2,1,0:T(8,128)(2,1)} %refs_1_.1, bf16[1,448,1024]{2,1,0:T(8,128)(2,1)} %refs_2_.3, bf16[1,448,1024]{2,1,0:T(8,128)(2,1)S(1)} %collective-permute-done.2.refs_4_.refs_3_, ...), custom_call_target="tpu_custom_call" | custom-call | tf_op jit(solution)/shard_map/pallas_call | solution.py:403
  122.9 0.0 copy-start.3
  122.9 15.0 %all_to_all.49.refs_0_ = bf16[8,272,128]{2,1,0:T(8,128)(2,1)S(1)} all-to-all(bf16[8,272,128]{2,1,0:T(8,128)(2,1)S(1)} %shard_map.183), channel_id=1, replica_groups={{0,64,128,192,256,320,384,448},{32,96,160,224,288,352,416,480},{1,65,12..., dimensions={0} | all-to-all | bytes 1114112 | tf_op jit(solution)/shard_map/all_to_all | solution.py:509
  137.9 0.1 shard_map.184
  138.1 0.0 copy-start.6
  138.1 0.0 copy-start.7
  138.1 11.7 %all_to_all.50.refs_0_ = bf16[8,128,128]{2,1,0:T(8,128)(2,1)S(1)} all-to-all(bf16[8,128,128]{2,1,0:T(8,128)(2,1)S(1)} %shard_map.184), channel_id=1, replica_groups={{0,64,128,192,256,320,384,448},{32,96,160,224,288,352,416,480},{1,65,12..., dimensions={0} | all-to-all | bytes 524288 | tf_op jit(solution)/shard_map/all_to_all | solution.py:509
  149.8 0.0 copy-done.3
  149.8 2.1 %shard_map.185 = bf16[64,16,128]{2,1,0:T(8,128)(2,1)} custom-call(bf16[8,128,128]{2,1,0:T(8,128)(2,1)S(1)} %all_to_all.50.refs_0_, bf16[1,448,1024]{2,1,0:T(8,128)(2,1)S(1)} %bitcast.10, bf16[1,448,1024]{2,1,0:T(8,128)(2,1)S(1)} %collective-permute-done.4.refs_6_.refs_2_), custom_call_target="tpu_custom_call" | custom-call | tf_op jit(solution)/shard_map/pallas_call | solution.py:403
  151.8 13.1 %all-to-all-start.8 = ((bf16[64,16,128]{2,1,0:T(8,128)(2,1)}), bf16[64,16,128]{2,1,0:T(8,128)(2,1)S(1)}, u32[]{:S(2)}, u32[]{:S(2)}) async-start(bf16[64,16,128]{2,1,0:T(8,128)(2,1)} %shard_map.185), calls=%async_computation.8 | async-start | bytes 524288 | tf_op jit(solution)/shard_map/all_to_all | solution.py:509
  164.9 2.3 %collective-permute-start.7 = (bf16[8,448]{1,0:T(8,128)(2,1)S(1)}, bf16[8,448]{1,0:T(8,128)(2,1)S(1)}, u32[]{:S(2)}, u32[]{:S(2)}) collective-permute-start(bf16[8,448]{1,0:T(8,128)(2,1)S(1)} %get-tuple-element.35.refs_2_), channel_id=1, source_target_pairs={{0,32},{32,0},{64,96},{96,64},{128,160},{160,128},{192,224},{224,1... | collective-permute-start | bytes 21512 | tf_op jit(solution)/shard_map/ppermute | solution.py:522
  167.2 0.8 collective-permute-done.7.refs_3_
  168.0 10.3 %all-to-all-done.8.refs_0_ = bf16[64,16,128]{2,1,0:T(8,128)(2,1)S(1)} async-done(((bf16[64,16,128]{2,1,0:T(8,128)(2,1)}), bf16[64,16,128]{2,1,0:T(8,128)(2,1)S(1)}, u32[]{:S(2)}, u32[]{:S(2)}) %all-to-all-start.8) | async-done | bytes 262176 | tf_op jit(solution)/shard_map/all_to_all | solution.py:509
  178.3 0.0 copy-done.6
  178.3 0.0 copy-done.7
  178.3 0.8 shard_map.186
  (1 shorter events, 0.0 us)
Async XLA Ops:
  2.8 32.4 %collective-permute-start = (bf16[2,576,768]{2,1,0:T(8,128)(2,1)}, bf16[2,576,768]{2,1,0:T(8,128)(2,1)}, u32[]{:S(2)}, u32[]{:S(2)}) collective-permute-start(bf16[2,576,768]{2,1,0:T(8,128)(2,1)} %bitcast.20), channel_id=1, source_target_pairs={{0,32},{32,0},{64,96},{96,64},{128,160},{160,128},{192,224},{224,1... | collective-permute-start | bytes 5308424 | tf_op jit(solution)/shard_map/ppermute | solution.py:522
  11.6 23.6 %all-to-all-start = ((bf16[8,304,128]{2,1,0:T(8,128)(2,1)}), bf16[8,304,128]{2,1,0:T(8,128)(2,1)S(1)}, u32[]{:S(2)}, u32[]{:S(2)}) async-start(bf16[8,304,128]{2,1,0:T(8,128)(2,1)} %get-tuple-element.20), calls=%async_computation | async-start | bytes 1245184 | tf_op jit(solution)/shard_map/all_to_all | solution.py:509
  15.1 11.1 %collective-permute-start.2 = (bf16[1,448,1024]{2,1,0:T(8,128)(2,1)}, bf16[1,448,1024]{2,1,0:T(8,128)(2,1)S(1)}, u32[]{:S(2)}, u32[]{:S(2)}) collective-permute-start(bf16[1,448,1024]{2,1,0:T(8,128)(2,1)} %refs_1_.1), channel_id=1, source_target_pairs={{0,32},{32,0},{64,96},{96,64},{128,160},{160,128},{192,224},{224,1... | collective-permute-start | bytes 2752520 | tf_op jit(solution)/shard_map/ppermute | solution.py:522
  17.1 9.2 %collective-permute-start.3 = (bf16[1,448,1024]{2,1,0:T(8,128)(2,1)}, bf16[1,448,1024]{2,1,0:T(8,128)(2,1)S(1)}, u32[]{:S(2)}, u32[]{:S(2)}) collective-permute-start(bf16[1,448,1024]{2,1,0:T(8,128)(2,1)} %refs_2_.3), channel_id=1, source_target_pairs={{0,32},{32,0},{64,96},{96,64},{128,160},{160,128},{192,224},{224,1... | collective-permute-start | bytes 2752520 | tf_op jit(solution)/shard_map/ppermute | solution.py:522
  19.5 6.8 %collective-permute-start.4 = (bf16[1,448,1024]{2,1,0:T(8,128)(2,1)}, bf16[1,448,1024]{2,1,0:T(8,128)(2,1)S(1)}, u32[]{:S(2)}, u32[]{:S(2)}) collective-permute-start(bf16[1,448,1024]{2,1,0:T(8,128)(2,1)} %bitcast.9), channel_id=1, source_target_pairs={{0,32},{32,0},{64,96},{96,64},{128,160},{160,128},{192,224},{224,1... | collective-permute-start | bytes 2752520 | tf_op jit(solution)/shard_map/ppermute | solution.py:522
  21.4 4.0 %collective-permute-start.1 = (bf16[448,512]{1,0:T(8,128)(2,1)}, bf16[448,512]{1,0:T(8,128)(2,1)S(1)}, u32[]{:S(2)}, u32[]{:S(2)}) collective-permute-start(bf16[448,512]{1,0:T(8,128)(2,1)} %bitcast.11), channel_id=1, source_target_pairs={{0,32},{32,0},{64,96},{96,64},{128,160},{160,128},{192,224},{224,1... | collective-permute-start | bytes 1376264 | tf_op jit(solution)/shard_map/ppermute | solution.py:522
  25.5 0.8 copy-start
  35.2 1.0 copy-start.1
  36.2 4.1 %copy-start.8 = (f32[512]{0:T(512)S(1)}, f32[512]{0:T(512)}, u32[]{:S(2)}) copy-start(f32[512]{0:T(512)} %param.20) | copy-start | bytes 6148
  36.2 4.1 %copy-start.9 = (s32[2]{0:T(128)S(1)}, s32[2]{0:T(128)}, u32[]{:S(2)}) copy-start(s32[2]{0:T(128)} %param.24) | copy-start | bytes 28
  37.1 3.2 %collective-permute-start.5 = (f32[112,128]{1,0:T(8,128)S(1)}, f32[112,128]{1,0:T(8,128)S(1)}, u32[]{:S(2)}, u32[]{:S(2)}) collective-permute-start(f32[112,128]{1,0:T(8,128)S(1)} %shard_map.177.refs_0_.refs_1_), channel_id=1, source_target_pairs={{0,32},{32,0},{64,96},{96,64},{128,160},{160,128},{192,224},{224,1... | collective-permute-start | bytes 172040 | tf_op jit(solution)/shard_map/ppermute | solution.py:522
  41.3 13.3 %collective-permute-start.6 = (bf16[8,304,128]{2,1,0:T(8,128)(2,1)S(1)}, bf16[8,304,128]{2,1,0:T(8,128)(2,1)}, u32[]{:S(2)}, u32[]{:S(2)}) collective-permute-start(bf16[8,304,128]{2,1,0:T(8,128)(2,1)S(1)} %all-to-all-done.refs_0_.refs_1_), channel_id=1, source_target_pairs={{0,32},{32,0},{64,96},{96,64},{128,160},{160,128},{192,224},{224,1... | collective-permute-start | bytes 1867784 | tf_op jit(solution)/shard_map/ppermute | solution.py:522
  43.6 20.4 %all-to-all-start.1 = ((bf16[32,8,384]{2,1,0:T(8,128)(2,1)}), bf16[32,8,384]{2,1,0:T(8,128)(2,1)}, u32[]{:S(2)}, u32[]{:S(2)}) async-start(bf16[32,8,384]{2,1,0:T(8,128)(2,1)} %shard_map.178), calls=%async_computation.1 | async-start | bytes 393216 | tf_op jit(solution)/shard_map/all_to_all | solution.py:509
  60.5 0.7 copy-start.5
  61.2 27.6 %copy-start.2 = (bf16[448,512]{1,0:T(8,128)(2,1)S(1)}, bf16[448,512]{1,0:T(8,128)(2,1)}, u32[]{:S(2)}) copy-start(bf16[448,512]{1,0:T(8,128)(2,1)} %copy-done) | copy-start | bytes 1376260
  64.0 24.8 %copy-start.4 = (bf16[512,448]{0,1:T(8,128)(2,1)S(1)}, bf16[512,448]{0,1:T(8,128)(2,1)}, u32[]{:S(2)}) copy-start(bf16[512,448]{0,1:T(8,128)(2,1)} %param.27) | copy-start | bytes 1376260
  122.9 26.9 %copy-start.3 = (bf16[1,1024,448]{1,2,0:T(8,128)(2,1)S(1)}, bf16[1,1024,448]{1,2,0:T(8,128)(2,1)}, u32[]{:S(2)}) copy-start(bf16[1,1024,448]{1,2,0:T(8,128)(2,1)} %param.33) | copy-start | bytes 2752516
  138.1 40.2 %copy-start.6 = (s32[8,8]{1,0:T(8,128)S(1)}, s32[8,8]{1,0:T(8,128)}, u32[]{:S(2)}) copy-start(s32[8,8]{1,0:T(8,128)} %refs_4_.5) | copy-start | bytes 772
  138.1 40.2 %copy-start.7 = (f32[8,8]{1,0:T(8,128)S(1)}, f32[8,8]{1,0:T(8,128)}, u32[]{:S(2)}) copy-start(f32[8,8]{1,0:T(8,128)} %refs_5_.1) | copy-start | bytes 772
  151.8 26.5 %all-to-all-start.8 = ((bf16[64,16,128]{2,1,0:T(8,128)(2,1)}), bf16[64,16,128]{2,1,0:T(8,128)(2,1)S(1)}, u32[]{:S(2)}, u32[]{:S(2)}) async-start(bf16[64,16,128]{2,1,0:T(8,128)(2,1)} %shard_map.185), calls=%async_computation.8 | async-start | bytes 524288 | tf_op jit(solution)/shard_map/all_to_all | solution.py:509
  164.9 3.1 %collective-permute-start.7 = (bf16[8,448]{1,0:T(8,128)(2,1)S(1)}, bf16[8,448]{1,0:T(8,128)(2,1)S(1)}, u32[]{:S(2)}, u32[]{:S(2)}) collective-permute-start(bf16[8,448]{1,0:T(8,128)(2,1)S(1)} %get-tuple-element.35.refs_2_), channel_id=1, source_target_pairs={{0,32},{32,0},{64,96},{96,64},{128,160},{160,128},{192,224},{224,1... | collective-permute-start | bytes 21512 | tf_op jit(solution)/shard_map/ppermute | solution.py:522

commit v4 on v3

--- a/solution.py
+++ b/solution.py
@@ -34,9 +34,8 @@
 UP_ROWS = 2 * HEADS_DEV * LAT_KV
 FRESH_W = KEY + ROPE
 FRESH_ROWS = 48
-TOKEN_AT = FRESH_ROWS
+TOKEN_AT = 0
 GAIN_AT = TOKEN_AT + 4 * ROWS_TP
-PACK_ROWS = GAIN_AT + 4 * ROWS_TP
 CLASS = TOKROWS // 2
 PART_ROWS = 2 * CLASS + 16
 KEY_W = 384
@@ -120,21 +119,17 @@
         out_ref[place, UP_ROWS:, :] = packed
 
 
-def sum_kernel(ups_hbm, mine_hbm, out_ref, fresh_ref, mine_ref, sems):
+def fresh_kernel(gain_ref, lengths_ref, freq_ref, own_hbm, other_hbm, out_hbm, own_ref, other_ref, out_ref, sems):
+    rows = pl.ds(UP_ROWS, FRESH_ROWS)
     fetches = [
-        pltpu.make_async_copy(ups_hbm.at[:, pl.ds(UP_ROWS, FRESH_ROWS), :], fresh_ref, sems.at[0]),
-        pltpu.make_async_copy(mine_hbm, mine_ref, sems.at[1]),
+        pltpu.make_async_copy(own_hbm.at[:, rows, :], own_ref, sems.at[0]),
+        pltpu.make_async_copy(other_hbm.at[:, rows, :], other_ref, sems.at[1]),
     ]
     for fetch in fetches:
         fetch.start()
     for fetch in fetches:
         fetch.wait()
-    out_ref[FRESH_ROWS:, :] = mine_ref[...]
-    out_ref[:FRESH_ROWS, :] = jnp.sum(fresh_ref[...].astype(F32), axis=0)
-
-
-def fresh_kernel(own_ref, other_ref, gain_ref, lengths_ref, freq_ref, out_hbm, out_ref, sem):
-    packed = own_ref[:FRESH_ROWS, :] + other_ref[:FRESH_ROWS, :]
+    packed = jnp.sum(own_ref[...].astype(F32), axis=0) + jnp.sum(other_ref[...].astype(F32), axis=0)
     tiles = [packed[at * ROWS_TP : (at + 1) * ROWS_TP] for at in range(FRESH_W // 128)]
     fresh = jnp.concatenate(tiles[:-1], axis=1)
     turn = tiles[-1][:, :ROPE]
@@ -153,7 +148,7 @@
     key = jnp.where(iota(upper.shape, 0) < ROWS_TP // 2, upper, lower).astype(BF16)
     for place in range(N_TP):
         out_ref[place] = key
-    leave = pltpu.make_async_copy(out_ref, out_hbm, sem)
+    leave = pltpu.make_async_copy(out_ref, out_hbm, sems.at[2])
     leave.start()
     leave.wait()
 
@@ -309,7 +304,16 @@
         out_ref[place] = row_data
 
 
-def gate_kernel(rows_ref, own_gate_ref, own_up_ref, other_gate_ref, other_up_ref, out_ref):
+def gate_kernel(
+    rows_ref, other_gate_ref, other_up_ref, own_gate_hbm, own_up_hbm, out_ref, own_gate_ref, own_up_ref, sems,
+):
+    fetches = []
+    for place in range(CHIPS):
+        columns = pl.ds(place * HID_Y, HID_Y)
+        for source, target in ((own_gate_hbm, own_gate_ref), (own_up_hbm, own_up_ref)):
+            at = (0, slice(None), columns)
+            fetches.append(pltpu.make_async_copy(source.at[at], target.at[at], sems.at[len(fetches)]))
+            fetches[-1].start()
     rows = rows_ref[...].astype(F32).reshape(TOKROWS, 512).astype(BF16)
     shape = (CLASS, TOKROWS)
     place, row = iota(shape, 0), iota(shape, 1)
@@ -323,6 +327,8 @@
     own, other = own[:, :FEAT], other[:, :FEAT]
     for place in range(CHIPS):
         columns = slice(place * HID_Y, (place + 1) * HID_Y)
+        fetches[2 * place].wait()
+        fetches[2 * place + 1].wait()
         gate = dot(own, own_gate_ref[0, :, columns]) + dot(other, other_gate_ref[0, :, columns])
         up = dot(own, own_up_ref[0, :, columns]) + dot(other, other_up_ref[0, :, columns])
         out_ref[place, :CLASS, :] = gate.astype(BF16)
@@ -344,49 +350,33 @@
         out_ref[place] = hidden
 
 
-def down_kernel(hidden_ref, own_ref, other_ref, out_ref):
+def down_kernel(hidden_ref, weights_ref, out_ref):
     hidden = jnp.concatenate([hidden_ref[chip] for chip in range(CHIPS)], axis=1)
-    shape = (4 * CLASS, 4 * CLASS)
+    out_ref[...] = dot(hidden, weights_ref[0], NT).astype(BF16)
+
+
+def join_kernel(own_ref, came_ref, out_ref):
+    shape = (TOKROWS, CLASS)
     row, source = iota(shape, 0), iota(shape, 1)
-    order = (source == row % 16 // 4 * CLASS + row // 16 * 4 + row % 4).astype(F32).astype(BF16)
-    core = kv_index() % 2
-    for weights_ref, whose in ((own_ref, core), (other_ref, 1 - core)):
-        rows = dot(hidden, weights_ref[0], NT)
-        rows = jnp.concatenate([rows, jnp.zeros((CLASS, 512 - FEAT), F32)], axis=1).astype(BF16)
-        tiles = jnp.concatenate([rows[:, at * 128 : (at + 1) * 128] for at in range(4)], axis=0)
-        place = pl.ds(pl.multiple_of(whose * N_TP, N_TP), N_TP)
-        out_ref[place] = dot(order, tiles).reshape(N_TP, 16, 128).astype(BF16)
+    match = source == row // ROWS_TP * (ROWS_TP // 2) + row % (ROWS_TP // 2)
+    own = (match & own_half(shape, 0)).astype(F32).astype(BF16)
+    other = (match & ~own_half(shape, 0)).astype(F32).astype(BF16)
+    out = dot(own, own_ref[...]) + dot(other, came_ref[...])
+    out_ref[...] = out.reshape(N_TP, ROWS_TP, FEAT).astype(BF16)
 
 
 def mix_kernel(parts_ref, mine_ref, own_ref, other_ref, ids_ref, weights_ref, attended_ref, out_ref):
     own = own_ref[...].astype(F32)
     attended = jnp.where(own_half(own.shape, 0), own, swap_halves(other_ref[...].astype(F32)))
     attended_ref[...] = attended.astype(BF16)
+    total = from_tiles(mine_ref[TOKEN_AT:, :]) + attended
     ids = ids_ref[...]
     weights = weights_ref[...]
-    lane = iota((ROWS_TP, 128), 1)
-    upper = iota((ROWS_TP, 128), 0) < ROWS_TP // 2
-    shares = jnp.zeros(lane.shape, F32)
-    for choice in range(ids.shape[1]):
-        one = slice(choice, choice + 1)
-        shares = jnp.where(ids[:, one] == lane, weights[:, one], shares)
-    sums = []
-    for core in range(2):
-        mine = jnp.where(upper == (core == 0), shares, swap_halves(shares))
-        mine = jnp.concatenate([mine, mine], axis=0)
-        total = jnp.zeros((16, 128), F32)
-        for expert in range(EXPERTS):
-            at = core * N_TP + 2 * expert
-            both = parts_ref[at].astype(F32) + parts_ref[at + 1].astype(F32)
-            total = total + mine[:, expert : expert + 1] * both
-        sums.append(total)
-    tiles = []
-    for at in range(2):
-        first, second = (total[at * ROWS_TP : (at + 1) * ROWS_TP] for total in sums)
-        tiles.append(jnp.where(upper, first, swap_halves(second)))
-        tiles.append(jnp.where(upper, swap_halves(first), second))
-    experts = jnp.concatenate(tiles, axis=1)[:, :FEAT]
-    out_ref[...] = (from_tiles(mine_ref[TOKEN_AT:, :]) + attended + experts).astype(BF16)
+    for expert in range(EXPERTS):
+        share = jnp.sum(jnp.where(ids == expert, weights, 0.0), axis=1, keepdims=True)
+        both = parts_ref[2 * expert].astype(F32) + parts_ref[2 * expert + 1].astype(F32)
+        total = total + share * both
+    out_ref[...] = total.astype(BF16)
 
 
 def run(kernel, outs, *operands, fetched=(), left=0, scratch=(), cost=None, limit=24, after=()):
@@ -427,21 +417,13 @@
     )
 
 
-def own_sum(ups, mine, after):
-    return run(
-        sum_kernel, shaped(PACK_ROWS, 128, dtype=F32), fetched=(ups, in_hbm(mine)), after=after,
-        scratch=[
-            pltpu.VMEM((CHIPS, FRESH_ROWS, 128), BF16), pltpu.VMEM(mine.shape, F32), pltpu.SemaphoreType.DMA((2,)),
-        ],
-    )
-
-
 def fresh(own, other, latent_gain, lengths):
     freq = 10000.0 ** (-2.0 * jnp.arange(ROPE // 2, dtype=F32) / ROPE)
+    part = pltpu.VMEM((CHIPS, FRESH_ROWS, 128), BF16)
     return run(
         fresh_kernel, shaped(N_TP, ROWS_TP, KEY_W),
-        own, other, latent_gain.reshape(1, LAT), lengths.reshape(1, SEQS), freq[None],
-        left=1, scratch=[pltpu.VMEM((N_TP, ROWS_TP, KEY_W), BF16), pltpu.SemaphoreType.DMA],
+        latent_gain.reshape(1, LAT), lengths.reshape(1, SEQS), freq[None], fetched=(own, other),
+        left=1, scratch=[part, part, pltpu.VMEM((N_TP, ROWS_TP, KEY_W), BF16), pltpu.SemaphoreType.DMA((3,))],
     )
 
 
@@ -489,15 +471,23 @@
 
 
 def gate(rows, own_gate, own_up, other_gate, other_up):
-    return run(gate_kernel, shaped(CHIPS, PART_ROWS, 128), rows, own_gate, own_up, other_gate, other_up)
+    weights = pltpu.VMEM(own_gate.shape, BF16)
+    return run(
+        gate_kernel, shaped(CHIPS, PART_ROWS, 128), rows, other_gate, other_up,
+        fetched=(in_hbm(own_gate), in_hbm(own_up)), scratch=[weights, weights, pltpu.SemaphoreType.DMA((2 * CHIPS,))],
+    )
 
 
 def hidden(parts):
     return run(hidden_kernel, shaped(CHIPS, CLASS, HID_Y), parts)
 
 
-def down(packed, own, other):
-    return run(down_kernel, shaped(2 * N_TP, 16, 128), packed, own, other)
+def down(packed, weights):
+    return run(down_kernel, shaped(CLASS, FEAT), packed, weights)
+
+
+def join(own, came):
+    return run(join_kernel, shaped(N_TP, ROWS_TP, FEAT), own, came)
 
 
 def mix(parts, mine, own, other, expert_ids, expert_weights):
@@ -511,11 +501,6 @@
 
 def along_y(array):
     return exchange(array, "kv", [[2 * chip + core for chip in range(CHIPS)] for core in range(2)])
-
-
-def to_owners(array):
-    groups = [[(2 * chip + core) * N_TP + place for core in range(2) for place in range(N_TP)] for chip in range(CHIPS)]
-    return exchange(array, ("kv", "tp"), groups)
 
 
 def other_core(array):
@@ -528,26 +513,30 @@
 ):
     ups, mine = start(tokens, attn_gain, down_kv, key_up, value_up, mlp_gain)
     own_cache, own_out, own_down = jnp.swapaxes(cache, 1, 2), out_proj.T, jnp.swapaxes(down_proj, 1, 2)
-    ups, *moved = lax.optimization_barrier((ups, own_cache, own_out, gate_proj, up_proj, own_down))
+    ups, waiting, *moved = lax.optimization_barrier((ups, own_cache, own_out, mine, gate_proj, up_proj, own_down))
     own = along_y(ups)
     moved = [other_core(array) for array in moved]
-    other_cache, other_out, other_gate, other_up, other_down = moved
-    mine = own_sum(own, mine, moved)
-    other = other_core(mine)
-    keys = fresh(mine, other, latent_gain, lengths)
-    keys, own = lax.optimization_barrier((keys, own))
+    other_out, other_mine, other_gate, other_up, other_down = moved
+    other_cache = other_core(waiting)
+    own, *moved = lax.optimization_barrier((own, other_out, other_mine, other_gate, other_up, other_down))
+    other_out, other_mine, other_gate, other_up, other_down = moved
+    other = other_core(own)
+    keys = fresh(own, other, latent_gain, lengths)
+    keys, own, other = lax.optimization_barrier((keys, own, other))
     keys = exchange(keys, "tp")
-    parts, queries, values = attend(lengths, own, other_core(own), query_nope, query_rope, own_cache, other_cache)
+    parts, queries, values = attend(lengths, own, other, query_nope, query_rope, own_cache, other_cache)
     parts, keys = lax.optimization_barrier((parts, keys))
     parts = along_y(parts.reshape(CHIPS, ROWS_KV, ATT_W))
     values = along_y(combine(parts, queries, values, keys))
     parts = exchange(project(values, own_out, other_out), "tp")
-    attended, rows = route(parts, mine, other)
-    other_attended = other_core(attended)
+    attended, rows = route(parts, mine, other_mine)
     rows = exchange(rows, "tp")
     parts = along_y(gate(rows, gate_proj, up_proj, other_gate, other_up))
     packed = along_y(hidden(parts))
-    parts = to_owners(down(packed, own_down, other_down))
+    came = other_core(down(packed, other_down))
+    parts, leaving = lax.optimization_barrier((join(down(packed, own_down), came), attended))
+    other_attended = other_core(leaving)
+    parts = exchange(parts, "tp")
     return mix(parts, mine, attended, other_attended, expert_ids, expert_weights)
 
 

time: 180 us -> 177 us (0.983)
  waiting for transfers between devices: 25.4 us -> 14.6 us
  starting transfers between devices: 51.9 us -> 55.4 us
    all_to_all x3, waiting for transfers between devices: 22.1 us -> 8.89 us  [exchange(): lax.all_to_all(array, axis, split_axis=0, concat_axis=0, axis_index_group...]
    ppermute x8 -> x9, starting transfers between devices: 24.3 us -> 30.9 us  [other_core(): lax.ppermute(array, 'kv', [(index, index ^ 1) for index in range(N_KV)])]
    all_to_all x3, starting transfers between devices: 27.6 us -> 24.5 us  [exchange(): lax.all_to_all(array, axis, split_axis=0, concat_axis=0, axis_index_group...]
    ppermute x8 -> x9, waiting for transfers between devices: 3.31 us -> 5.71 us  [other_core(): lax.ppermute(array, 'kv', [(index, index ^ 1) for index in range(N_KV)])]
    all_to_all x6, blocking collectives: 78.9 us -> 80.7 us  [exchange(): lax.all_to_all(array, axis, split_axis=0, concat_axis=0, axis_index_group...]
    unnamed x20 -> x30, local copies, waits for them, and re-layouts: 2.5 us -> 4.26 us
    pallas_call x11 -> x12, Pallas kernels: 19.5 us -> 19 us  [run(): pl.pallas_call(body, out_shape=outs[0] if single else tuple(outs), in_spe...]
  transfers between devices with their start and end apart: 11 -> 12, of which waited for: 6 -> 7; matrix products, arithmetic and copies ran while one was open for 0% -> 0% of each run, Pallas kernels for 3% -> 4%
where the time goes in v4:
time: 177 us; the launch traced here: 175 us
  blocking collectives  80.7 us (46%)
  starting transfers between devices  55.4 us (31%)
  Pallas kernels  19 us (11%)
  waiting for transfers between devices  14.6 us (8%)
  local copies, waits for them, and re-layouts  4.26 us (2%)
    all_to_all x6, blocking collectives, exchange(): lax.all_to_all(array, axis, split_axis=0, concat_axis=0, axis_index_group...  80.7 us
    ppermute x9, starting transfers between devices, other_core(): lax.ppermute(array, 'kv', [(index, index ^ 1) for index in range(N_KV)])  30.9 us
    all_to_all x3, starting transfers between devices, exchange(): lax.all_to_all(array, axis, split_axis=0, concat_axis=0, axis_index_group...  24.5 us
    pallas_call x12, Pallas kernels, run(): pl.pallas_call(body, out_shape=outs[0] if single else tuple(outs), in_spe...  19 us
    all_to_all x3, waiting for transfers between devices, exchange(): lax.all_to_all(array, axis, split_axis=0, concat_axis=0, axis_index_group...  8.89 us
    ppermute x9, waiting for transfers between devices, other_core(): lax.ppermute(array, 'kv', [(index, index ^ 1) for index in range(N_KV)])  5.71 us
    unnamed x30, local copies, waits for them, and re-layouts  4.26 us
  transfers between devices with their start and end apart: 12, of which 7 were waited for; matrix products, arithmetic and copies ran while one was open for 0% of the time, Pallas kernels for 4%

profile of v4, /device:TPU:1, one launch (start us, length us, event | category | flops | bytes accessed | tf_op | source)
XLA Modules:
  0.0 175.0 jit_solution(6661519992666431905)
XLA Ops:
  0.6 0.0 copy-start
  0.6 0.0 copy-start.14
  0.7 0.0 copy-start.13
  0.7 2.2 %shard_map.176 = (bf16[8,304,128]{2,1,0:T(8,128)(2,1)}, f32[64,128]{1,0:T(8,128)}) custom-call(bf16[8,448]{1,0:T(8,128)(2,1)} %refs_0_.1, f32[1,448]{1,0:T(1,128)} %bitcast.18, bf16[448,576]{1,0:T(8,128)(2,1)} %refs_2_.1, bf16[4,32,128]{2,1,0:T(8,128)(2,1)} %bitcast.17, bf16[4,32,128]{2,1,0:T(8,128)(2,1)} %refs_4_.4, f32[1,448]{1,0:T(1,128)} %bitcast.19), custom_call_target="tpu_custom_call" | custom-call | tf_op jit(solution)/shard_map/pallas_call | solution.py:393
  2.9 7.7 %all-to-all-start = ((bf16[8,304,128]{2,1,0:T(8,128)(2,1)}), bf16[8,304,128]{2,1,0:T(8,128)(2,1)S(1)}, u32[]{:S(2)}, u32[]{:S(2)}) async-start(bf16[8,304,128]{2,1,0:T(8,128)(2,1)} %get-tuple-element.31), calls=%async_computation | async-start | bytes 1245184 | tf_op jit(solution)/shard_map/all_to_all | solution.py:499
  10.5 4.7 %collective-permute-start.6 = (bf16[2,576,768]{2,1,0:T(8,128)(2,1)}, bf16[2,576,768]{2,1,0:T(8,128)(2,1)}, u32[]{:S(2)}, u32[]{:S(2)}) collective-permute-start(bf16[2,576,768]{2,1,0:T(8,128)(2,1)} %bitcast.20), channel_id=1, source_target_pairs={{0,32},{32,0},{64,96},{96,64},{128,160},{160,128},{192,224},{224,1... | collective-permute-start | bytes 5308424 | tf_op jit(solution)/shard_map/ppermute | solution.py:507
  15.2 1.9 %collective-permute-start.2 = (bf16[1,448,1024]{2,1,0:T(8,128)(2,1)}, bf16[1,448,1024]{2,1,0:T(8,128)(2,1)S(1)}, u32[]{:S(2)}, u32[]{:S(2)}) collective-permute-start(bf16[1,448,1024]{2,1,0:T(8,128)(2,1)} %refs_3_.3), channel_id=1, source_target_pairs={{0,32},{32,0},{64,96},{96,64},{128,160},{160,128},{192,224},{224,1... | collective-permute-start | bytes 2752520 | tf_op jit(solution)/shard_map/ppermute | solution.py:507
  17.2 2.4 %collective-permute-start.3 = (bf16[1,448,1024]{2,1,0:T(8,128)(2,1)}, bf16[1,448,1024]{2,1,0:T(8,128)(2,1)S(1)}, u32[]{:S(2)}, u32[]{:S(2)}) collective-permute-start(bf16[1,448,1024]{2,1,0:T(8,128)(2,1)} %refs_4_.6), channel_id=1, source_target_pairs={{0,32},{32,0},{64,96},{96,64},{128,160},{160,128},{192,224},{224,1... | collective-permute-start | bytes 2752520 | tf_op jit(solution)/shard_map/ppermute | solution.py:507
  19.6 0.0 copy-done
  19.6 1.9 %collective-permute-start.4 = (bf16[1,448,1024]{2,1,0:T(8,128)(2,1)S(1)}, bf16[1,448,1024]{2,1,0:T(8,128)(2,1)S(1)}, u32[]{:S(2)}, u32[]{:S(2)}) collective-permute-start(bf16[1,448,1024]{2,1,0:T(8,128)(2,1)S(1)} %bitcast.9), channel_id=1, source_target_pairs={{0,32},{32,0},{64,96},{96,64},{128,160},{160,128},{192,224},{224,1... | collective-permute-start | bytes 2752520 | tf_op jit(solution)/shard_map/ppermute | solution.py:507
  21.5 2.4 %collective-permute-start.1 = (f32[64,128]{1,0:T(8,128)}, f32[64,128]{1,0:T(8,128)S(1)}, u32[]{:S(2)}, u32[]{:S(2)}) collective-permute-start(f32[64,128]{1,0:T(8,128)} %get-tuple-element.33.refs_1_), channel_id=1, source_target_pairs={{0,32},{32,0},{64,96},{96,64},{128,160},{160,128},{192,224},{224,1... | collective-permute-start | bytes 98312 | tf_op jit(solution)/shard_map/ppermute | solution.py:507
  23.9 1.0 collective-permute-done.1.refs_2_
  25.0 0.6 copy-done.9
  25.6 2.2 %collective-permute-start = (bf16[448,512]{1,0:T(8,128)(2,1)}, bf16[448,512]{1,0:T(8,128)(2,1)S(1)}, u32[]{:S(2)}, u32[]{:S(2)}) collective-permute-start(bf16[448,512]{1,0:T(8,128)(2,1)} %bitcast.11), channel_id=1, source_target_pairs={{0,32},{32,0},{64,96},{96,64},{128,160},{160,128},{192,224},{224,1... | collective-permute-start | bytes 1376264 | tf_op jit(solution)/shard_map/ppermute | solution.py:507
  27.9 1.7 collective-permute-done.refs_2_
  29.5 0.8 copy-done.6
  30.3 0.0 collective-permute-done.2.refs_1_
  30.3 0.0 collective-permute-done.3.refs_2_
  30.3 0.9 copy-done.1
  31.2 0.0 collective-permute-done.4.refs_1_
  31.2 0.0 all-to-all-done.refs_3_.refs_1_
  31.2 2.2 %collective-permute-start.5 = (bf16[8,304,128]{2,1,0:T(8,128)(2,1)S(1)}, bf16[8,304,128]{2,1,0:T(8,128)(2,1)S(1)}, u32[]{:S(2)}, u32[]{:S(2)}) collective-permute-start(bf16[8,304,128]{2,1,0:T(8,128)(2,1)S(1)} %all-to-all-done.refs_3_.refs_1_), channel_id=1, source_target_pairs={{0,32},{32,0},{64,96},{96,64},{128,160},{160,128},{192,224},{224,1... | collective-permute-start | bytes 1867784 | tf_op jit(solution)/shard_map/ppermute | solution.py:507
  33.5 1.7 collective-permute-done.5.refs_4_.refs_2_
  35.2 0.0 copy-done.14
  35.2 0.0 copy-done.13
  35.2 1.1 shard_map.177
  36.2 0.0 copy-start.3
  36.3 0.8 copy-done.3
  37.1 12.5 %all-to-all-start.1 = ((bf16[32,8,384]{2,1,0:T(8,128)(2,1)}), bf16[32,8,384]{2,1,0:T(8,128)(2,1)}, u32[]{:S(2)}, u32[]{:S(2)}) async-start(bf16[32,8,384]{2,1,0:T(8,128)(2,1)} %shard_map.177), calls=%async_computation.1 | async-start | bytes 393216 | tf_op jit(solution)/shard_map/all_to_all | solution.py:499
  49.6 0.0 collective-permute-done.6.refs_6_
  49.6 0.0 copy-start.4
  49.6 1.1 copy-done.4
  50.7 5.7 %shard_map.178 = (bf16[128,640]{1,0:T(8,128)(2,1)S(1)}, bf16[64,576]{1,0:T(8,128)(2,1)}, bf16[4,8,2,32,128]{4,3,2,1,0:T(8,128)(2,1)}) custom-call(s32[1,2]{1,0:T(1,128)S(1)} %bitcast.16, bf16[8,304,128]{2,1,0:T(8,128)(2,1)S(1)} %all-to-all-done.refs_3_.refs_1_, bf16[8,304,128]{2,1,0:T(8,128)(2,1)S(1)} %copy-done.4, bf16[256,512]{1,0:T(8,128)(2,1)} %refs_3_.2, ...), custom_call_target="tpu_custom_call" | custom-call | flops 2200000000 | bytes 4000000 | tf_op jit(solution)/shard_map/pallas_call | solution.py:393
  56.4 0.0 copy-start.5
  56.4 0.0 copy-start.8
  56.4 0.0 copy-start.10
  56.4 2.6 %all-to-all-done.1.refs_1_ = bf16[32,8,384]{2,1,0:T(8,128)(2,1)} async-done(((bf16[32,8,384]{2,1,0:T(8,128)(2,1)}), bf16[32,8,384]{2,1,0:T(8,128)(2,1)}, u32[]{:S(2)}, u32[]{:S(2)}) %all-to-all-start.1) | async-done | bytes 196640 | tf_op jit(solution)/shard_map/all_to_all | solution.py:499
  59.0 13.9 %all_to_all.45.refs_0_ = bf16[8,16,640]{2,1,0:T(8,128)(2,1)S(1)} all-to-all(bf16[8,16,640]{2,1,0:T(8,128)(2,1)S(1)} %bitcast.13), channel_id=1, replica_groups={{0,64,128,192,256,320,384,448},{32,96,160,224,288,352,416,480},{1,65,12..., dimensions={0} | all-to-all | bytes 327680 | tf_op jit(solution)/shard_map/all_to_all | solution.py:499
  72.9 2.8 %shard_map.179 = bf16[8,16,512]{2,1,0:T(8,128)(2,1)S(1)} custom-call(bf16[8,16,640]{2,1,0:T(8,128)(2,1)S(1)} %all_to_all.45.refs_0_, bf16[32,8,384]{2,1,0:T(8,128)(2,1)} %all-to-all-done.1.refs_1_, bf16[64,576]{1,0:T(8,128)(2,1)} %get-tuple-element.45.refs_2_, bf16[4,8,2,32,128]{4,3,2,1,0:T(8,128)(2,1)} %get-tuple-element.46.refs_3_), custom_call_target="tpu_custom_call" | custom-call | tf_op jit(solution)/shard_map/pallas_call | solution.py:393
  75.7 10.3 %all_to_all.46.refs_0_ = bf16[8,16,512]{2,1,0:T(8,128)(2,1)S(1)} all-to-all(bf16[8,16,512]{2,1,0:T(8,128)(2,1)S(1)} %shard_map.179), channel_id=1, replica_groups={{0,64,128,192,256,320,384,448},{32,96,160,224,288,352,416,480},{1,65,12..., dimensions={0} | all-to-all | bytes 262144 | tf_op jit(solution)/shard_map/all_to_all | solution.py:499
  86.0 0.0 copy-done.5
  86.0 0.0 copy-done.7
  86.0 0.7 shard_map.180
  86.7 15.8 %all_to_all.47.refs_0_ = bf16[32,8,448]{2,1,0:T(8,128)(2,1)S(1)} all-to-all(bf16[32,8,448]{2,1,0:T(8,128)(2,1)S(1)} %shard_map.180), channel_id=1, replica_groups=mesh['kv'=16,'tp'=32] {'tp'}, dimensions={0} | all-to-all | bytes 458752 | tf_op jit(solution)/shard_map/all_to_all | solution.py:499
  102.5 0.0 copy-done.8
  102.5 0.0 copy-done.10
  102.5 0.2 shard_map.181
  102.7 14.1 %all_to_all.48.refs_0_ = bf16[32,8,512]{2,1,0:T(8,128)(2,1)S(1)} all-to-all(bf16[32,8,512]{2,1,0:T(8,128)(2,1)S(1)} %get-tuple-element.49), channel_id=1, replica_groups=mesh['kv'=16,'tp'=32] {'tp'}, dimensions={0} | all-to-all | bytes 524288 | tf_op jit(solution)/shard_map/all_to_all | solution.py:499
  116.8 0.0 copy-done.2
  116.8 3.7 %shard_map.182 = bf16[8,272,128]{2,1,0:T(8,128)(2,1)S(1)} custom-call(bf16[32,8,512]{2,1,0:T(8,128)(2,1)S(1)} %all_to_all.48.refs_0_, bf16[1,448,1024]{2,1,0:T(8,128)(2,1)S(1)} %collective-permute-done.2.refs_1_, bf16[1,448,1024]{2,1,0:T(8,128)(2,1)S(1)} %copy-done.2, bf16[1,448,1024]{2,1,0:T(8,128)(2,1)} %refs_3_.3, bf16[1,448,1024]{2,1,0:T(8,128)(2,1)} %refs_4_.6), custom_call_target="tpu_custom_call" | custom-call | tf_op jit(solution)/shard_map/pallas_call | solution.py:393
  120.5 14.9 %all_to_all.49.refs_0_ = bf16[8,272,128]{2,1,0:T(8,128)(2,1)S(1)} all-to-all(bf16[8,272,128]{2,1,0:T(8,128)(2,1)S(1)} %shard_map.182), channel_id=1, replica_groups={{0,64,128,192,256,320,384,448},{32,96,160,224,288,352,416,480},{1,65,12..., dimensions={0} | all-to-all | bytes 1114112 | tf_op jit(solution)/shard_map/all_to_all | solution.py:499
  135.4 0.1 shard_map.183
  135.5 11.7 %all_to_all.50.refs_0_ = bf16[8,128,128]{2,1,0:T(8,128)(2,1)S(1)} all-to-all(bf16[8,128,128]{2,1,0:T(8,128)(2,1)S(1)} %shard_map.183), channel_id=1, replica_groups={{0,64,128,192,256,320,384,448},{32,96,160,224,288,352,416,480},{1,65,12..., dimensions={0} | all-to-all | bytes 524288 | tf_op jit(solution)/shard_map/all_to_all | solution.py:499
  147.3 0.4 shard_map.185
  147.7 10.5 %collective-permute-start.7 = (bf16[128,448]{1,0:T(8,128)(2,1)S(1)}, bf16[128,448]{1,0:T(8,128)(2,1)S(1)}, u32[]{:S(2)}, u32[]{:S(2)}) collective-permute-start(bf16[128,448]{1,0:T(8,128)(2,1)S(1)} %shard_map.185), channel_id=1, source_target_pairs={{0,32},{32,0},{64,96},{96,64},{128,160},{160,128},{192,224},{224,1... | collective-permute-start | bytes 344072 | tf_op jit(solution)/shard_map/ppermute | solution.py:507
  158.2 0.4 shard_map.184.refs_0_
  158.7 0.5 collective-permute-done.7.refs_1_
  159.2 1.0 shard_map.186
  160.2 4.4 %all-to-all-start.8 = ((bf16[32,8,448]{2,1,0:T(8,128)(2,1)}), bf16[32,8,448]{2,1,0:T(8,128)(2,1)S(1)}, u32[]{:S(2)}, u32[]{:S(2)}) async-start(bf16[32,8,448]{2,1,0:T(8,128)(2,1)} %shard_map.186), calls=%async_computation.8 | async-start | bytes 524288 | tf_op jit(solution)/shard_map/all_to_all | solution.py:499
  164.6 2.6 %collective-permute-start.8 = (bf16[8,448]{1,0:T(8,128)(2,1)S(1)}, bf16[8,448]{1,0:T(8,128)(2,1)S(1)}, u32[]{:S(2)}, u32[]{:S(2)}) collective-permute-start(bf16[8,448]{1,0:T(8,128)(2,1)S(1)} %get-tuple-element.55.refs_2_), channel_id=1, source_target_pairs={{0,32},{32,0},{64,96},{96,64},{128,160},{160,128},{192,224},{224,1... | collective-permute-start | bytes 21512 | tf_op jit(solution)/shard_map/ppermute | solution.py:507
  167.1 0.8 collective-permute-done.8.refs_3_
  167.9 6.3 %all-to-all-done.8.refs_0_ = bf16[32,8,448]{2,1,0:T(8,128)(2,1)S(1)} async-done(((bf16[32,8,448]{2,1,0:T(8,128)(2,1)}), bf16[32,8,448]{2,1,0:T(8,128)(2,1)S(1)}, u32[]{:S(2)}, u32[]{:S(2)}) %all-to-all-start.8) | async-done | bytes 229408 | tf_op jit(solution)/shard_map/all_to_all | solution.py:499
  174.3 0.0 copy-done.12
  174.3 0.7 shard_map.187
  (9 shorter events, 0.0 us)
Async XLA Ops:
  0.6 19.0 %copy-start = (bf16[1,1024,448]{1,2,0:T(8,128)(2,1)S(1)}, bf16[1,1024,448]{1,2,0:T(8,128)(2,1)}, u32[]{:S(2)}) copy-start(bf16[1,1024,448]{1,2,0:T(8,128)(2,1)} %param.33) | copy-start | bytes 2752516
  0.6 34.5 %copy-start.14 = (s32[2]{0:T(128)S(1)}, s32[2]{0:T(128)}, u32[]{:S(2)}) copy-start(s32[2]{0:T(128)} %param.24) | copy-start | bytes 28
  0.7 34.5 %copy-start.13 = (f32[512]{0:T(512)S(1)}, f32[512]{0:T(512)}, u32[]{:S(2)}) copy-start(f32[512]{0:T(512)} %param.20) | copy-start | bytes 6148
  2.9 28.3 %all-to-all-start = ((bf16[8,304,128]{2,1,0:T(8,128)(2,1)}), bf16[8,304,128]{2,1,0:T(8,128)(2,1)S(1)}, u32[]{:S(2)}, u32[]{:S(2)}) async-start(bf16[8,304,128]{2,1,0:T(8,128)(2,1)} %get-tuple-element.31), calls=%async_computation | async-start | bytes 1245184 | tf_op jit(solution)/shard_map/all_to_all | solution.py:499
  10.5 39.0 %collective-permute-start.6 = (bf16[2,576,768]{2,1,0:T(8,128)(2,1)}, bf16[2,576,768]{2,1,0:T(8,128)(2,1)}, u32[]{:S(2)}, u32[]{:S(2)}) collective-permute-start(bf16[2,576,768]{2,1,0:T(8,128)(2,1)} %bitcast.20), channel_id=1, source_target_pairs={{0,32},{32,0},{64,96},{96,64},{128,160},{160,128},{192,224},{224,1... | collective-permute-start | bytes 5308424 | tf_op jit(solution)/shard_map/ppermute | solution.py:507
  15.2 15.0 %collective-permute-start.2 = (bf16[1,448,1024]{2,1,0:T(8,128)(2,1)}, bf16[1,448,1024]{2,1,0:T(8,128)(2,1)S(1)}, u32[]{:S(2)}, u32[]{:S(2)}) collective-permute-start(bf16[1,448,1024]{2,1,0:T(8,128)(2,1)} %refs_3_.3), channel_id=1, source_target_pairs={{0,32},{32,0},{64,96},{96,64},{128,160},{160,128},{192,224},{224,1... | collective-permute-start | bytes 2752520 | tf_op jit(solution)/shard_map/ppermute | solution.py:507
  17.2 13.1 %collective-permute-start.3 = (bf16[1,448,1024]{2,1,0:T(8,128)(2,1)}, bf16[1,448,1024]{2,1,0:T(8,128)(2,1)S(1)}, u32[]{:S(2)}, u32[]{:S(2)}) collective-permute-start(bf16[1,448,1024]{2,1,0:T(8,128)(2,1)} %refs_4_.6), channel_id=1, source_target_pairs={{0,32},{32,0},{64,96},{96,64},{128,160},{160,128},{192,224},{224,1... | collective-permute-start | bytes 2752520 | tf_op jit(solution)/shard_map/ppermute | solution.py:507
  19.6 11.6 %collective-permute-start.4 = (bf16[1,448,1024]{2,1,0:T(8,128)(2,1)S(1)}, bf16[1,448,1024]{2,1,0:T(8,128)(2,1)S(1)}, u32[]{:S(2)}, u32[]{:S(2)}) collective-permute-start(bf16[1,448,1024]{2,1,0:T(8,128)(2,1)S(1)} %bitcast.9), channel_id=1, source_target_pairs={{0,32},{32,0},{64,96},{96,64},{128,160},{160,128},{192,224},{224,1... | collective-permute-start | bytes 2752520 | tf_op jit(solution)/shard_map/ppermute | solution.py:507
  21.5 3.5 %collective-permute-start.1 = (f32[64,128]{1,0:T(8,128)}, f32[64,128]{1,0:T(8,128)S(1)}, u32[]{:S(2)}, u32[]{:S(2)}) collective-permute-start(f32[64,128]{1,0:T(8,128)} %get-tuple-element.33.refs_1_), channel_id=1, source_target_pairs={{0,32},{32,0},{64,96},{96,64},{128,160},{160,128},{192,224},{224,1... | collective-permute-start | bytes 98312 | tf_op jit(solution)/shard_map/ppermute | solution.py:507
  25.0 0.6 copy-start.9
  25.6 3.9 %collective-permute-start = (bf16[448,512]{1,0:T(8,128)(2,1)}, bf16[448,512]{1,0:T(8,128)(2,1)S(1)}, u32[]{:S(2)}, u32[]{:S(2)}) collective-permute-start(bf16[448,512]{1,0:T(8,128)(2,1)} %bitcast.11), channel_id=1, source_target_pairs={{0,32},{32,0},{64,96},{96,64},{128,160},{160,128},{192,224},{224,1... | collective-permute-start | bytes 1376264 | tf_op jit(solution)/shard_map/ppermute | solution.py:507
  29.5 0.8 copy-start.6
  30.3 0.9 copy-start.1
  31.2 3.9 %collective-permute-start.5 = (bf16[8,304,128]{2,1,0:T(8,128)(2,1)S(1)}, bf16[8,304,128]{2,1,0:T(8,128)(2,1)S(1)}, u32[]{:S(2)}, u32[]{:S(2)}) collective-permute-start(bf16[8,304,128]{2,1,0:T(8,128)(2,1)S(1)} %all-to-all-done.refs_3_.refs_1_), channel_id=1, source_target_pairs={{0,32},{32,0},{64,96},{96,64},{128,160},{160,128},{192,224},{224,1... | collective-permute-start | bytes 1867784 | tf_op jit(solution)/shard_map/ppermute | solution.py:507
  36.2 0.8 copy-start.3
  37.1 21.9 %all-to-all-start.1 = ((bf16[32,8,384]{2,1,0:T(8,128)(2,1)}), bf16[32,8,384]{2,1,0:T(8,128)(2,1)}, u32[]{:S(2)}, u32[]{:S(2)}) async-start(bf16[32,8,384]{2,1,0:T(8,128)(2,1)} %shard_map.177), calls=%async_computation.1 | async-start | bytes 393216 | tf_op jit(solution)/shard_map/all_to_all | solution.py:499
  49.6 1.1 copy-start.4
  56.4 29.7 %copy-start.5 = (bf16[512,448]{0,1:T(8,128)(2,1)S(1)}, bf16[512,448]{0,1:T(8,128)(2,1)}, u32[]{:S(2)}) copy-start(bf16[512,448]{0,1:T(8,128)(2,1)} %param.27) | copy-start | bytes 1376260
  56.4 46.1 %copy-start.8 = (f32[64,128]{1,0:T(8,128)S(1)}, f32[64,128]{1,0:T(8,128)}, u32[]{:S(2)}) copy-start(f32[64,128]{1,0:T(8,128)} %get-tuple-element.33.refs_1_) | copy-start | bytes 98308
  56.4 46.1 %copy-start.10 = (f32[64,128]{1,0:T(8,128)S(1)}, f32[64,128]{1,0:T(8,128)}, u32[]{:S(2)}) copy-start(f32[64,128]{1,0:T(8,128)} %copy-done.9) | copy-start | bytes 98308
  59.0 27.0 %copy-start.7 = (bf16[448,512]{1,0:T(8,128)(2,1)S(1)}, bf16[448,512]{1,0:T(8,128)(2,1)}, u32[]{:S(2)}) copy-start(bf16[448,512]{1,0:T(8,128)(2,1)} %copy-done.6) | copy-start | bytes 1376260
  72.9 43.9 %copy-start.2 = (bf16[1,448,1024]{2,1,0:T(8,128)(2,1)S(1)}, bf16[1,448,1024]{2,1,0:T(8,128)(2,1)}, u32[]{:S(2)}) copy-start(bf16[1,448,1024]{2,1,0:T(8,128)(2,1)} %copy-done.1) | copy-start | bytes 2752516
  147.3 27.0 %copy-start.11 = (s32[8,8]{1,0:T(8,128)S(1)}, s32[8,8]{1,0:T(8,128)}, u32[]{:S(2)}) copy-start(s32[8,8]{1,0:T(8,128)} %refs_4_.7) | copy-start | bytes 772
  147.3 27.0 %copy-start.12 = (f32[8,8]{1,0:T(8,128)S(1)}, f32[8,8]{1,0:T(8,128)}, u32[]{:S(2)}) copy-start(f32[8,8]{1,0:T(8,128)} %refs_5_.1) | copy-start | bytes 772
  147.7 11.5 %collective-permute-start.7 = (bf16[128,448]{1,0:T(8,128)(2,1)S(1)}, bf16[128,448]{1,0:T(8,128)(2,1)S(1)}, u32[]{:S(2)}, u32[]{:S(2)}) collective-permute-start(bf16[128,448]{1,0:T(8,128)(2,1)S(1)} %shard_map.185), channel_id=1, source_target_pairs={{0,32},{32,0},{64,96},{96,64},{128,160},{160,128},{192,224},{224,1... | collective-permute-start | bytes 344072 | tf_op jit(solution)/shard_map/ppermute | solution.py:507
  160.2 14.1 %all-to-all-start.8 = ((bf16[32,8,448]{2,1,0:T(8,128)(2,1)}), bf16[32,8,448]{2,1,0:T(8,128)(2,1)S(1)}, u32[]{:S(2)}, u32[]{:S(2)}) async-start(bf16[32,8,448]{2,1,0:T(8,128)(2,1)} %shard_map.186), calls=%async_computation.8 | async-start | bytes 524288 | tf_op jit(solution)/shard_map/all_to_all | solution.py:499
  164.6 3.4 %collective-permute-start.8 = (bf16[8,448]{1,0:T(8,128)(2,1)S(1)}, bf16[8,448]{1,0:T(8,128)(2,1)S(1)}, u32[]{:S(2)}, u32[]{:S(2)}) collective-permute-start(bf16[8,448]{1,0:T(8,128)(2,1)S(1)} %get-tuple-element.55.refs_2_), channel_id=1, source_target_pairs={{0,32},{32,0},{64,96},{96,64},{128,160},{160,128},{192,224},{224,1... | collective-permute-start | bytes 21512 | tf_op jit(solution)/shard_map/ppermute | solution.py:507

commit v5 on v4

--- a/solution.py
+++ b/solution.py
@@ -244,6 +244,14 @@
         block = keys_ref[step * (PAIRS // ROWS_TP) + kv // 2].astype(F32)
         keys.append(jnp.concatenate([block[:, :256], swap_halves(block[:, :256]), block[:, 256 : 256 + ROPE]], axis=1))
     keys = jnp.concatenate(keys, axis=0).astype(BF16)
+    cached = []
+    for head in range(HEADS_DEV):
+        peak = stats[:, :, head : head + 1]
+        total = stats[:, :, HEADS_DEV + head : HEADS_DEV + head + 1]
+        top = jnp.max(peak, axis=0)
+        keep = jnp.exp(peak - top[None])
+        part = parts_ref[:, :, head * VDIM : (head + 1) * VDIM].astype(F32)
+        cached.append((top, jnp.sum(part * keep, axis=0), jnp.sum(total * keep, axis=0)))
     for fetch in fetches:
         fetch.wait()
     scores = dot(own_ref[...], keys, NT) * SCALE
@@ -255,18 +263,13 @@
     weights = jnp.where(causal, jnp.exp(scores - fresh_peak), 0.0).astype(BF16)
     fresh_total = jnp.sum(weights.astype(F32), axis=1, keepdims=True)
     fresh_latent = dot(weights, keys[:, :LAT]).astype(BF16)
-    for head in range(HEADS_DEV):
+    for head, (peak, value, total) in enumerate(cached):
         own = slice(head * ROWS_KV, (head + 1) * ROWS_KV)
-        peak = stats[:, :, head : head + 1]
-        total = stats[:, :, HEADS_DEV + head : HEADS_DEV + head + 1]
-        top = jnp.maximum(jnp.max(peak, axis=0), fresh_peak[own])
-        keep = jnp.exp(peak - top[None])
-        fresh_keep = jnp.exp(fresh_peak[own] - top)
+        top = jnp.maximum(peak, fresh_peak[own])
+        keep, fresh_keep = jnp.exp(peak - top), jnp.exp(fresh_peak[own] - top)
         value_up = values_ref[head].reshape(LAT, VDIM)
-        part = parts_ref[:, :, head * VDIM : (head + 1) * VDIM].astype(F32)
-        value = jnp.sum(part * keep, axis=0) + dot(fresh_latent[own], value_up) * fresh_keep
-        whole = jnp.sum(total * keep, axis=0) + fresh_total[own] * fresh_keep
-        value = (value / whole).astype(BF16)
+        value = value * keep + dot(fresh_latent[own], value_up) * fresh_keep
+        value = (value / (total * keep + fresh_total[own] * fresh_keep)).astype(BF16)
         for place in range(CHIPS):
             out_ref[place, :, head * VDIM : (head + 1) * VDIM] = value
 
@@ -307,13 +310,12 @@
 def gate_kernel(
     rows_ref, other_gate_ref, other_up_ref, own_gate_hbm, own_up_hbm, out_ref, own_gate_ref, own_up_ref, sems,
 ):
-    fetches = []
-    for place in range(CHIPS):
-        columns = pl.ds(place * HID_Y, HID_Y)
-        for source, target in ((own_gate_hbm, own_gate_ref), (own_up_hbm, own_up_ref)):
-            at = (0, slice(None), columns)
-            fetches.append(pltpu.make_async_copy(source.at[at], target.at[at], sems.at[len(fetches)]))
-            fetches[-1].start()
+    fetches = [
+        pltpu.make_async_copy(own_gate_hbm, own_gate_ref, sems.at[0]),
+        pltpu.make_async_copy(own_up_hbm, own_up_ref, sems.at[1]),
+    ]
+    for fetch in fetches:
+        fetch.start()
     rows = rows_ref[...].astype(F32).reshape(TOKROWS, 512).astype(BF16)
     shape = (CLASS, TOKROWS)
     place, row = iota(shape, 0), iota(shape, 1)
@@ -325,14 +327,16 @@
     second = ((sixteen >= 3) & (sixteen < 6) & (column == FEAT + sixteen - 3)).astype(F32).astype(BF16)
     squares = (dot(first, own, NT) + dot(second, other, NT)).astype(BF16)
     own, other = own[:, :FEAT], other[:, :FEAT]
+    gate = dot(other, other_gate_ref[0])
+    up = dot(other, other_up_ref[0])
+    for fetch in fetches:
+        fetch.wait()
+    gate = gate + dot(own, own_gate_ref[0])
+    up = up + dot(own, own_up_ref[0])
     for place in range(CHIPS):
         columns = slice(place * HID_Y, (place + 1) * HID_Y)
-        fetches[2 * place].wait()
-        fetches[2 * place + 1].wait()
-        gate = dot(own, own_gate_ref[0, :, columns]) + dot(other, other_gate_ref[0, :, columns])
-        up = dot(own, own_up_ref[0, :, columns]) + dot(other, other_up_ref[0, :, columns])
-        out_ref[place, :CLASS, :] = gate.astype(BF16)
-        out_ref[place, CLASS : 2 * CLASS, :] = up.astype(BF16)
+        out_ref[place, :CLASS, :] = gate[:, columns].astype(BF16)
+        out_ref[place, CLASS : 2 * CLASS, :] = up[:, columns].astype(BF16)
         out_ref[place, 2 * CLASS :, :] = squares
 
 
@@ -436,7 +440,7 @@
             shaped(HEADS_DEV, CHIPS, 2, LAT_KV, 128),
         ],
         lengths.reshape(1, SEQS),
-        fetched=(own, other, in_hbm(query_nope), in_hbm(query_rope), in_hbm(keys), other_keys),
+        fetched=(in_hbm(own), in_hbm(other), in_hbm(query_nope), in_hbm(query_rope), in_hbm(keys), other_keys),
         left=2,
         scratch=[
             pltpu.VMEM((2 * HEADS_DEV, CHIPS, 2, LAT_KV, 128), BF16),
@@ -474,7 +478,7 @@
     weights = pltpu.VMEM(own_gate.shape, BF16)
     return run(
         gate_kernel, shaped(CHIPS, PART_ROWS, 128), rows, other_gate, other_up,
-        fetched=(in_hbm(own_gate), in_hbm(own_up)), scratch=[weights, weights, pltpu.SemaphoreType.DMA((2 * CHIPS,))],
+        fetched=(in_hbm(own_gate), in_hbm(own_up)), scratch=[weights, weights, pltpu.SemaphoreType.DMA((2,))],
     )
 
 
@@ -513,21 +517,22 @@
 ):
     ups, mine = start(tokens, attn_gain, down_kv, key_up, value_up, mlp_gain)
     own_cache, own_out, own_down = jnp.swapaxes(cache, 1, 2), out_proj.T, jnp.swapaxes(down_proj, 1, 2)
-    ups, waiting, *moved = lax.optimization_barrier((ups, own_cache, own_out, mine, gate_proj, up_proj, own_down))
+    ups, waiting, *moved = lax.optimization_barrier((ups, own_cache, gate_proj, up_proj, own_down))
     own = along_y(ups)
+    other_cache = other_core(waiting)
     moved = [other_core(array) for array in moved]
-    other_out, other_mine, other_gate, other_up, other_down = moved
-    other_cache = other_core(waiting)
-    own, *moved = lax.optimization_barrier((own, other_out, other_mine, other_gate, other_up, other_down))
-    other_out, other_mine, other_gate, other_up, other_down = moved
+    own, other_gate, other_up, other_down = lax.optimization_barrier((own, *moved))
     other = other_core(own)
     keys = fresh(own, other, latent_gain, lengths)
     keys, own, other = lax.optimization_barrier((keys, own, other))
     keys = exchange(keys, "tp")
     parts, queries, values = attend(lengths, own, other, query_nope, query_rope, own_cache, other_cache)
-    parts, keys = lax.optimization_barrier((parts, keys))
+    parts, keys, *moved = lax.optimization_barrier((parts, keys, own_out, mine))
+    other_out, other_mine = (other_core(array) for array in moved)
     parts = along_y(parts.reshape(CHIPS, ROWS_KV, ATT_W))
-    values = along_y(combine(parts, queries, values, keys))
+    values = combine(parts, queries, values, keys)
+    values, other_out, other_mine = lax.optimization_barrier((values, other_out, other_mine))
+    values = along_y(values)
     parts = exchange(project(values, own_out, other_out), "tp")
     attended, rows = route(parts, mine, other_mine)
     rows = exchange(rows, "tp")

time: 177 us -> 181 us (1.023)
  blocking collectives: 80.7 us -> 68.9 us
  waiting for transfers between devices: 14.6 us -> 25.6 us
  starting transfers between devices: 55.4 us -> 62 us
  local copies, waits for them, and re-layouts: 4.26 us -> 1.81 us
    all_to_all x3 -> x4, waiting for transfers between devices: 8.89 us -> 21.1 us  [exchange(): lax.all_to_all(array, axis, split_axis=0, concat_axis=0, axis_index_group...]
    all_to_all x6 -> x5, blocking collectives: 80.7 us -> 68.9 us  [exchange(): lax.all_to_all(array, axis, split_axis=0, concat_axis=0, axis_index_group...]
    all_to_all x3 -> x4, starting transfers between devices: 24.5 us -> 29.1 us  [exchange(): lax.all_to_all(array, axis, split_axis=0, concat_axis=0, axis_index_group...]
    unnamed x30 -> x22, local copies, waits for them, and re-layouts: 4.26 us -> 1.81 us
    ppermute x9, starting transfers between devices: 30.9 us -> 32.9 us  [other_core(): lax.ppermute(array, 'kv', [(index, index ^ 1) for index in range(N_KV)])]
  transfers between devices with their start and end apart: 12 -> 13, of which waited for: 7 -> 9; matrix products, arithmetic and copies ran while one was open for 0% -> 0% of each run, Pallas kernels for 4% -> 6%
where the time goes in v5:
time: 181 us; the launch traced here: 179 us
  blocking collectives  68.9 us (38%)
  starting transfers between devices  62 us (34%)
  waiting for transfers between devices  25.6 us (14%)
  Pallas kernels  19.5 us (11%)
  local copies, waits for them, and re-layouts  1.81 us (1%)
    all_to_all x5, blocking collectives, exchange(): lax.all_to_all(array, axis, split_axis=0, concat_axis=0, axis_index_group...  68.9 us
    ppermute x9, starting transfers between devices, other_core(): lax.ppermute(array, 'kv', [(index, index ^ 1) for index in range(N_KV)])  32.9 us
    all_to_all x4, starting transfers between devices, exchange(): lax.all_to_all(array, axis, split_axis=0, concat_axis=0, axis_index_group...  29.1 us
    all_to_all x4, waiting for transfers between devices, exchange(): lax.all_to_all(array, axis, split_axis=0, concat_axis=0, axis_index_group...  21.1 us
    pallas_call x12, Pallas kernels, run(): pl.pallas_call(body, out_shape=outs[0] if single else tuple(outs), in_spe...  19.5 us
    ppermute x9, waiting for transfers between devices, other_core(): lax.ppermute(array, 'kv', [(index, index ^ 1) for index in range(N_KV)])  4.45 us
  transfers between devices with their start and end apart: 13, of which 9 were waited for; matrix products, arithmetic and copies ran while one was open for 0% of the time, Pallas kernels for 6%

profile of v5, /device:TPU:1, one launch (start us, length us, event | category | flops | bytes accessed | tf_op | source)
XLA Modules:
  0.0 178.8 jit_solution(1622097061558438465)
XLA Ops:
  0.6 0.0 copy-start.1
  0.6 0.0 copy-start.10
  0.7 0.0 copy-start.9
  0.7 2.2 %shard_map.176 = (bf16[8,304,128]{2,1,0:T(8,128)(2,1)}, f32[64,128]{1,0:T(8,128)}) custom-call(bf16[8,448]{1,0:T(8,128)(2,1)} %refs_0_.1, f32[1,448]{1,0:T(1,128)} %bitcast.17, bf16[448,576]{1,0:T(8,128)(2,1)} %refs_2_.1, bf16[4,32,128]{2,1,0:T(8,128)(2,1)} %bitcast.16, bf16[4,32,128]{2,1,0:T(8,128)(2,1)} %refs_4_.4, f32[1,448]{1,0:T(1,128)} %bitcast.18), custom_call_target="tpu_custom_call" | custom-call | tf_op jit(solution)/shard_map/pallas_call | solution.py:397
  2.9 7.7 %all-to-all-start = ((bf16[8,304,128]{2,1,0:T(8,128)(2,1)}), bf16[8,304,128]{2,1,0:T(8,128)(2,1)S(1)}, u32[]{:S(2)}, u32[]{:S(2)}) async-start(bf16[8,304,128]{2,1,0:T(8,128)(2,1)} %get-tuple-element.31), calls=%async_computation | async-start | bytes 1245184 | tf_op jit(solution)/shard_map/all_to_all | solution.py:503
  10.5 4.7 %collective-permute-start.4 = (bf16[2,576,768]{2,1,0:T(8,128)(2,1)}, bf16[2,576,768]{2,1,0:T(8,128)(2,1)}, u32[]{:S(2)}, u32[]{:S(2)}) collective-permute-start(bf16[2,576,768]{2,1,0:T(8,128)(2,1)} %bitcast.19), channel_id=1, source_target_pairs={{0,32},{32,0},{64,96},{96,64},{128,160},{160,128},{192,224},{224,1... | collective-permute-start | bytes 5308424 | tf_op jit(solution)/shard_map/ppermute | solution.py:511
  15.2 1.9 %collective-permute-start = (bf16[1,448,1024]{2,1,0:T(8,128)(2,1)}, bf16[1,448,1024]{2,1,0:T(8,128)(2,1)S(1)}, u32[]{:S(2)}, u32[]{:S(2)}) collective-permute-start(bf16[1,448,1024]{2,1,0:T(8,128)(2,1)} %refs_3_.3), channel_id=1, source_target_pairs={{0,32},{32,0},{64,96},{96,64},{128,160},{160,128},{192,224},{224,1... | collective-permute-start | bytes 2752520 | tf_op jit(solution)/shard_map/ppermute | solution.py:511
  17.2 2.4 %collective-permute-start.1 = (bf16[1,448,1024]{2,1,0:T(8,128)(2,1)}, bf16[1,448,1024]{2,1,0:T(8,128)(2,1)S(1)}, u32[]{:S(2)}, u32[]{:S(2)}) collective-permute-start(bf16[1,448,1024]{2,1,0:T(8,128)(2,1)} %refs_4_.6), channel_id=1, source_target_pairs={{0,32},{32,0},{64,96},{96,64},{128,160},{160,128},{192,224},{224,1... | collective-permute-start | bytes 2752520 | tf_op jit(solution)/shard_map/ppermute | solution.py:511
  19.6 0.0 copy-done.1
  19.6 1.9 %collective-permute-start.2 = (bf16[1,448,1024]{2,1,0:T(8,128)(2,1)S(1)}, bf16[1,448,1024]{2,1,0:T(8,128)(2,1)S(1)}, u32[]{:S(2)}, u32[]{:S(2)}) collective-permute-start(bf16[1,448,1024]{2,1,0:T(8,128)(2,1)S(1)} %bitcast.9), channel_id=1, source_target_pairs={{0,32},{32,0},{64,96},{96,64},{128,160},{160,128},{192,224},{224,1... | collective-permute-start | bytes 2752520 | tf_op jit(solution)/shard_map/ppermute | solution.py:511
  21.5 0.0 collective-permute-done.refs_1_
  21.5 0.3 collective-permute-done.1.refs_2_
  21.9 1.0 copy-done.2
  22.8 1.1 collective-permute-done.2.refs_1_
  24.0 3.9 %all-to-all-done.refs_3_.refs_1_ = bf16[8,304,128]{2,1,0:T(8,128)(2,1)S(1)} async-done(((bf16[8,304,128]{2,1,0:T(8,128)(2,1)}), bf16[8,304,128]{2,1,0:T(8,128)(2,1)S(1)}, u32[]{:S(2)}, u32[]{:S(2)}) %all-to-all-start) | async-done | bytes 622624 | tf_op jit(solution)/shard_map/all_to_all | solution.py:503
  27.8 0.0 copy-start
  27.8 5.2 %collective-permute-start.3 = (bf16[8,304,128]{2,1,0:T(8,128)(2,1)S(1)}, bf16[8,304,128]{2,1,0:T(8,128)(2,1)S(1)}, u32[]{:S(2)}, u32[]{:S(2)}) collective-permute-start(bf16[8,304,128]{2,1,0:T(8,128)(2,1)S(1)} %all-to-all-done.refs_3_.refs_1_), channel_id=1, source_target_pairs={{0,32},{32,0},{64,96},{96,64},{128,160},{160,128},{192,224},{224,1... | collective-permute-start | bytes 1867784 | tf_op jit(solution)/shard_map/ppermute | solution.py:511
  33.1 1.6 collective-permute-done.3.refs_4_.refs_2_
  34.7 0.0 copy-done.10
  34.7 0.0 copy-done.9
  34.7 1.1 shard_map.177
  35.8 0.0 copy-start.4
  35.8 0.8 copy-done.4
  36.6 13.0 %all-to-all-start.1 = ((bf16[32,8,384]{2,1,0:T(8,128)(2,1)}), bf16[32,8,384]{2,1,0:T(8,128)(2,1)}, u32[]{:S(2)}, u32[]{:S(2)}) async-start(bf16[32,8,384]{2,1,0:T(8,128)(2,1)} %shard_map.177), calls=%async_computation.1 | async-start | bytes 393216 | tf_op jit(solution)/shard_map/all_to_all | solution.py:503
  49.6 0.0 copy-start.6
  49.6 0.0 collective-permute-done.4.refs_6_
  49.6 0.0 copy-done
  49.6 6.7 %shard_map.178 = (bf16[128,640]{1,0:T(8,128)(2,1)}, bf16[64,576]{1,0:T(8,128)(2,1)}, bf16[4,8,2,32,128]{4,3,2,1,0:T(8,128)(2,1)}) custom-call(s32[1,2]{1,0:T(1,128)S(1)} %bitcast.15, bf16[8,304,128]{2,1,0:T(8,128)(2,1)} %copy-done, bf16[8,304,128]{2,1,0:T(8,128)(2,1)} %copy-done.4, bf16[256,512]{1,0:T(8,128)(2,1)} %refs_3_.2, bf16[256,256]{1,0:T(8,128)(2,1)} %refs_4_.5, ...), custom_call_target="tpu_custom_call" | custom-call | flops 2200000000 | bytes 4000000 | tf_op jit(solution)/shard_map/pallas_call | solution.py:397
  56.3 0.0 copy-start.5
  56.3 2.6 %all-to-all-done.1.refs_1_ = bf16[32,8,384]{2,1,0:T(8,128)(2,1)} async-done(((bf16[32,8,384]{2,1,0:T(8,128)(2,1)}), bf16[32,8,384]{2,1,0:T(8,128)(2,1)}, u32[]{:S(2)}, u32[]{:S(2)}) %all-to-all-start.1) | async-done | bytes 196640 | tf_op jit(solution)/shard_map/all_to_all | solution.py:503
  59.0 4.8 %collective-permute-start.5 = (bf16[448,512]{1,0:T(8,128)(2,1)}, bf16[448,512]{1,0:T(8,128)(2,1)}, u32[]{:S(2)}, u32[]{:S(2)}) collective-permute-start(bf16[448,512]{1,0:T(8,128)(2,1)} %bitcast.11), channel_id=1, source_target_pairs={{0,32},{32,0},{64,96},{96,64},{128,160},{160,128},{192,224},{224,1... | collective-permute-start | bytes 1376264 | tf_op jit(solution)/shard_map/ppermute | solution.py:511
  63.8 3.4 %all-to-all-start.2 = ((bf16[8,16,640]{2,1,0:T(8,128)(2,1)}), bf16[8,16,640]{2,1,0:T(8,128)(2,1)S(1)}, u32[]{:S(2)}, u32[]{:S(2)}) async-start(bf16[8,16,640]{2,1,0:T(8,128)(2,1)} %bitcast.8), calls=%async_computation.2 | async-start | bytes 327680 | tf_op jit(solution)/shard_map/all_to_all | solution.py:503
  67.2 0.0 copy-done.6
  67.2 1.9 %collective-permute-start.6 = (f32[64,128]{1,0:T(8,128)S(1)}, f32[64,128]{1,0:T(8,128)S(1)}, u32[]{:S(2)}, u32[]{:S(2)}) collective-permute-start(f32[64,128]{1,0:T(8,128)S(1)} %copy-done.6), channel_id=1, source_target_pairs={{0,32},{32,0},{64,96},{96,64},{128,160},{160,128},{192,224},{224,1... | collective-permute-start | bytes 98312 | tf_op jit(solution)/shard_map/ppermute | solution.py:511
  69.1 8.3 %all-to-all-done.2.refs_0_ = bf16[8,16,640]{2,1,0:T(8,128)(2,1)S(1)} async-done(((bf16[8,16,640]{2,1,0:T(8,128)(2,1)}), bf16[8,16,640]{2,1,0:T(8,128)(2,1)S(1)}, u32[]{:S(2)}, u32[]{:S(2)}) %all-to-all-start.2) | async-done | bytes 163872 | tf_op jit(solution)/shard_map/all_to_all | solution.py:503
  77.4 0.0 copy-start.3
  77.4 2.7 %shard_map.179 = bf16[8,16,512]{2,1,0:T(8,128)(2,1)S(1)} custom-call(bf16[8,16,640]{2,1,0:T(8,128)(2,1)S(1)} %all-to-all-done.2.refs_0_, bf16[32,8,384]{2,1,0:T(8,128)(2,1)} %all-to-all-done.1.refs_1_, bf16[64,576]{1,0:T(8,128)(2,1)} %get-tuple-element.44.refs_2_, bf16[4,8,2,32,128]{4,3,2,1,0:T(8,128)(2,1)} %get-tuple-element.45.refs_3_), custom_call_target="tpu_custom_call" | custom-call | tf_op jit(solution)/shard_map/pallas_call | solution.py:397
  80.1 0.0 collective-permute-done.6.refs_2_
  80.1 0.0 collective-permute-done.5.refs_2_
  80.1 10.7 %all_to_all.45.refs_0_ = bf16[8,16,512]{2,1,0:T(8,128)(2,1)S(1)} all-to-all(bf16[8,16,512]{2,1,0:T(8,128)(2,1)S(1)} %shard_map.179), channel_id=1, replica_groups={{0,64,128,192,256,320,384,448},{32,96,160,224,288,352,416,480},{1,65,12..., dimensions={0} | all-to-all | bytes 262144 | tf_op jit(solution)/shard_map/all_to_all | solution.py:503
  90.8 0.0 copy-done.5
  90.8 1.7 shard_map.180
  92.5 14.1 %all_to_all.46.refs_0_ = bf16[32,8,448]{2,1,0:T(8,128)(2,1)S(1)} all-to-all(bf16[32,8,448]{2,1,0:T(8,128)(2,1)S(1)} %shard_map.180), channel_id=1, replica_groups=mesh['kv'=16,'tp'=32] {'tp'}, dimensions={0} | all-to-all | bytes 458752 | tf_op jit(solution)/shard_map/all_to_all | solution.py:503
  106.6 0.2 shard_map.181
  106.8 14.6 %all_to_all.47.refs_0_ = bf16[32,8,512]{2,1,0:T(8,128)(2,1)S(1)} all-to-all(bf16[32,8,512]{2,1,0:T(8,128)(2,1)S(1)} %get-tuple-element.51), channel_id=1, replica_groups=mesh['kv'=16,'tp'=32] {'tp'}, dimensions={0} | all-to-all | bytes 524288 | tf_op jit(solution)/shard_map/all_to_all | solution.py:503
  121.4 0.0 copy-done.3
  121.4 2.3 %shard_map.182 = bf16[8,272,128]{2,1,0:T(8,128)(2,1)S(1)} custom-call(bf16[32,8,512]{2,1,0:T(8,128)(2,1)S(1)} %all_to_all.47.refs_0_, bf16[1,448,1024]{2,1,0:T(8,128)(2,1)S(1)} %collective-permute-done.refs_1_, bf16[1,448,1024]{2,1,0:T(8,128)(2,1)S(1)} %copy-done.3, bf16[1,448,1024]{2,1,0:T(8,128)(2,1)} %refs_3_.3, bf16[1,448,1024]{2,1,0:T(8,128)(2,1)} %refs_4_.6), custom_call_target="tpu_custom_call" | custom-call | tf_op jit(solution)/shard_map/pallas_call | solution.py:397
  123.7 16.4 %all_to_all.48.refs_0_ = bf16[8,272,128]{2,1,0:T(8,128)(2,1)S(1)} all-to-all(bf16[8,272,128]{2,1,0:T(8,128)(2,1)S(1)} %shard_map.182), channel_id=1, replica_groups={{0,64,128,192,256,320,384,448},{32,96,160,224,288,352,416,480},{1,65,12..., dimensions={0} | all-to-all | bytes 1114112 | tf_op jit(solution)/shard_map/all_to_all | solution.py:503
  140.1 0.1 shard_map.183
  140.2 13.1 %all_to_all.49.refs_0_ = bf16[8,128,128]{2,1,0:T(8,128)(2,1)S(1)} all-to-all(bf16[8,128,128]{2,1,0:T(8,128)(2,1)S(1)} %shard_map.183), channel_id=1, replica_groups={{0,64,128,192,256,320,384,448},{32,96,160,224,288,352,416,480},{1,65,12..., dimensions={0} | all-to-all | bytes 524288 | tf_op jit(solution)/shard_map/all_to_all | solution.py:503
  153.3 0.0 copy-start.7
  153.3 0.0 copy-start.8
  153.3 0.4 shard_map.185
  153.8 7.5 %collective-permute-start.7 = (bf16[128,448]{1,0:T(8,128)(2,1)S(1)}, bf16[128,448]{1,0:T(8,128)(2,1)S(1)}, u32[]{:S(2)}, u32[]{:S(2)}) collective-permute-start(bf16[128,448]{1,0:T(8,128)(2,1)S(1)} %shard_map.185), channel_id=1, source_target_pairs={{0,32},{32,0},{64,96},{96,64},{128,160},{160,128},{192,224},{224,1... | collective-permute-start | bytes 344072 | tf_op jit(solution)/shard_map/ppermute | solution.py:511
  161.3 0.4 shard_map.184.refs_0_
  161.7 0.5 collective-permute-done.7.refs_1_
  162.2 1.0 shard_map.186
  163.2 5.1 %all-to-all-start.8 = ((bf16[32,8,448]{2,1,0:T(8,128)(2,1)}), bf16[32,8,448]{2,1,0:T(8,128)(2,1)S(1)}, u32[]{:S(2)}, u32[]{:S(2)}) async-start(bf16[32,8,448]{2,1,0:T(8,128)(2,1)} %shard_map.186), calls=%async_computation.8 | async-start | bytes 524288 | tf_op jit(solution)/shard_map/all_to_all | solution.py:503
  168.4 2.6 %collective-permute-start.8 = (bf16[8,448]{1,0:T(8,128)(2,1)S(1)}, bf16[8,448]{1,0:T(8,128)(2,1)S(1)}, u32[]{:S(2)}, u32[]{:S(2)}) collective-permute-start(bf16[8,448]{1,0:T(8,128)(2,1)S(1)} %get-tuple-element.57.refs_2_), channel_id=1, source_target_pairs={{0,32},{32,0},{64,96},{96,64},{128,160},{160,128},{192,224},{224,1... | collective-permute-start | bytes 21512 | tf_op jit(solution)/shard_map/ppermute | solution.py:511
  170.9 0.8 collective-permute-done.8.refs_3_
  171.7 6.3 %all-to-all-done.8.refs_0_ = bf16[32,8,448]{2,1,0:T(8,128)(2,1)S(1)} async-done(((bf16[32,8,448]{2,1,0:T(8,128)(2,1)}), bf16[32,8,448]{2,1,0:T(8,128)(2,1)S(1)}, u32[]{:S(2)}, u32[]{:S(2)}) %all-to-all-start.8) | async-done | bytes 229408 | tf_op jit(solution)/shard_map/all_to_all | solution.py:503
  178.0 0.0 copy-done.7
  178.0 0.0 copy-done.8
  178.0 0.7 shard_map.187
  (2 shorter events, 0.0 us)
Async XLA Ops:
  0.6 18.9 %copy-start.1 = (bf16[1,1024,448]{1,2,0:T(8,128)(2,1)S(1)}, bf16[1,1024,448]{1,2,0:T(8,128)(2,1)}, u32[]{:S(2)}) copy-start(bf16[1,1024,448]{1,2,0:T(8,128)(2,1)} %param.33) | copy-start | bytes 2752516
  0.6 34.1 %copy-start.10 = (s32[2]{0:T(128)S(1)}, s32[2]{0:T(128)}, u32[]{:S(2)}) copy-start(s32[2]{0:T(128)} %param.24) | copy-start | bytes 28
  0.7 34.1 %copy-start.9 = (f32[512]{0:T(512)S(1)}, f32[512]{0:T(512)}, u32[]{:S(2)}) copy-start(f32[512]{0:T(512)} %param.20) | copy-start | bytes 6148
  2.9 25.0 %all-to-all-start = ((bf16[8,304,128]{2,1,0:T(8,128)(2,1)}), bf16[8,304,128]{2,1,0:T(8,128)(2,1)S(1)}, u32[]{:S(2)}, u32[]{:S(2)}) async-start(bf16[8,304,128]{2,1,0:T(8,128)(2,1)} %get-tuple-element.31), calls=%async_computation | async-start | bytes 1245184 | tf_op jit(solution)/shard_map/all_to_all | solution.py:503
  10.5 39.1 %collective-permute-start.4 = (bf16[2,576,768]{2,1,0:T(8,128)(2,1)}, bf16[2,576,768]{2,1,0:T(8,128)(2,1)}, u32[]{:S(2)}, u32[]{:S(2)}) collective-permute-start(bf16[2,576,768]{2,1,0:T(8,128)(2,1)} %bitcast.19), channel_id=1, source_target_pairs={{0,32},{32,0},{64,96},{96,64},{128,160},{160,128},{192,224},{224,1... | collective-permute-start | bytes 5308424 | tf_op jit(solution)/shard_map/ppermute | solution.py:511
  15.2 6.3 %collective-permute-start = (bf16[1,448,1024]{2,1,0:T(8,128)(2,1)}, bf16[1,448,1024]{2,1,0:T(8,128)(2,1)S(1)}, u32[]{:S(2)}, u32[]{:S(2)}) collective-permute-start(bf16[1,448,1024]{2,1,0:T(8,128)(2,1)} %refs_3_.3), channel_id=1, source_target_pairs={{0,32},{32,0},{64,96},{96,64},{128,160},{160,128},{192,224},{224,1... | collective-permute-start | bytes 2752520 | tf_op jit(solution)/shard_map/ppermute | solution.py:511
  17.2 4.7 %collective-permute-start.1 = (bf16[1,448,1024]{2,1,0:T(8,128)(2,1)}, bf16[1,448,1024]{2,1,0:T(8,128)(2,1)S(1)}, u32[]{:S(2)}, u32[]{:S(2)}) collective-permute-start(bf16[1,448,1024]{2,1,0:T(8,128)(2,1)} %refs_4_.6), channel_id=1, source_target_pairs={{0,32},{32,0},{64,96},{96,64},{128,160},{160,128},{192,224},{224,1... | collective-permute-start | bytes 2752520 | tf_op jit(solution)/shard_map/ppermute | solution.py:511
  19.6 4.4 %collective-permute-start.2 = (bf16[1,448,1024]{2,1,0:T(8,128)(2,1)S(1)}, bf16[1,448,1024]{2,1,0:T(8,128)(2,1)S(1)}, u32[]{:S(2)}, u32[]{:S(2)}) collective-permute-start(bf16[1,448,1024]{2,1,0:T(8,128)(2,1)S(1)} %bitcast.9), channel_id=1, source_target_pairs={{0,32},{32,0},{64,96},{96,64},{128,160},{160,128},{192,224},{224,1... | collective-permute-start | bytes 2752520 | tf_op jit(solution)/shard_map/ppermute | solution.py:511
  21.9 1.0 copy-start.2
  27.8 21.8 %copy-start = (bf16[8,304,128]{2,1,0:T(8,128)(2,1)}, bf16[8,304,128]{2,1,0:T(8,128)(2,1)S(1)}, u32[]{:S(2)}) copy-start(bf16[8,304,128]{2,1,0:T(8,128)(2,1)S(1)} %all-to-all-done.refs_3_.refs_1_) | copy-start | bytes 1867780
  27.8 6.9 %collective-permute-start.3 = (bf16[8,304,128]{2,1,0:T(8,128)(2,1)S(1)}, bf16[8,304,128]{2,1,0:T(8,128)(2,1)S(1)}, u32[]{:S(2)}, u32[]{:S(2)}) collective-permute-start(bf16[8,304,128]{2,1,0:T(8,128)(2,1)S(1)} %all-to-all-done.refs_3_.refs_1_), channel_id=1, source_target_pairs={{0,32},{32,0},{64,96},{96,64},{128,160},{160,128},{192,224},{224,1... | collective-permute-start | bytes 1867784 | tf_op jit(solution)/shard_map/ppermute | solution.py:511
  35.8 0.8 copy-start.4
  36.6 22.3 %all-to-all-start.1 = ((bf16[32,8,384]{2,1,0:T(8,128)(2,1)}), bf16[32,8,384]{2,1,0:T(8,128)(2,1)}, u32[]{:S(2)}, u32[]{:S(2)}) async-start(bf16[32,8,384]{2,1,0:T(8,128)(2,1)} %shard_map.177), calls=%async_computation.1 | async-start | bytes 393216 | tf_op jit(solution)/shard_map/all_to_all | solution.py:503
  49.6 17.6 %copy-start.6 = (f32[64,128]{1,0:T(8,128)S(1)}, f32[64,128]{1,0:T(8,128)}, u32[]{:S(2)}) copy-start(f32[64,128]{1,0:T(8,128)} %get-tuple-element.47.refs_1_) | copy-start | bytes 98308
  56.3 34.5 %copy-start.5 = (bf16[512,448]{0,1:T(8,128)(2,1)S(1)}, bf16[512,448]{0,1:T(8,128)(2,1)}, u32[]{:S(2)}) copy-start(bf16[512,448]{0,1:T(8,128)(2,1)} %param.27) | copy-start | bytes 1376260
  59.0 21.1 %collective-permute-start.5 = (bf16[448,512]{1,0:T(8,128)(2,1)}, bf16[448,512]{1,0:T(8,128)(2,1)}, u32[]{:S(2)}, u32[]{:S(2)}) collective-permute-start(bf16[448,512]{1,0:T(8,128)(2,1)} %bitcast.11), channel_id=1, source_target_pairs={{0,32},{32,0},{64,96},{96,64},{128,160},{160,128},{192,224},{224,1... | collective-permute-start | bytes 1376264 | tf_op jit(solution)/shard_map/ppermute | solution.py:511
  63.8 13.6 %all-to-all-start.2 = ((bf16[8,16,640]{2,1,0:T(8,128)(2,1)}), bf16[8,16,640]{2,1,0:T(8,128)(2,1)S(1)}, u32[]{:S(2)}, u32[]{:S(2)}) async-start(bf16[8,16,640]{2,1,0:T(8,128)(2,1)} %bitcast.8), calls=%async_computation.2 | async-start | bytes 327680 | tf_op jit(solution)/shard_map/all_to_all | solution.py:503
  67.2 12.9 %collective-permute-start.6 = (f32[64,128]{1,0:T(8,128)S(1)}, f32[64,128]{1,0:T(8,128)S(1)}, u32[]{:S(2)}, u32[]{:S(2)}) collective-permute-start(f32[64,128]{1,0:T(8,128)S(1)} %copy-done.6), channel_id=1, source_target_pairs={{0,32},{32,0},{64,96},{96,64},{128,160},{160,128},{192,224},{224,1... | collective-permute-start | bytes 98312 | tf_op jit(solution)/shard_map/ppermute | solution.py:511
  77.4 44.0 %copy-start.3 = (bf16[1,448,1024]{2,1,0:T(8,128)(2,1)S(1)}, bf16[1,448,1024]{2,1,0:T(8,128)(2,1)}, u32[]{:S(2)}) copy-start(bf16[1,448,1024]{2,1,0:T(8,128)(2,1)} %copy-done.2) | copy-start | bytes 2752516
  153.3 24.7 %copy-start.7 = (s32[8,8]{1,0:T(8,128)S(1)}, s32[8,8]{1,0:T(8,128)}, u32[]{:S(2)}) copy-start(s32[8,8]{1,0:T(8,128)} %refs_4_.7) | copy-start | bytes 772
  153.3 24.7 %copy-start.8 = (f32[8,8]{1,0:T(8,128)S(1)}, f32[8,8]{1,0:T(8,128)}, u32[]{:S(2)}) copy-start(f32[8,8]{1,0:T(8,128)} %refs_5_.1) | copy-start | bytes 772
  153.8 8.5 %collective-permute-start.7 = (bf16[128,448]{1,0:T(8,128)(2,1)S(1)}, bf16[128,448]{1,0:T(8,128)(2,1)S(1)}, u32[]{:S(2)}, u32[]{:S(2)}) collective-permute-start(bf16[128,448]{1,0:T(8,128)(2,1)S(1)} %shard_map.185), channel_id=1, source_target_pairs={{0,32},{32,0},{64,96},{96,64},{128,160},{160,128},{192,224},{224,1... | collective-permute-start | bytes 344072 | tf_op jit(solution)/shard_map/ppermute | solution.py:511
  163.2 14.8 %all-to-all-start.8 = ((bf16[32,8,448]{2,1,0:T(8,128)(2,1)}), bf16[32,8,448]{2,1,0:T(8,128)(2,1)S(1)}, u32[]{:S(2)}, u32[]{:S(2)}) async-start(bf16[32,8,448]{2,1,0:T(8,128)(2,1)} %shard_map.186), calls=%async_computation.8 | async-start | bytes 524288 | tf_op jit(solution)/shard_map/all_to_all | solution.py:503
  168.4 3.4 %collective-permute-start.8 = (bf16[8,448]{1,0:T(8,128)(2,1)S(1)}, bf16[8,448]{1,0:T(8,128)(2,1)S(1)}, u32[]{:S(2)}, u32[]{:S(2)}) collective-permute-start(bf16[8,448]{1,0:T(8,128)(2,1)S(1)} %get-tuple-element.57.refs_2_), channel_id=1, source_target_pairs={{0,32},{32,0},{64,96},{96,64},{128,160},{160,128},{192,224},{224,1... | collective-permute-start | bytes 21512 | tf_op jit(solution)/shard_map/ppermute | solution.py:511

commit v6 on v5

--- a/solution.py
+++ b/solution.py
@@ -34,8 +34,7 @@
 UP_ROWS = 2 * HEADS_DEV * LAT_KV
 FRESH_W = KEY + ROPE
 FRESH_ROWS = 48
-TOKEN_AT = 0
-GAIN_AT = TOKEN_AT + 4 * ROWS_TP
+LENT_ROWS = 4 * ROWS_TP
 CLASS = TOKROWS // 2
 PART_ROWS = 2 * CLASS + 16
 KEY_W = 384
@@ -92,20 +91,19 @@
     return pltpu.roll(rows, 4, 0)
 
 
-def in_tiles(rows):
-    rows = jnp.concatenate([rows, jnp.zeros((ROWS_TP, 512 - FEAT), F32)], axis=1)
-    return [rows[:, at * 128 : (at + 1) * 128] for at in range(4)]
-
-
-def from_tiles(tiles):
-    return jnp.concatenate([tiles[at * ROWS_TP : (at + 1) * ROWS_TP] for at in range(4)], axis=1)[:, :FEAT]
-
-
-def start_kernel(tokens_ref, gain_ref, down_ref, key_ref, value_ref, mlp_gain_ref, out_ref, mine_ref):
+def start_kernel(
+    tokens_ref, gain_ref, down_ref, key_ref, value_ref, mlp_gain_ref, project_hbm, out_ref, lent_hbm, lent_ref, sems,
+):
+    fetch = pltpu.make_async_copy(project_hbm, lent_ref.at[pl.ds(0, FEAT), :], sems.at[0])
+    fetch.start()
     wide_tokens = tokens_ref[...].astype(F32)
-    mine_ref[...] = jnp.concatenate(
-        in_tiles(wide_tokens) + in_tiles(jnp.broadcast_to(mlp_gain_ref[...], (ROWS_TP, FEAT))), axis=0
-    )
+    mlp_gain = jnp.broadcast_to(mlp_gain_ref[...], (ROWS_TP, FEAT))
+    rows = jnp.concatenate([wide_tokens, *parts_of(mlp_gain)], axis=0)
+    rows = jnp.concatenate([rows, jnp.zeros((LENT_ROWS, 512 - FEAT), F32)], axis=1)
+    lent_ref[FEAT:, :] = rows.astype(BF16)
+    fetch.wait()
+    leave = pltpu.make_async_copy(lent_ref, lent_hbm, sems.at[1])
+    leave.start()
     normed = (wide_tokens * gain_ref[...]).astype(BF16)
     fresh = dot(normed, down_ref[...])
     fresh = jnp.concatenate([fresh, jnp.zeros((ROWS_TP, ROPE), F32)], axis=1)
@@ -117,6 +115,7 @@
             out_ref[place, head * LAT_KV : (head + 1) * LAT_KV, :] = key_ref[head]
             out_ref[place, UP_ROWS // 2 + head * LAT_KV : UP_ROWS // 2 + (head + 1) * LAT_KV, :] = value_ref[head]
         out_ref[place, UP_ROWS:, :] = packed
+    leave.wait()
 
 
 def fresh_kernel(gain_ref, lengths_ref, freq_ref, own_hbm, other_hbm, out_hbm, own_ref, other_ref, out_ref, sems):
@@ -287,16 +286,18 @@
     own = (match & own_half(shape, 0)).astype(F32).astype(BF16)
     other = (match & ~own_half(shape, 0)).astype(F32).astype(BF16)
     out = dot(dot(own, values).astype(BF16), own_ref[...], NT)
-    out = out + dot(dot(other, values).astype(BF16), other_ref[...], NT)
+    out = out + dot(dot(other, values).astype(BF16), other_ref[:FEAT, :], NT)
     out_ref[...] = out.reshape(N_TP, ROWS_TP, FEAT).astype(BF16)
 
 
-def route_kernel(parts_ref, mine_ref, other_ref, attended_ref, out_ref):
+def route_kernel(parts_ref, tokens_ref, gain_ref, lent_ref, attended_ref, out_ref):
     attended = jnp.sum(parts_ref[...].astype(F32), axis=0).astype(BF16)
     attended_ref[...] = attended
     own = own_half((ROWS_TP, FEAT), 0)
-    tokens = jnp.where(own, from_tiles(mine_ref[TOKEN_AT:, :]), swap_halves(from_tiles(other_ref[TOKEN_AT:, :])))
-    gain = jnp.where(own, from_tiles(mine_ref[GAIN_AT:, :]), from_tiles(other_ref[GAIN_AT:, :]))
+    lent = lent_ref[FEAT:, :].astype(F32)[:, :FEAT]
+    tokens = jnp.where(own, tokens_ref[...].astype(F32), swap_halves(lent[:ROWS_TP]))
+    gain = lent[ROWS_TP : 2 * ROWS_TP] + lent[2 * ROWS_TP : 3 * ROWS_TP] + lent[3 * ROWS_TP :]
+    gain = jnp.where(own, gain_ref[...], gain)
     mid = tokens + attended.astype(F32)
     lane = iota((ROWS_TP, 512 - FEAT), 1)
     extra = jnp.zeros(lane.shape, F32)
@@ -369,11 +370,11 @@
     out_ref[...] = out.reshape(N_TP, ROWS_TP, FEAT).astype(BF16)
 
 
-def mix_kernel(parts_ref, mine_ref, own_ref, other_ref, ids_ref, weights_ref, attended_ref, out_ref):
+def mix_kernel(parts_ref, tokens_ref, own_ref, other_ref, ids_ref, weights_ref, attended_ref, out_ref):
     own = own_ref[...].astype(F32)
     attended = jnp.where(own_half(own.shape, 0), own, swap_halves(other_ref[...].astype(F32)))
     attended_ref[...] = attended.astype(BF16)
-    total = from_tiles(mine_ref[TOKEN_AT:, :]) + attended
+    total = tokens_ref[...].astype(F32) + attended
     ids = ids_ref[...]
     weights = weights_ref[...]
     for expert in range(EXPERTS):
@@ -413,11 +414,12 @@
     return jax.ShapeDtypeStruct(shape, dtype)
 
 
-def start(tokens, attn_gain, down_kv, key_up, value_up, mlp_gain):
+def start(tokens, attn_gain, down_kv, key_up, value_up, mlp_gain, project_weights):
     return run(
-        start_kernel, [shaped(CHIPS, UP_ROWS + FRESH_ROWS, 128), shaped(8 * ROWS_TP, 128, dtype=F32)],
-        tokens, attn_gain.reshape(1, FEAT), down_kv, jnp.swapaxes(key_up, 1, 2), value_up,
-        mlp_gain.reshape(1, FEAT), limit=60,
+        start_kernel, [shaped(CHIPS, UP_ROWS + FRESH_ROWS, 128), shaped(FEAT + LENT_ROWS, 512)],
+        tokens, attn_gain.reshape(1, FEAT), down_kv, jnp.swapaxes(key_up, 1, 2), value_up, mlp_gain.reshape(1, FEAT),
+        fetched=(in_hbm(project_weights),), left=1, limit=60,
+        scratch=[pltpu.VMEM((FEAT + LENT_ROWS, 512), BF16), pltpu.SemaphoreType.DMA((2,))],
     )
 
 
@@ -470,8 +472,9 @@
     return run(project_kernel, shaped(N_TP, ROWS_TP, FEAT), values, own, other)
 
 
-def route(parts, mine, other):
-    return run(route_kernel, [shaped(ROWS_TP, FEAT), shaped(N_TP, ROWS_TP, 512)], parts, mine, other)
+def route(parts, tokens, mlp_gain, lent):
+    outs = [shaped(ROWS_TP, FEAT), shaped(N_TP, ROWS_TP, 512)]
+    return run(route_kernel, outs, parts, tokens, mlp_gain.reshape(1, FEAT), lent)
 
 
 def gate(rows, own_gate, own_up, other_gate, other_up):
@@ -494,9 +497,9 @@
     return run(join_kernel, shaped(N_TP, ROWS_TP, FEAT), own, came)
 
 
-def mix(parts, mine, own, other, expert_ids, expert_weights):
+def mix(parts, tokens, own, other, expert_ids, expert_weights):
     outs = [shaped(ROWS_TP, FEAT), shaped(ROWS_TP, FEAT)]
-    return run(mix_kernel, outs, parts, mine, own, other, expert_ids, expert_weights)
+    return run(mix_kernel, outs, parts, tokens, own, other, expert_ids, expert_weights)
 
 
 def exchange(array, axis, groups=None):
@@ -515,26 +518,23 @@
     tokens, attn_gain, down_kv, latent_gain, query_nope, query_rope, cache, lengths, key_up, value_up,
     out_proj, mlp_gain, expert_ids, expert_weights, gate_proj, up_proj, down_proj,
 ):
-    ups, mine = start(tokens, attn_gain, down_kv, key_up, value_up, mlp_gain)
     own_cache, own_out, own_down = jnp.swapaxes(cache, 1, 2), out_proj.T, jnp.swapaxes(down_proj, 1, 2)
-    ups, waiting, *moved = lax.optimization_barrier((ups, own_cache, gate_proj, up_proj, own_down))
+    ups, lent = start(tokens, attn_gain, down_kv, key_up, value_up, mlp_gain, own_out)
+    ups, waiting, *moved = lax.optimization_barrier((ups, own_cache, lent, gate_proj, up_proj, own_down))
     own = along_y(ups)
     other_cache = other_core(waiting)
     moved = [other_core(array) for array in moved]
-    own, other_gate, other_up, other_down = lax.optimization_barrier((own, *moved))
+    own, lent, other_gate, other_up, other_down = lax.optimization_barrier((own, *moved))
     other = other_core(own)
     keys = fresh(own, other, latent_gain, lengths)
     keys, own, other = lax.optimization_barrier((keys, own, other))
     keys = exchange(keys, "tp")
     parts, queries, values = attend(lengths, own, other, query_nope, query_rope, own_cache, other_cache)
-    parts, keys, *moved = lax.optimization_barrier((parts, keys, own_out, mine))
-    other_out, other_mine = (other_core(array) for array in moved)
+    parts, keys = lax.optimization_barrier((parts, keys))
     parts = along_y(parts.reshape(CHIPS, ROWS_KV, ATT_W))
-    values = combine(parts, queries, values, keys)
-    values, other_out, other_mine = lax.optimization_barrier((values, other_out, other_mine))
-    values = along_y(values)
-    parts = exchange(project(values, own_out, other_out), "tp")
-    attended, rows = route(parts, mine, other_mine)
+    values = along_y(combine(parts, queries, values, keys))
+    parts = exchange(project(values, own_out, lent), "tp")
+    attended, rows = route(parts, tokens, mlp_gain, lent)
     rows = exchange(rows, "tp")
     parts = along_y(gate(rows, gate_proj, up_proj, other_gate, other_up))
     packed = along_y(hidden(parts))
@@ -542,7 +542,7 @@
     parts, leaving = lax.optimization_barrier((join(down(packed, own_down), came), attended))
     other_attended = other_core(leaving)
     parts = exchange(parts, "tp")
-    return mix(parts, mine, attended, other_attended, expert_ids, expert_weights)
+    return mix(parts, tokens, attended, other_attended, expert_ids, expert_weights)
 
 
 def solution(mesh):

time: 181 us -> 173 us (0.956)
  waiting for transfers between devices: 25.6 us -> 14.6 us
  blocking collectives: 68.9 us -> 77.4 us
  starting transfers between devices: 62 us -> 56.3 us
    all_to_all x4 -> x3, waiting for transfers between devices: 21.1 us -> 9.99 us  [exchange(): lax.all_to_all(array, axis, split_axis=0, concat_axis=0, axis_index_group...]
    all_to_all x5 -> x6, blocking collectives: 68.9 us -> 77.4 us  [exchange(): lax.all_to_all(array, axis, split_axis=0, concat_axis=0, axis_index_group...]
    all_to_all x4 -> x3, starting transfers between devices: 29.1 us -> 24.9 us  [exchange(): lax.all_to_all(array, axis, split_axis=0, concat_axis=0, axis_index_group...]
    ppermute x9 -> x8, starting transfers between devices: 32.9 us -> 31.4 us  [other_core(): lax.ppermute(array, 'kv', [(index, index ^ 1) for index in range(N_KV)])]
    ppermute x9 -> x8, waiting for transfers between devices: 4.45 us -> 4.66 us  [other_core(): lax.ppermute(array, 'kv', [(index, index ^ 1) for index in range(N_KV)])]
  transfers between devices with their start and end apart: 13 -> 11, of which waited for: 9 -> 7; matrix products, arithmetic and copies ran while one was open for 0% -> 0% of each run, Pallas kernels for 6% -> 4%
where the time goes in v6:
time: 173 us; the launch traced here: 170 us
  blocking collectives  77.4 us (45%)
  starting transfers between devices  56.3 us (33%)
  Pallas kernels  18.5 us (11%)
  waiting for transfers between devices  14.6 us (8%)
  local copies, waits for them, and re-layouts  2.75 us (2%)
    all_to_all x6, blocking collectives, exchange(): lax.all_to_all(array, axis, split_axis=0, concat_axis=0, axis_index_group...  77.4 us
    ppermute x8, starting transfers between devices, other_core(): lax.ppermute(array, 'kv', [(index, index ^ 1) for index in range(N_KV)])  31.4 us
    all_to_all x3, starting transfers between devices, exchange(): lax.all_to_all(array, axis, split_axis=0, concat_axis=0, axis_index_group...  24.9 us
    pallas_call x12, Pallas kernels, run(): pl.pallas_call(body, out_shape=outs[0] if single else tuple(outs), in_spe...  18.5 us
    all_to_all x3, waiting for transfers between devices, exchange(): lax.all_to_all(array, axis, split_axis=0, concat_axis=0, axis_index_group...  9.99 us
    ppermute x8, waiting for transfers between devices, other_core(): lax.ppermute(array, 'kv', [(index, index ^ 1) for index in range(N_KV)])  4.66 us
  transfers between devices with their start and end apart: 11, of which 7 were waited for; matrix products, arithmetic and copies ran while one was open for 0% of the time, Pallas kernels for 4%

profile of v6, /device:TPU:1, one launch (start us, length us, event | category | flops | bytes accessed | tf_op | source)
XLA Modules:
  0.0 170.4 jit_solution(7847521313663200935)
XLA Ops:
  0.6 0.0 copy-start.2
  0.6 0.0 copy-start.13
  0.7 0.0 copy-start.12
  0.7 3.9 %shard_map.176 = (bf16[8,304,128]{2,1,0:T(8,128)(2,1)}, bf16[480,512]{1,0:T(8,128)(2,1)}) custom-call(bf16[8,448]{1,0:T(8,128)(2,1)} %refs_1_.3, f32[1,448]{1,0:T(1,128)} %bitcast.20, bf16[448,576]{1,0:T(8,128)(2,1)} %refs_2_.1, bf16[4,32,128]{2,1,0:T(8,128)(2,1)} %bitcast.19, bf16[4,32,128]{2,1,0:T(8,128)(2,1)} %refs_4_.4, f32[1,448]{1,0:T(1,128)} %bitcast.14, ...), custom_call_target="tpu_custom_call" | custom-call | tf_op jit(solution)/shard_map/pallas_call | solution.py:398
  4.5 7.7 %all-to-all-start = ((bf16[8,304,128]{2,1,0:T(8,128)(2,1)}), bf16[8,304,128]{2,1,0:T(8,128)(2,1)S(1)}, u32[]{:S(2)}, u32[]{:S(2)}) async-start(bf16[8,304,128]{2,1,0:T(8,128)(2,1)} %get-tuple-element.29), calls=%async_computation | async-start | bytes 1245184 | tf_op jit(solution)/shard_map/all_to_all | solution.py:506
  12.2 4.7 %collective-permute-start.5 = (bf16[2,576,768]{2,1,0:T(8,128)(2,1)}, bf16[2,576,768]{2,1,0:T(8,128)(2,1)}, u32[]{:S(2)}, u32[]{:S(2)}) collective-permute-start(bf16[2,576,768]{2,1,0:T(8,128)(2,1)} %bitcast.21), channel_id=1, source_target_pairs={{0,32},{32,0},{64,96},{96,64},{128,160},{160,128},{192,224},{224,1... | collective-permute-start | bytes 5308424 | tf_op jit(solution)/shard_map/ppermute | solution.py:514
  16.9 1.9 %collective-permute-start.1 = (bf16[1,448,1024]{2,1,0:T(8,128)(2,1)}, bf16[1,448,1024]{2,1,0:T(8,128)(2,1)S(1)}, u32[]{:S(2)}, u32[]{:S(2)}) collective-permute-start(bf16[1,448,1024]{2,1,0:T(8,128)(2,1)} %refs_3_.3), channel_id=1, source_target_pairs={{0,32},{32,0},{64,96},{96,64},{128,160},{160,128},{192,224},{224,1... | collective-permute-start | bytes 2752520 | tf_op jit(solution)/shard_map/ppermute | solution.py:514
  18.8 2.4 %collective-permute-start.2 = (bf16[1,448,1024]{2,1,0:T(8,128)(2,1)}, bf16[1,448,1024]{2,1,0:T(8,128)(2,1)S(1)}, u32[]{:S(2)}, u32[]{:S(2)}) collective-permute-start(bf16[1,448,1024]{2,1,0:T(8,128)(2,1)} %refs_4_.6), channel_id=1, source_target_pairs={{0,32},{32,0},{64,96},{96,64},{128,160},{160,128},{192,224},{224,1... | collective-permute-start | bytes 2752520 | tf_op jit(solution)/shard_map/ppermute | solution.py:514
  21.2 0.0 copy-done.2
  21.2 1.9 %collective-permute-start.3 = (bf16[1,448,1024]{2,1,0:T(8,128)(2,1)S(1)}, bf16[1,448,1024]{2,1,0:T(8,128)(2,1)S(1)}, u32[]{:S(2)}, u32[]{:S(2)}) collective-permute-start(bf16[1,448,1024]{2,1,0:T(8,128)(2,1)S(1)} %bitcast.11), channel_id=1, source_target_pairs={{0,32},{32,0},{64,96},{96,64},{128,160},{160,128},{192,224},{224,1... | collective-permute-start | bytes 2752520 | tf_op jit(solution)/shard_map/ppermute | solution.py:514
  23.2 2.4 %collective-permute-start = (bf16[480,512]{1,0:T(8,128)(2,1)}, bf16[480,512]{1,0:T(8,128)(2,1)S(1)}, u32[]{:S(2)}, u32[]{:S(2)}) collective-permute-start(bf16[480,512]{1,0:T(8,128)(2,1)} %get-tuple-element.30), channel_id=1, source_target_pairs={{0,32},{32,0},{64,96},{96,64},{128,160},{160,128},{192,224},{224,1... | collective-permute-start | bytes 1474568 | tf_op jit(solution)/shard_map/ppermute | solution.py:514
  25.6 1.7 collective-permute-done.refs_2_.refs_3_
  27.3 0.0 collective-permute-done.1.refs_1_
  27.3 0.0 copy-start.3
  27.3 1.0 copy-done.3
  28.2 0.0 collective-permute-done.2.refs_2_
  28.2 0.0 copy-start.5
  28.2 0.9 copy-done.5
  29.1 0.0 collective-permute-done.3.refs_1_
  29.2 0.3 all-to-all-done.refs_3_.refs_1_
  29.5 0.0 copy-start
  29.5 5.2 %collective-permute-start.4 = (bf16[8,304,128]{2,1,0:T(8,128)(2,1)S(1)}, bf16[8,304,128]{2,1,0:T(8,128)(2,1)S(1)}, u32[]{:S(2)}, u32[]{:S(2)}) collective-permute-start(bf16[8,304,128]{2,1,0:T(8,128)(2,1)S(1)} %all-to-all-done.refs_3_.refs_1_), channel_id=1, source_target_pairs={{0,32},{32,0},{64,96},{96,64},{128,160},{160,128},{192,224},{224,1... | collective-permute-start | bytes 1867784 | tf_op jit(solution)/shard_map/ppermute | solution.py:514
  34.7 1.6 collective-permute-done.4.refs_4_.refs_2_
  36.4 0.0 copy-done.13
  36.4 0.0 copy-done.12
  36.4 1.1 shard_map.177
  37.4 0.0 copy-start.7
  37.4 0.8 copy-done.7
  38.3 12.8 %all-to-all-start.1 = ((bf16[32,8,384]{2,1,0:T(8,128)(2,1)}), bf16[32,8,384]{2,1,0:T(8,128)(2,1)S(1)}, u32[]{:S(2)}, u32[]{:S(2)}) async-start(bf16[32,8,384]{2,1,0:T(8,128)(2,1)} %shard_map.177), calls=%async_computation.1 | async-start | bytes 393216 | tf_op jit(solution)/shard_map/all_to_all | solution.py:506
  51.1 0.0 collective-permute-done.5.refs_6_
  51.1 0.0 copy-done
  51.1 6.0 %shard_map.178 = (bf16[128,640]{1,0:T(8,128)(2,1)S(1)}, bf16[64,576]{1,0:T(8,128)(2,1)}, bf16[4,8,2,32,128]{4,3,2,1,0:T(8,128)(2,1)}) custom-call(s32[1,2]{1,0:T(1,128)S(1)} %bitcast.18, bf16[8,304,128]{2,1,0:T(8,128)(2,1)} %copy-done, bf16[8,304,128]{2,1,0:T(8,128)(2,1)} %copy-done.7, bf16[256,512]{1,0:T(8,128)(2,1)} %refs_3_.2, bf16[256,256]{1,0:T(8,128)(2,1)} %refs_4_.5, ...), custom_call_target="tpu_custom_call" | custom-call | flops 2200000000 | bytes 4000000 | tf_op jit(solution)/shard_map/pallas_call | solution.py:398
  57.2 0.0 copy-start.1
  57.2 3.3 %all-to-all-done.1.refs_1_ = bf16[32,8,384]{2,1,0:T(8,128)(2,1)S(1)} async-done(((bf16[32,8,384]{2,1,0:T(8,128)(2,1)}), bf16[32,8,384]{2,1,0:T(8,128)(2,1)S(1)}, u32[]{:S(2)}, u32[]{:S(2)}) %all-to-all-start.1) | async-done | bytes 196640 | tf_op jit(solution)/shard_map/all_to_all | solution.py:506
  60.5 10.8 %all_to_all.45.refs_0_ = bf16[8,16,640]{2,1,0:T(8,128)(2,1)S(1)} all-to-all(bf16[8,16,640]{2,1,0:T(8,128)(2,1)S(1)} %bitcast.13), channel_id=1, replica_groups={{0,64,128,192,256,320,384,448},{32,96,160,224,288,352,416,480},{1,65,12..., dimensions={0} | all-to-all | bytes 327680 | tf_op jit(solution)/shard_map/all_to_all | solution.py:506
  71.3 1.7 shard_map.179
  73.0 0.0 copy-start.4
  73.0 0.0 copy-start.6
  73.0 10.4 %all_to_all.46.refs_0_ = bf16[8,16,512]{2,1,0:T(8,128)(2,1)S(1)} all-to-all(bf16[8,16,512]{2,1,0:T(8,128)(2,1)S(1)} %shard_map.179), channel_id=1, replica_groups={{0,64,128,192,256,320,384,448},{32,96,160,224,288,352,416,480},{1,65,12..., dimensions={0} | all-to-all | bytes 262144 | tf_op jit(solution)/shard_map/all_to_all | solution.py:506
  83.4 0.0 copy-done.1
  83.5 0.7 shard_map.180
  84.1 15.5 %all_to_all.47.refs_0_ = bf16[32,8,448]{2,1,0:T(8,128)(2,1)S(1)} all-to-all(bf16[32,8,448]{2,1,0:T(8,128)(2,1)S(1)} %shard_map.180), channel_id=1, replica_groups=mesh['kv'=16,'tp'=32] {'tp'}, dimensions={0} | all-to-all | bytes 458752 | tf_op jit(solution)/shard_map/all_to_all | solution.py:506
  99.6 0.0 copy-done.8
  99.6 0.0 copy-done.9
  99.6 0.2 shard_map.181
  99.8 14.1 %all_to_all.48.refs_0_ = bf16[32,8,512]{2,1,0:T(8,128)(2,1)S(1)} all-to-all(bf16[32,8,512]{2,1,0:T(8,128)(2,1)S(1)} %get-tuple-element.45), channel_id=1, replica_groups=mesh['kv'=16,'tp'=32] {'tp'}, dimensions={0} | all-to-all | bytes 524288 | tf_op jit(solution)/shard_map/all_to_all | solution.py:506
  113.9 0.0 copy-done.4
  113.9 0.0 copy-done.6
  113.9 2.3 %shard_map.182 = bf16[8,272,128]{2,1,0:T(8,128)(2,1)S(1)} custom-call(bf16[32,8,512]{2,1,0:T(8,128)(2,1)S(1)} %all_to_all.48.refs_0_, bf16[1,448,1024]{2,1,0:T(8,128)(2,1)S(1)} %copy-done.4, bf16[1,448,1024]{2,1,0:T(8,128)(2,1)S(1)} %copy-done.6, bf16[1,448,1024]{2,1,0:T(8,128)(2,1)} %refs_3_.3, bf16[1,448,1024]{2,1,0:T(8,128)(2,1)} %refs_4_.6), custom_call_target="tpu_custom_call" | custom-call | tf_op jit(solution)/shard_map/pallas_call | solution.py:398
  116.2 14.9 %all_to_all.49.refs_0_ = bf16[8,272,128]{2,1,0:T(8,128)(2,1)S(1)} all-to-all(bf16[8,272,128]{2,1,0:T(8,128)(2,1)S(1)} %shard_map.182), channel_id=1, replica_groups={{0,64,128,192,256,320,384,448},{32,96,160,224,288,352,416,480},{1,65,12..., dimensions={0} | all-to-all | bytes 1114112 | tf_op jit(solution)/shard_map/all_to_all | solution.py:506
  131.1 0.1 shard_map.183
  131.2 11.7 %all_to_all.50.refs_0_ = bf16[8,128,128]{2,1,0:T(8,128)(2,1)S(1)} all-to-all(bf16[8,128,128]{2,1,0:T(8,128)(2,1)S(1)} %shard_map.183), channel_id=1, replica_groups={{0,64,128,192,256,320,384,448},{32,96,160,224,288,352,416,480},{1,65,12..., dimensions={0} | all-to-all | bytes 524288 | tf_op jit(solution)/shard_map/all_to_all | solution.py:506
  143.0 0.4 shard_map.185
  143.4 10.3 %collective-permute-start.6 = (bf16[128,448]{1,0:T(8,128)(2,1)S(1)}, bf16[128,448]{1,0:T(8,128)(2,1)S(1)}, u32[]{:S(2)}, u32[]{:S(2)}) collective-permute-start(bf16[128,448]{1,0:T(8,128)(2,1)S(1)} %shard_map.185), channel_id=1, source_target_pairs={{0,32},{32,0},{64,96},{96,64},{128,160},{160,128},{192,224},{224,1... | collective-permute-start | bytes 344072 | tf_op jit(solution)/shard_map/ppermute | solution.py:514
  153.7 0.4 shard_map.184.refs_0_
  154.1 0.5 collective-permute-done.6.refs_1_
  154.7 1.0 shard_map.186
  155.7 4.4 %all-to-all-start.8 = ((bf16[32,8,448]{2,1,0:T(8,128)(2,1)}), bf16[32,8,448]{2,1,0:T(8,128)(2,1)S(1)}, u32[]{:S(2)}, u32[]{:S(2)}) async-start(bf16[32,8,448]{2,1,0:T(8,128)(2,1)} %shard_map.186), calls=%async_computation.8 | async-start | bytes 524288 | tf_op jit(solution)/shard_map/all_to_all | solution.py:506
  160.0 2.6 %collective-permute-start.7 = (bf16[8,448]{1,0:T(8,128)(2,1)S(1)}, bf16[8,448]{1,0:T(8,128)(2,1)S(1)}, u32[]{:S(2)}, u32[]{:S(2)}) collective-permute-start(bf16[8,448]{1,0:T(8,128)(2,1)S(1)} %get-tuple-element.51.refs_2_), channel_id=1, source_target_pairs={{0,32},{32,0},{64,96},{96,64},{128,160},{160,128},{192,224},{224,1... | collective-permute-start | bytes 21512 | tf_op jit(solution)/shard_map/ppermute | solution.py:514
  162.6 0.8 collective-permute-done.7.refs_3_
  163.4 6.3 %all-to-all-done.8.refs_0_ = bf16[32,8,448]{2,1,0:T(8,128)(2,1)S(1)} async-done(((bf16[32,8,448]{2,1,0:T(8,128)(2,1)}), bf16[32,8,448]{2,1,0:T(8,128)(2,1)S(1)}, u32[]{:S(2)}, u32[]{:S(2)}) %all-to-all-start.8) | async-done | bytes 229408 | tf_op jit(solution)/shard_map/all_to_all | solution.py:506
  169.7 0.0 copy-done.10
  169.7 0.0 copy-done.11
  169.7 0.7 shard_map.187
  (5 shorter events, 0.0 us)
Async XLA Ops:
  0.6 20.6 %copy-start.2 = (bf16[1,1024,448]{1,2,0:T(8,128)(2,1)S(1)}, bf16[1,1024,448]{1,2,0:T(8,128)(2,1)}, u32[]{:S(2)}) copy-start(bf16[1,1024,448]{1,2,0:T(8,128)(2,1)} %param.33) | copy-start | bytes 2752516
  0.6 35.7 %copy-start.13 = (s32[2]{0:T(128)S(1)}, s32[2]{0:T(128)}, u32[]{:S(2)}) copy-start(s32[2]{0:T(128)} %param.24) | copy-start | bytes 28
  0.7 35.7 %copy-start.12 = (f32[512]{0:T(512)S(1)}, f32[512]{0:T(512)}, u32[]{:S(2)}) copy-start(f32[512]{0:T(512)} %param.20) | copy-start | bytes 6148
  4.5 25.0 %all-to-all-start = ((bf16[8,304,128]{2,1,0:T(8,128)(2,1)}), bf16[8,304,128]{2,1,0:T(8,128)(2,1)S(1)}, u32[]{:S(2)}, u32[]{:S(2)}) async-start(bf16[8,304,128]{2,1,0:T(8,128)(2,1)} %get-tuple-element.29), calls=%async_computation | async-start | bytes 1245184 | tf_op jit(solution)/shard_map/all_to_all | solution.py:506
  12.2 38.9 %collective-permute-start.5 = (bf16[2,576,768]{2,1,0:T(8,128)(2,1)}, bf16[2,576,768]{2,1,0:T(8,128)(2,1)}, u32[]{:S(2)}, u32[]{:S(2)}) collective-permute-start(bf16[2,576,768]{2,1,0:T(8,128)(2,1)} %bitcast.21), channel_id=1, source_target_pairs={{0,32},{32,0},{64,96},{96,64},{128,160},{160,128},{192,224},{224,1... | collective-permute-start | bytes 5308424 | tf_op jit(solution)/shard_map/ppermute | solution.py:514
  16.9 10.4 %collective-permute-start.1 = (bf16[1,448,1024]{2,1,0:T(8,128)(2,1)}, bf16[1,448,1024]{2,1,0:T(8,128)(2,1)S(1)}, u32[]{:S(2)}, u32[]{:S(2)}) collective-permute-start(bf16[1,448,1024]{2,1,0:T(8,128)(2,1)} %refs_3_.3), channel_id=1, source_target_pairs={{0,32},{32,0},{64,96},{96,64},{128,160},{160,128},{192,224},{224,1... | collective-permute-start | bytes 2752520 | tf_op jit(solution)/shard_map/ppermute | solution.py:514
  18.8 9.4 %collective-permute-start.2 = (bf16[1,448,1024]{2,1,0:T(8,128)(2,1)}, bf16[1,448,1024]{2,1,0:T(8,128)(2,1)S(1)}, u32[]{:S(2)}, u32[]{:S(2)}) collective-permute-start(bf16[1,448,1024]{2,1,0:T(8,128)(2,1)} %refs_4_.6), channel_id=1, source_target_pairs={{0,32},{32,0},{64,96},{96,64},{128,160},{160,128},{192,224},{224,1... | collective-permute-start | bytes 2752520 | tf_op jit(solution)/shard_map/ppermute | solution.py:514
  21.2 7.9 %collective-permute-start.3 = (bf16[1,448,1024]{2,1,0:T(8,128)(2,1)S(1)}, bf16[1,448,1024]{2,1,0:T(8,128)(2,1)S(1)}, u32[]{:S(2)}, u32[]{:S(2)}) collective-permute-start(bf16[1,448,1024]{2,1,0:T(8,128)(2,1)S(1)} %bitcast.11), channel_id=1, source_target_pairs={{0,32},{32,0},{64,96},{96,64},{128,160},{160,128},{192,224},{224,1... | collective-permute-start | bytes 2752520 | tf_op jit(solution)/shard_map/ppermute | solution.py:514
  23.2 4.1 %collective-permute-start = (bf16[480,512]{1,0:T(8,128)(2,1)}, bf16[480,512]{1,0:T(8,128)(2,1)S(1)}, u32[]{:S(2)}, u32[]{:S(2)}) collective-permute-start(bf16[480,512]{1,0:T(8,128)(2,1)} %get-tuple-element.30), channel_id=1, source_target_pairs={{0,32},{32,0},{64,96},{96,64},{128,160},{160,128},{192,224},{224,1... | collective-permute-start | bytes 1474568 | tf_op jit(solution)/shard_map/ppermute | solution.py:514
  27.3 1.0 copy-start.3
  28.2 0.9 copy-start.5
  29.5 21.6 %copy-start = (bf16[8,304,128]{2,1,0:T(8,128)(2,1)}, bf16[8,304,128]{2,1,0:T(8,128)(2,1)S(1)}, u32[]{:S(2)}) copy-start(bf16[8,304,128]{2,1,0:T(8,128)(2,1)S(1)} %all-to-all-done.refs_3_.refs_1_) | copy-start | bytes 1867780
  29.5 6.9 %collective-permute-start.4 = (bf16[8,304,128]{2,1,0:T(8,128)(2,1)S(1)}, bf16[8,304,128]{2,1,0:T(8,128)(2,1)S(1)}, u32[]{:S(2)}, u32[]{:S(2)}) collective-permute-start(bf16[8,304,128]{2,1,0:T(8,128)(2,1)S(1)} %all-to-all-done.refs_3_.refs_1_), channel_id=1, source_target_pairs={{0,32},{32,0},{64,96},{96,64},{128,160},{160,128},{192,224},{224,1... | collective-permute-start | bytes 1867784 | tf_op jit(solution)/shard_map/ppermute | solution.py:514
  37.4 0.8 copy-start.7
  38.3 22.2 %all-to-all-start.1 = ((bf16[32,8,384]{2,1,0:T(8,128)(2,1)}), bf16[32,8,384]{2,1,0:T(8,128)(2,1)S(1)}, u32[]{:S(2)}, u32[]{:S(2)}) async-start(bf16[32,8,384]{2,1,0:T(8,128)(2,1)} %shard_map.177), calls=%async_computation.1 | async-start | bytes 393216 | tf_op jit(solution)/shard_map/all_to_all | solution.py:506
  57.2 26.3 %copy-start.1 = (bf16[512,448]{0,1:T(8,128)(2,1)S(1)}, bf16[512,448]{0,1:T(8,128)(2,1)}, u32[]{:S(2)}) copy-start(bf16[512,448]{0,1:T(8,128)(2,1)} %param.27) | copy-start | bytes 1376260
  60.5 39.1 %copy-start.8 = (bf16[8,448]{1,0:T(8,128)(2,1)S(1)}, bf16[8,448]{1,0:T(8,128)(2,1)}, u32[]{:S(2)}) copy-start(bf16[8,448]{1,0:T(8,128)(2,1)} %refs_1_.3) | copy-start | bytes 21508
  60.5 39.1 %copy-start.9 = (f32[448]{0:T(512)S(1)}, f32[448]{0:T(512)}, u32[]{:S(2)}) copy-start(f32[448]{0:T(512)} %param.28) | copy-start | bytes 5380
  73.0 40.9 %copy-start.4 = (bf16[1,448,1024]{2,1,0:T(8,128)(2,1)S(1)}, bf16[1,448,1024]{2,1,0:T(8,128)(2,1)}, u32[]{:S(2)}) copy-start(bf16[1,448,1024]{2,1,0:T(8,128)(2,1)} %copy-done.3) | copy-start | bytes 2752516
  73.0 40.9 %copy-start.6 = (bf16[1,448,1024]{2,1,0:T(8,128)(2,1)S(1)}, bf16[1,448,1024]{2,1,0:T(8,128)(2,1)}, u32[]{:S(2)}) copy-start(bf16[1,448,1024]{2,1,0:T(8,128)(2,1)} %copy-done.5) | copy-start | bytes 2752516
  143.0 26.8 %copy-start.10 = (s32[8,8]{1,0:T(8,128)S(1)}, s32[8,8]{1,0:T(8,128)}, u32[]{:S(2)}) copy-start(s32[8,8]{1,0:T(8,128)} %refs_4_.7) | copy-start | bytes 772
  143.0 26.8 %copy-start.11 = (f32[8,8]{1,0:T(8,128)S(1)}, f32[8,8]{1,0:T(8,128)}, u32[]{:S(2)}) copy-start(f32[8,8]{1,0:T(8,128)} %refs_5_.1) | copy-start | bytes 772
  143.4 11.3 %collective-permute-start.6 = (bf16[128,448]{1,0:T(8,128)(2,1)S(1)}, bf16[128,448]{1,0:T(8,128)(2,1)S(1)}, u32[]{:S(2)}, u32[]{:S(2)}) collective-permute-start(bf16[128,448]{1,0:T(8,128)(2,1)S(1)} %shard_map.185), channel_id=1, source_target_pairs={{0,32},{32,0},{64,96},{96,64},{128,160},{160,128},{192,224},{224,1... | collective-permute-start | bytes 344072 | tf_op jit(solution)/shard_map/ppermute | solution.py:514
  155.7 14.1 %all-to-all-start.8 = ((bf16[32,8,448]{2,1,0:T(8,128)(2,1)}), bf16[32,8,448]{2,1,0:T(8,128)(2,1)S(1)}, u32[]{:S(2)}, u32[]{:S(2)}) async-start(bf16[32,8,448]{2,1,0:T(8,128)(2,1)} %shard_map.186), calls=%async_computation.8 | async-start | bytes 524288 | tf_op jit(solution)/shard_map/all_to_all | solution.py:506
  160.0 3.4 %collective-permute-start.7 = (bf16[8,448]{1,0:T(8,128)(2,1)S(1)}, bf16[8,448]{1,0:T(8,128)(2,1)S(1)}, u32[]{:S(2)}, u32[]{:S(2)}) collective-permute-start(bf16[8,448]{1,0:T(8,128)(2,1)S(1)} %get-tuple-element.51.refs_2_), channel_id=1, source_target_pairs={{0,32},{32,0},{64,96},{96,64},{128,160},{160,128},{192,224},{224,1... | collective-permute-start | bytes 21512 | tf_op jit(solution)/shard_map/ppermute | solution.py:514
